TPU v7x, 32 devices: a whole 2x2x4 slice. The times are simulated.
32 devices in a mesh: dp: 8 (over z, x), tensor: 4 (over y, core).
Axes of the slice: x: 2, y: 2, z: 4, core: 2. Of those that a mesh axis runs over, the one named last changes fastest.
Arguments:
- tokens: bfloat16 [4096, 2304], P(('dp', 'tensor')), may hold values from -6 to 6
- cotangent: bfloat16 [4096, 2304], P(('dp', 'tensor')), may hold values from -6 to 6
- dealt_lengths: int32 [8, 4], P('dp'), may hold values from 0 to 512, as said below
- norm_gains: float32 [4, 2304], replicated, may hold values from 0.25 to 1.75
- query_weight: bfloat16 [2304, 2048], P('dp', 'tensor'), may hold values from -0.25 to 0.25
- key_matrix: bfloat16 [2304, 1024], P('dp', 'tensor'), may hold values from -0.125 to 0.125
- value_matrix: bfloat16 [2304, 1024], P('dp', 'tensor'), may hold values from -0.125 to 0.125
- out_weight: bfloat16 [2304, 2048], P('dp', 'tensor'), may hold values from -0.125 to 0.125
- gate_weight: bfloat16 [2304, 9216], P('dp', 'tensor'), may hold values from -0.125 to 0.125
- up_weight: bfloat16 [2304, 9216], P('dp', 'tensor'), may hold values from -0.125 to 0.125
- down_weight: bfloat16 [2304, 9216], P('dp', 'tensor'), may hold values from -0.0625 to 0.0625
- moment_query: float32 [2304, 2048], P('dp', 'tensor'), may hold values from -256 to 256
- moment_key: float32 [2304, 1024], P('dp', 'tensor'), may hold values from -256 to 256
- moment_value: float32 [2304, 1024], P('dp', 'tensor'), may hold values from -768 to 768
- moment_out: float32 [2304, 2048], P('dp', 'tensor'), may hold values from -768 to 768
- moment_gate: float32 [2304, 9216], P('dp', 'tensor'), may hold values from -768 to 768
- moment_up: float32 [2304, 9216], P('dp', 'tensor'), may hold values from -768 to 768
- moment_down: float32 [2304, 9216], P('dp', 'tensor'), may hold values from -768 to 768
Outputs:
- block_output: bfloat16 [4096, 2304], P(('dp', 'tensor'))
- input_grad: float32 [4096, 2304], P(('dp', 'tensor'))
- gain_grads: float32 [4, 2304], replicated
- grad_query: float32 [2304, 2048], P('dp', 'tensor')
- grad_key: float32 [2304, 1024], P('dp', 'tensor')
- grad_value: float32 [2304, 1024], P('dp', 'tensor')
- grad_out: float32 [2304, 2048], P('dp', 'tensor')
- grad_gate: float32 [2304, 9216], P('dp', 'tensor')
- grad_up: float32 [2304, 9216], P('dp', 'tensor')
- grad_down: float32 [2304, 9216], P('dp', 'tensor')
- momentum_query: float32 [2304, 2048], P('dp', 'tensor')
- momentum_key: float32 [2304, 1024], P('dp', 'tensor')
- momentum_value: float32 [2304, 1024], P('dp', 'tensor')
- momentum_out: float32 [2304, 2048], P('dp', 'tensor')
- momentum_gate: float32 [2304, 9216], P('dp', 'tensor')
- momentum_up: float32 [2304, 9216], P('dp', 'tensor')
- momentum_down: float32 [2304, 9216], P('dp', 'tensor')
- update_query: float32 [2304, 2048], P('dp', 'tensor')
- update_key: float32 [2304, 1024], P('dp', 'tensor')
- update_value: float32 [2304, 1024], P('dp', 'tensor')
- update_out: float32 [2304, 2048], P('dp', 'tensor')
- update_gate: float32 [2304, 9216], P('dp', 'tensor')
- update_up: float32 [2304, 9216], P('dp', 'tensor')
- update_down: float32 [2304, 9216], P('dp', 'tensor')
Inputs may be any that keep to these rules, and one draw needn't show every extreme that they name: `dealt_lengths`: row g lists the lengths of the sequences dealt to group g in order, 0 only after its last sequence; padded to whole blocks of 128 slots, one row's sequences take at most 4 blocks; in every draw some row holds a single sequence of 512 tokens.
All inputs are finite; a program needn't handle non-finite values.
Results may differ from a plain program's by a relative error of at most 0.03.
Values may be sent and summed in bfloat16 or wider, within the bound.
No kernel may reach another device: no remote copies, remote signals or barrier semaphores. Data moves between devices by JAX's collectives and lax.ppermute only.
A program may use at most 384 MiB of HBM per device.

v0:
```python
from functools import partial

import jax
import jax.numpy as jnp
from jax import lax
from jax.sharding import PartitionSpec as P

MODEL_WIDTH = 2304
QUERY_HEADS = 8
KEY_VALUE_HEADS = 4
HEAD_SIZE = 256
WINDOW = 4096
BLK = 128
NS_STEPS = 5
GROUP_BLOCKS = 4
GROUP_SLOTS = 512


epsilon = 1e-06
softcap = 50.0
rope_base = 10000.0
coef_first = 3.4445
coef_second = -4.775
coef_third = 2.0315
momentum_decay = 0.95
learn_rate = 0.2
masked_value = -1e30


def as_sent(shard):
    return jax.tree.map(lambda a: a.astype(jnp.bfloat16) if a.dtype == jnp.float32 else a, shard)


def slot_layout(lengths):
    blocks = (lengths + BLK - 1) // BLK
    block_ends = jnp.cumsum(blocks, dtype=jnp.int32) * BLK
    slot_index = jnp.arange(GROUP_SLOTS, dtype=jnp.int32)
    passed = slot_index[:, None] >= block_ends[None, :]
    segment = jnp.sum(passed.astype(jnp.int32), axis=1, dtype=jnp.int32)
    before = jnp.sum(jnp.where(passed, blocks[None, :] * BLK, 0), axis=1, dtype=jnp.int32)
    position = slot_index - before
    in_segment = segment[:, None] == jnp.arange(GROUP_BLOCKS, dtype=jnp.int32)[None, :]
    own_length = jnp.sum(jnp.where(in_segment, lengths[None, :], 0), axis=1, dtype=jnp.int32)
    is_alive = position < own_length
    return (segment, position, is_alive)


def allowed_pairs(segment, is_alive):
    slot_index = jnp.arange(GROUP_SLOTS, dtype=jnp.int32)
    distance = slot_index[:, None] - slot_index[None, :]
    same_segment = segment[:, None] == segment[None, :]
    inside = (
        is_alive[:, None] & is_alive[None, :] & same_segment & (distance >= 0) & (distance < WINDOW)
    )
    return (distance == 0) | inside


def rope_tables(position):
    half_width = HEAD_SIZE // 2
    frequency = rope_base ** (-2.0 * jnp.arange(half_width, dtype=jnp.float32) / HEAD_SIZE)
    angles = position.astype(jnp.float32)[:, None] * frequency[None, :]
    return (jnp.cos(angles), jnp.sin(angles))


def apply_rotary(values, rotary_cosines, rotary_sines):
    half_width = HEAD_SIZE // 2
    first_half = values[..., :half_width]
    second_half = values[..., half_width:]
    rotary_cosines = rotary_cosines[:, None, :]
    rotary_sines = rotary_sines[:, None, :]
    return jnp.concatenate(
        [
            first_half * rotary_cosines - second_half * rotary_sines,
            second_half * rotary_cosines + first_half * rotary_sines,
        ],
        axis=-1,
    )


def norm_forward(values, gain):
    inverse = lax.rsqrt(jnp.mean(values * values, axis=-1, keepdims=True) + epsilon)
    return (values * inverse * gain, inverse)


def norm_backward(values, inverse, gain, upstream):
    scaled = upstream * gain
    row_inner = jnp.mean(scaled * values, axis=-1, keepdims=True)
    return (
        inverse * scaled - values * inverse**3 * row_inner,
        jnp.sum(upstream * values * inverse, axis=0),
    )


def contract_last(left_side, right_side):
    return lax.dot_general(
        left_side, right_side, (((1,), (1,)), ((), ())), preferred_element_type=jnp.float32
    )


def contract_first(left_side, right_side):
    return lax.dot_general(
        left_side, right_side, (((0,), (0,)), ((), ())), preferred_element_type=jnp.float32
    )


def gather_rows(values):
    return lax.all_gather(values, "tensor", axis=0, tiled=True)


def sum_rows(values):
    return lax.psum_scatter(values, "tensor", scatter_dimension=0, tiled=True)


def attention_scores(query_rows_rotated, key_vectors, allowed):
    raw_scores = jnp.einsum(
        "tkgd,skd->kgts", query_rows_rotated, key_vectors, preferred_element_type=jnp.float32
    )
    tanh_part = jnp.tanh(raw_scores / softcap)
    masked = jnp.where(allowed[None, None], softcap * tanh_part, masked_value)
    return (tanh_part, masked)


def gradient_terms(left_parts, right_parts):
    pieces = []
    for left_side, rights in zip(left_parts, right_parts):
        for right_side in rights:
            pieces.append(contract_first(left_side, right_side))
    return jnp.concatenate(pieces, axis=1)


def orthogonal_step(columns, count):
    blocks = columns.reshape(columns.shape[0], count, HEAD_SIZE)
    frobenius = jnp.sqrt(jnp.sum(blocks * blocks, axis=(0, 2), keepdims=True)) + 1e-07
    current = blocks / frobenius
    for repeat in range(NS_STEPS):
        square = jnp.einsum(
            "dbi,dbj->bij",
            current,
            current,
            precision=lax.Precision.HIGHEST,
            preferred_element_type=jnp.float32,
        )
        polynomial = coef_second * square + coef_third * jnp.einsum(
            "bij,bjk->bik",
            square,
            square,
            precision=lax.Precision.HIGHEST,
            preferred_element_type=jnp.float32,
        )
        current = coef_first * current + jnp.einsum(
            "dbi,bij->dbj",
            current,
            polynomial,
            precision=lax.Precision.HIGHEST,
            preferred_element_type=jnp.float32,
        )
    return (-learn_rate * (MODEL_WIDTH / HEAD_SIZE) ** 0.5 * current).reshape(
        columns.shape[0], count * HEAD_SIZE
    )


def shards(
    tokens,
    cotangent,
    dealt_lengths,
    norm_gains,
    query_weight,
    key_matrix,
    value_matrix,
    out_weight,
    gate_weight,
    up_weight,
    down_weight,
    moment_query,
    moment_key,
    moment_value,
    moment_out,
    moment_gate,
    moment_up,
    moment_down,
):
    local_rows = tokens.shape[0]
    shard_rows = query_weight.shape[0]
    segment, position, is_alive = slot_layout(dealt_lengths[0])
    allowed = allowed_pairs(segment, is_alive)
    rotary_cosines, rotary_sines = rope_tables(position)
    my_alive = lax.dynamic_slice_in_dim(is_alive, lax.axis_index("tensor") * local_rows, local_rows)
    query_cols = query_weight.shape[1]
    kv_cols = key_matrix.shape[1]
    kv_heads = kv_cols // HEAD_SIZE
    group_width = QUERY_HEADS // KEY_VALUE_HEADS
    local_weights = (
        query_weight,
        key_matrix,
        value_matrix,
        out_weight,
        gate_weight,
        up_weight,
        down_weight,
    )
    full_weights = (
        lax.all_gather(local_weights[0], "dp", axis=0, tiled=True),
        lax.all_gather(local_weights[1], "dp", axis=0, tiled=True),
        lax.all_gather(local_weights[2], "dp", axis=0, tiled=True),
        lax.all_gather(local_weights[3], "dp", axis=0, tiled=True),
        lax.all_gather(local_weights[4], "dp", axis=0, tiled=True),
        lax.all_gather(local_weights[5], "dp", axis=0, tiled=True),
        lax.all_gather(local_weights[6], "dp", axis=0, tiled=True),
    )
    query_full, key_full, value_full, out_full, gate_full, up_full, down_full = full_weights
    inputs = tokens.astype(jnp.float32)
    normalized_input, inverse_in = norm_forward(inputs, norm_gains[0])
    normed_full = gather_rows(normalized_input.astype(jnp.bfloat16))
    projected_queries = jnp.dot(
        normed_full, query_full, preferred_element_type=jnp.float32
    ).reshape(GROUP_SLOTS, -1, HEAD_SIZE)
    projected_keys = jnp.dot(normed_full, key_full, preferred_element_type=jnp.float32).reshape(
        GROUP_SLOTS, kv_heads, HEAD_SIZE
    )
    value_rows_packed = (
        jnp.dot(normed_full, value_full, preferred_element_type=jnp.float32)
        .astype(jnp.bfloat16)
        .reshape(GROUP_SLOTS, kv_heads, HEAD_SIZE)
    )
    query_rows_rotated = (
        (apply_rotary(projected_queries, rotary_cosines, rotary_sines) * HEAD_SIZE ** (-0.5))
        .astype(jnp.bfloat16)
        .reshape(GROUP_SLOTS, kv_heads, group_width, HEAD_SIZE)
    )
    key_vectors = apply_rotary(projected_keys, rotary_cosines, rotary_sines).astype(jnp.bfloat16)
    tanh_part, masked = attention_scores(query_rows_rotated, key_vectors, allowed)
    row_max = jnp.max(masked, axis=-1, keepdims=True)
    exponent = jnp.exp(masked - row_max)
    row_total = jnp.sum(exponent, axis=-1, keepdims=True)
    log_total = row_max + jnp.log(row_total)
    prob_low = (exponent / row_total).astype(jnp.bfloat16)
    mixed_heads = (
        jnp.einsum(
            "kgts,skd->tkgd", prob_low, value_rows_packed, preferred_element_type=jnp.float32
        )
        .reshape(GROUP_SLOTS, query_cols)
        .astype(jnp.bfloat16)
    )
    attended = sum_rows(contract_last(mixed_heads, out_full))
    normed_attn, inverse_attn = norm_forward(attended, norm_gains[1])
    middle = inputs + normed_attn
    normed_mid, inverse_mid = norm_forward(middle, norm_gains[2])
    mid_full = gather_rows(normed_mid.astype(jnp.bfloat16))
    gate_proj = jnp.dot(mid_full, gate_full, preferred_element_type=jnp.float32)
    up_proj = jnp.dot(mid_full, up_full, preferred_element_type=jnp.float32)
    activated, gelu_pull = jax.vjp(partial(jax.nn.gelu, approximate=True), gate_proj)
    hidden = (activated * up_proj).astype(jnp.bfloat16)
    feed_out = sum_rows(contract_last(hidden, down_full))
    normed_feed, inverse_feed = norm_forward(feed_out, norm_gains[3])
    block_output = (middle + normed_feed).astype(jnp.bfloat16)
    back_weights = (
        lax.all_gather(local_weights[0], "dp", axis=0, tiled=True),
        lax.all_gather(local_weights[1], "dp", axis=0, tiled=True),
        lax.all_gather(local_weights[2], "dp", axis=0, tiled=True),
        lax.all_gather(local_weights[3], "dp", axis=0, tiled=True),
        lax.all_gather(local_weights[4], "dp", axis=0, tiled=True),
        lax.all_gather(local_weights[5], "dp", axis=0, tiled=True),
        lax.all_gather(local_weights[6], "dp", axis=0, tiled=True),
    )
    query_back, key_back, value_back, out_back, gate_back, up_back, down_back = back_weights
    upstream = jnp.where(my_alive[:, None], cotangent.astype(jnp.float32), 0.0)
    delta_feed, gain_feed = norm_backward(feed_out, inverse_feed, norm_gains[3], upstream)
    feed_grad = gather_rows(delta_feed.astype(jnp.bfloat16))
    delta_hidden = jnp.dot(feed_grad, down_back, preferred_element_type=jnp.float32)
    delta_gate = gelu_pull(delta_hidden * up_proj)[0].astype(jnp.bfloat16)
    delta_up = (delta_hidden * activated).astype(jnp.bfloat16)
    delta_mid = sum_rows(contract_last(delta_gate, gate_back) + contract_last(delta_up, up_back))
    mid_back, gain_mid = norm_backward(middle, inverse_mid, norm_gains[2], delta_mid)
    delta_middle = upstream + mid_back
    delta_attended, gain_attn = norm_backward(attended, inverse_attn, norm_gains[1], delta_middle)
    attn_grad = gather_rows(delta_attended.astype(jnp.bfloat16))
    delta_mixed = (
        jnp.dot(attn_grad, out_back, preferred_element_type=jnp.float32)
        .astype(jnp.bfloat16)
        .reshape(GROUP_SLOTS, kv_heads, group_width, HEAD_SIZE)
    )
    tanh_part, masked = attention_scores(query_rows_rotated, key_vectors, allowed)
    prob_exact = jnp.exp(masked - log_total)
    prob_again = prob_exact.astype(jnp.bfloat16)
    delta_prob = jnp.einsum(
        "tkgd,skd->kgts", delta_mixed, value_rows_packed, preferred_element_type=jnp.float32
    )
    delta_values = (
        jnp.einsum("kgts,tkgd->skd", prob_again, delta_mixed, preferred_element_type=jnp.float32)
        .reshape(GROUP_SLOTS, kv_cols)
        .astype(jnp.bfloat16)
    )
    row_inner = jnp.sum(prob_exact * delta_prob, axis=-1, keepdims=True)
    delta_raw = (
        jnp.where(allowed[None, None], prob_exact * (delta_prob - row_inner), 0.0)
        * (1.0 - tanh_part * tanh_part)
    ).astype(jnp.bfloat16)
    delta_queries = jnp.einsum(
        "kgts,skd->tkgd", delta_raw, key_vectors, preferred_element_type=jnp.float32
    ).reshape(GROUP_SLOTS, -1, HEAD_SIZE) * HEAD_SIZE ** (-0.5)
    delta_query_proj = (
        apply_rotary(delta_queries, rotary_cosines, -rotary_sines)
        .reshape(GROUP_SLOTS, query_cols)
        .astype(jnp.bfloat16)
    )
    delta_keys = jnp.einsum(
        "kgts,tkgd->skd", delta_raw, query_rows_rotated, preferred_element_type=jnp.float32
    )
    delta_key_proj = (
        apply_rotary(delta_keys, rotary_cosines, -rotary_sines)
        .reshape(GROUP_SLOTS, kv_cols)
        .astype(jnp.bfloat16)
    )
    delta_normed = sum_rows(
        contract_last(delta_query_proj, query_back)
        + contract_last(delta_key_proj, key_back)
        + contract_last(delta_values, value_back)
    )
    in_back, gain_in = norm_backward(inputs, inverse_in, norm_gains[0], delta_normed)
    input_grad = delta_middle + in_back
    weight_grads = lax.psum_scatter(
        gradient_terms(
            (normed_full, attn_grad, mid_full, feed_grad),
            (
                (delta_query_proj, delta_key_proj, delta_values),
                (mixed_heads,),
                (delta_gate, delta_up),
                (hidden,),
            ),
        ).astype(jnp.bfloat16),
        "dp",
        scatter_dimension=0,
        tiled=True,
    ).astype(jnp.float32)
    widths = [w.shape[1] for w in local_weights]
    offsets = [sum(widths[: i + 1]) for i in range(len(widths) - 1)]
    grad_list = jnp.split(weight_grads, offsets, axis=1)
    moments = (
        moment_query,
        moment_key,
        moment_value,
        moment_out,
        moment_gate,
        moment_up,
        moment_down,
    )
    states = [momentum_decay * m + g for m, g in zip(moments, grad_list)]
    stacked = jnp.concatenate(states, axis=1)
    block_count = stacked.shape[1] // HEAD_SIZE
    dp_size = lax.axis_size("dp")
    per_owner = block_count // dp_size
    main_cols = per_owner * dp_size * HEAD_SIZE
    owned_blocks = lax.all_to_all(
        as_sent(stacked[:, :main_cols]), "dp", split_axis=1, concat_axis=0, tiled=True
    )
    owned_update = orthogonal_step(owned_blocks, per_owner)
    main_update = lax.all_to_all(
        as_sent(owned_update), "dp", split_axis=0, concat_axis=1, tiled=True
    ).astype(owned_update.dtype)
    shared = lax.all_gather(as_sent(stacked[:, main_cols:]), "dp", axis=0, tiled=True)
    shared_update = orthogonal_step(shared, block_count - per_owner * dp_size)
    shared_rows = lax.dynamic_slice_in_dim(
        shared_update, lax.axis_index("dp") * shard_rows, shard_rows, 0
    )
    updates = jnp.split(jnp.concatenate([main_update, shared_rows], axis=1), offsets, axis=1)
    gain_rows = jnp.stack([gain_in, gain_attn, gain_mid, gain_feed])
    gain_grads = lax.psum(gain_rows, ("dp", "tensor"))
    return (
        block_output,
        input_grad,
        gain_grads,
        grad_list[0],
        grad_list[1],
        grad_list[2],
        grad_list[3],
        grad_list[4],
        grad_list[5],
        grad_list[6],
        states[0],
        states[1],
        states[2],
        states[3],
        states[4],
        states[5],
        states[6],
        updates[0],
        updates[1],
        updates[2],
        updates[3],
        updates[4],
        updates[5],
        updates[6],
    )


def solution(mesh):
    placed = (
        P(("dp", "tensor"), None),
        P(("dp", "tensor"), None),
        P("dp", None),
        P(),
        P("dp", "tensor"),
        P("dp", "tensor"),
        P("dp", "tensor"),
        P("dp", "tensor"),
        P("dp", "tensor"),
        P("dp", "tensor"),
        P("dp", "tensor"),
        P("dp", "tensor"),
        P("dp", "tensor"),
        P("dp", "tensor"),
        P("dp", "tensor"),
        P("dp", "tensor"),
        P("dp", "tensor"),
        P("dp", "tensor"),
    )
    return jax.shard_map(
        shards,
        mesh=mesh,
        in_specs=placed,
        out_specs=(
            P(("dp", "tensor"), None),
            P(("dp", "tensor"), None),
            P(),
            P("dp", "tensor"),
            P("dp", "tensor"),
            P("dp", "tensor"),
            P("dp", "tensor"),
            P("dp", "tensor"),
            P("dp", "tensor"),
            P("dp", "tensor"),
            P("dp", "tensor"),
            P("dp", "tensor"),
            P("dp", "tensor"),
            P("dp", "tensor"),
            P("dp", "tensor"),
            P("dp", "tensor"),
            P("dp", "tensor"),
            P("dp", "tensor"),
            P("dp", "tensor"),
            P("dp", "tensor"),
            P("dp", "tensor"),
            P("dp", "tensor"),
            P("dp", "tensor"),
            P("dp", "tensor"),
        ),
        check_vma=False,
    )
```

profile of v0, /device:TPU:0, one launch (start us, length us, event | category | flops | bytes accessed | tf_op | source)
XLA Modules:
  0.0 2218.1 jit_solution(14305376478910298961)
XLA Ops:
  17.9 36.1 %all-gather.17.cloned.1.call-done = bf16[2304,256]{1,0:T(8,128)(2,1)} async-done(((bf16[288,256]{1,0:T(8,128)(2,1)}), bf16[2304,256]{1,0:T(8,128)(2,1)}) %all-gather.17.cloned.1.call-update) | async-done | bytes 1179664 | tf_op jit(solution)/shard_map/all_gather | solution.py:203
  54.0 25.0 %all-gather.13.cloned.1.call-done = bf16[512,2304]{1,0:T(8,128)(2,1)} async-done(((bf16[128,2304]{1,0:T(8,128)(2,1)}), bf16[512,2304]{1,0:T(8,128)(2,1)}) %all-gather.13.cloned.1.call-update) | async-done | bytes 2359312 | tf_op jit(solution)/shard_map/all_gather | solution.py:107
  79.0 2.9 convolution_bitcast_fusion.7
  83.8 38.5 %all-gather.15.cloned.1.call-done = bf16[2304,256]{1,0:T(8,128)(2,1)} async-done(((bf16[288,256]{1,0:T(8,128)(2,1)}), bf16[2304,256]{1,0:T(8,128)(2,1)}) %all-gather.15.cloned.1.call-update) | async-done | bytes 1179664 | tf_op jit(solution)/shard_map/all_gather | solution.py:204
  125.0 50.2 %all-gather.19.cloned.1.call-done = bf16[2304,512]{1,0:T(8,128)(2,1)} async-done(((bf16[288,512]{1,0:T(8,128)(2,1)}), bf16[2304,512]{1,0:T(8,128)(2,1)}) %all-gather.19.cloned.1.call-update) | async-done | bytes 2359312 | tf_op jit(solution)/shard_map/all_gather | solution.py:202
  175.2 3.8 fusion.133
  183.3 44.6 %all-gather.21.cloned.1.call-done = bf16[2304,512]{1,0:T(8,128)(2,1)} async-done(((bf16[288,512]{1,0:T(8,128)(2,1)}), bf16[2304,512]{1,0:T(8,128)(2,1)}) %all-gather.21.cloned.1.call-update) | async-done | bytes 2359312 | tf_op jit(solution)/shard_map/all_gather | solution.py:205
  227.9 5.3 fusion.134
  233.2 46.5 %reduce-scatter.8.cloned.1.call-done = f32[128,2304]{1,0:T(8,128)} async-done(((f32[512,2304]{1,0:T(8,128)}), f32[128,2304]{1,0:T(8,128)}) %reduce-scatter.8.cloned.1.call-update) | async-done | bytes 1179664 | tf_op jit(solution)/shard_map/reduce_scatter | solution.py:111
  286.2 21.9 all-gather.23.cloned.1.call-done
  308.1 154.9 %all-gather.25.cloned.1.call-done = bf16[2304,2304]{1,0:T(8,128)(2,1)} async-done(((bf16[288,2304]{1,0:T(8,128)(2,1)}), bf16[2304,2304]{1,0:T(8,128)(2,1)}) %all-gather.25.cloned.1.call-update) | async-done | bytes 10616848 | tf_op jit(solution)/shard_map/all_gather | solution.py:206
  463.0 11.7 fusion.135
  474.7 141.4 %all-gather.27.cloned.1.call-done = bf16[2304,2304]{1,0:T(8,128)(2,1)} async-done(((bf16[288,2304]{1,0:T(8,128)(2,1)}), bf16[2304,2304]{1,0:T(8,128)(2,1)}) %all-gather.27.cloned.1.call-update) | async-done | bytes 10616848 | tf_op jit(solution)/shard_map/all_gather | solution.py:207
  616.1 12.8 multiply_convert_fusion.1
  628.9 140.1 %all-gather.29.cloned.1.call-done = bf16[2304,2304]{1,0:T(8,128)(2,1)} async-done(((bf16[288,2304]{1,0:T(8,128)(2,1)}), bf16[2304,2304]{1,0:T(8,128)(2,1)}) %all-gather.29.cloned.1.call-update) | async-done | bytes 10616848 | tf_op jit(solution)/shard_map/all_gather | solution.py:208
  769.0 11.8 fusion.136
  780.9 46.1 %reduce-scatter.10.cloned.1.call-done = f32[128,2304]{1,0:T(8,128)} async-done(((f32[512,2304]{1,0:T(8,128)}), f32[128,2304]{1,0:T(8,128)}) %reduce-scatter.10.cloned.1.call-update) | async-done | bytes 1179664 | tf_op jit(solution)/shard_map/reduce_scatter | solution.py:111
  833.0 23.8 %all-gather.31.cloned.1.call-done = bf16[512,2304]{1,0:T(8,128)(2,1)} async-done(((bf16[128,2304]{1,0:T(8,128)(2,1)}), bf16[512,2304]{1,0:T(8,128)(2,1)}) %all-gather.31.cloned.1.call-update) | async-done | bytes 2359312 | tf_op jit(solution)/shard_map/all_gather | solution.py:107
  856.7 14.2 multiply_convert_fusion
  871.0 9.8 fusion.137
  880.8 11.3 convolution_add_fusion.2
  892.2 47.9 %reduce-scatter.12.cloned.1.call-done = f32[128,2304]{1,0:T(8,128)} async-done(((f32[512,2304]{1,0:T(8,128)}), f32[128,2304]{1,0:T(8,128)}) %reduce-scatter.12.cloned.1.call-update) | async-done | bytes 1179664 | tf_op jit(solution)/shard_map/reduce_scatter | solution.py:111
  946.1 24.1 %all-gather.33.cloned.1.call-done = bf16[512,2304]{1,0:T(8,128)(2,1)} async-done(((bf16[128,2304]{1,0:T(8,128)(2,1)}), bf16[512,2304]{1,0:T(8,128)(2,1)}) %all-gather.33.cloned.1.call-update) | async-done | bytes 2359312 | tf_op jit(solution)/shard_map/all_gather | solution.py:107
  970.2 3.8 convolution_convert_fusion.8
  981.2 4.7 fusion.14
  992.7 8.3 fusion.2
  1001.0 8.3 fusion.1
  1009.2 8.5 fusion
  1017.7 47.4 %copy.332 = bf16[2304,8448]{1,0:T(8,128)(2,1)} copy(bf16[2304,8448]{0,1:T(8,128)(2,1)} %fusion) | data formatting | bytes 77856768
  1074.8 3.8 copy.268
  1081.0 600.5 %reduce-scatter.16.cloned.1.call-done = bf16[288,8448]{1,0:T(8,128)(2,1)} async-done(((bf16[2304,8448]{1,0:T(8,128)(2,1)}), bf16[288,8448]{1,0:T(8,128)(2,1)}) %reduce-scatter.16.cloned.1.call-update) | async-done | bytes 4866064
  1681.5 8.2 copy.333
  1689.6 3.4 convert_element_type.173
  1697.7 3.0 convert_dynamic-update-slice_fusion.1
  1700.7 3.1 convert_dynamic-update-slice_fusion
  1703.8 3.6 constant_dynamic-update-slice_fusion
  1707.4 6.1 slice.70
  1713.4 7.9 copy.270
  1721.4 4.7 all-to-all-start
  1730.0 3.0 convolution_add_fusion.1
  1732.9 97.9 %all-to-all-done = bf16[288,8,1024]{2,0,1:T(8,128)(2,1)} async-done(((bf16[288,8,1024]{2,0,1:T(8,128)(2,1)}), bf16[288,8,1024]{2,0,1:T(8,128)(2,1)}, u32[]{:S(2)}, u32[]{:S(2)}) %all-to-all-start) | async-done | bytes 4718624 | tf_op jit(solution)/shard_map/all_to_all | solution.py:353
  1830.9 9.2 reshape.655
  1840.1 8.5 copy.271
  1848.6 3.4 convert_reduce_fusion
  1852.1 5.4 fusion.126
  1858.8 6.4 fusion.125
  1865.3 17.4 fusion.5
  1883.9 21.3 bitcast_add_fusion.3
  1905.3 8.8 fusion.138
  1915.4 17.9 bitcast_add_fusion.2
  1933.3 8.8 fusion.139
  1943.4 12.3 bitcast_add_fusion.1
  1955.6 15.4 fusion.140
  1972.3 11.6 fusion.4
  1983.9 8.4 copy.287
  1992.2 8.7 convert_element_type.178
  2001.0 4.7 all-to-all-start.1
  2007.8 122.7 %psum.7 = f32[4,2304]{1,0:T(4,128)} all-reduce(f32[4,2304]{1,0:T(4,128)S(1)} %pad_maximum_fusion.2), channel_id=1, replica_groups=mesh['dp'=8,'tensor'=4] {'dp','tensor'}, use_global_device_ids=true, to_apply=%region_23.24 | all-reduce | flops 9216 | bytes 73728 | tf_op jit(solution)/shard_map/psum | solution.py:367
  2139.9 6.2 fusion.129
  2146.1 3.6 copy.296
  2149.7 3.6 copy.297
  2166.2 3.7 copy.304
  2200.6 3.5 convert_bitcast_fusion
  2208.0 3.4 pad_maximum_fusion
  (291 shorter events, 136.4 us)
Async XLA Ops:
  7.2 8.2 copy-start.53
  7.2 46.8 %all-gather.17.cloned.1.call-start = ((), (), s32[]{:S(2)}) async-start(), calls=%async_computation.9 | async-start | bytes 1327104 | tf_op jit(solution)/shard_map/all_gather | solution.py:203
  7.9 71.1 %all-gather.13.cloned.1.call-start = ((), (), s32[]{:S(2)}) async-start(), calls=%async_computation.7 | async-start | bytes 2949120 | tf_op jit(solution)/shard_map/all_gather | solution.py:107
  13.4 108.9 %all-gather.15.cloned.1.call-start = ((), (), s32[]{:S(2)}) async-start(), calls=%async_computation.8 | async-start | bytes 1327104 | tf_op jit(solution)/shard_map/all_gather | solution.py:204
  14.2 161.0 %all-gather.19.cloned.1.call-start = ((), (), s32[]{:S(2)}) async-start(), calls=%async_computation.10 | async-start | bytes 2654208 | tf_op jit(solution)/shard_map/all_gather | solution.py:202
  14.7 213.1 %all-gather.21.cloned.1.call-start = ((), (), s32[]{:S(2)}) async-start(), calls=%async_computation.11 | async-start | bytes 2654208 | tf_op jit(solution)/shard_map/all_gather | solution.py:205
  15.3 264.4 %reduce-scatter.8.cloned.1.call-start = ((), (), s32[]{:S(2)}) async-start(), calls=%async_computation.12 | async-start | bytes 5898240 | tf_op jit(solution)/shard_map/reduce_scatter | solution.py:111
  79.0 43.3 %copy-start.54 = (bf16[512,2304]{1,0:T(8,128)(2,1)S(1)}, bf16[512,2304]{1,0:T(8,128)(2,1)}, u32[]{:S(2)}) copy-start(bf16[512,2304]{1,0:T(8,128)(2,1)} %all-gather.13.cloned.1.call-done) | copy-start | bytes 7077892
  183.3 49.9 %copy-start.40 = (bf16[256,2,512]{2,0,1:T(8,128)(2,1)}, bf16[256,2,512]{2,0,1:T(8,128)(2,1)S(1)}, u32[]{:S(2)}) copy-start(bf16[256,2,512]{2,0,1:T(8,128)(2,1)S(1)} %convolution_convert_fusion.7) | copy-start | bytes 1572868
  233.2 48.0 %copy-start.3 = (bf16[128,2304]{1,0:T(8,128)(2,1)S(1)}, bf16[128,2304]{1,0:T(8,128)(2,1)}, u32[]{:S(2)}) copy-start(bf16[128,2304]{1,0:T(8,128)(2,1)} %param.18) | copy-start | bytes 1769476
  233.2 74.9 %all-gather.23.cloned.1.call-start = ((), (), s32[]{:S(2)}) async-start(), calls=%async_computation.13 | async-start | bytes 2949120 | tf_op jit(solution)/shard_map/all_gather | solution.py:107
  283.9 179.1 %all-gather.25.cloned.1.call-start = ((), (), s32[]{:S(2)}) async-start(), calls=%async_computation.14 | async-start | bytes 11943936 | tf_op jit(solution)/shard_map/all_gather | solution.py:206
  284.6 331.5 %all-gather.27.cloned.1.call-start = ((), (), s32[]{:S(2)}) async-start(), calls=%async_computation.15 | async-start | bytes 11943936 | tf_op jit(solution)/shard_map/all_gather | solution.py:207
  285.4 483.6 %all-gather.29.cloned.1.call-start = ((), (), s32[]{:S(2)}) async-start(), calls=%async_computation.16 | async-start | bytes 11943936 | tf_op jit(solution)/shard_map/all_gather | solution.py:208
  286.0 541.0 %reduce-scatter.10.cloned.1.call-start = ((), (), s32[]{:S(2)}) async-start(), calls=%async_computation.17 | async-start | bytes 5898240 | tf_op jit(solution)/shard_map/reduce_scatter | solution.py:111
  780.8 47.8 %copy-start.14 = (bf16[128,2304]{1,0:T(8,128)(2,1)S(1)}, bf16[128,2304]{1,0:T(8,128)(2,1)}, u32[]{:S(2)}) copy-start(bf16[128,2304]{1,0:T(8,128)(2,1)} %param.19) | copy-start | bytes 1769476
  780.8 75.9 %all-gather.31.cloned.1.call-start = ((), (), s32[]{:S(2)}) async-start(), calls=%async_computation.18 | async-start | bytes 2949120 | tf_op jit(solution)/shard_map/all_gather | solution.py:107
  827.0 3.9 copy-start.9
  832.5 107.7 %reduce-scatter.12.cloned.1.call-start = ((), (), s32[]{:S(2)}) async-start(), calls=%async_computation.19 | async-start | bytes 5898240 | tf_op jit(solution)/shard_map/reduce_scatter | solution.py:111
  870.9 9.8 copy-start.64
  871.0 9.8 copy-start.62
  892.2 50.3 %copy-start.2 = (f32[128,2304]{1,0:T(8,128)S(1)}, f32[128,2304]{1,0:T(8,128)}, u32[]{:S(2)}) copy-start(f32[128,2304]{1,0:T(8,128)} %reduce-scatter.8.cloned.1.call-done) | copy-start | bytes 3538948
  892.2 78.0 %all-gather.33.cloned.1.call-start = ((), (), s32[]{:S(2)}) async-start(), calls=%async_computation.20 | async-start | bytes 2949120 | tf_op jit(solution)/shard_map/all_gather | solution.py:107
  946.0 735.5 %reduce-scatter.16.cloned.1.call-start = ((), (), s32[]{:S(2)}) async-start(), calls=%async_computation.23 | async-start | bytes 43794432
  946.0 28.0 %copy-start.13 = (f32[512,512,2]{1,0,2:T(8,128)S(1)}, f32[512,512,2]{1,0,2:T(8,128)}, u32[]{:S(2)}) copy-start(f32[512,512,2]{1,0,2:T(8,128)} %copy-done.12) | copy-start | bytes 6291460
  946.0 28.0 %copy-start.60 = (bf16[512,256,1]{1,0,2:T(8,128)(2,1)S(1)}, bf16[512,256,1]{1,0,2:T(8,128)(2,1)}, u32[]{:S(2)}) copy-start(bf16[512,256,1]{1,0,2:T(8,128)(2,1)} %fusion.66) | copy-start | bytes 786436
  977.7 3.0 copy-start.30
  980.7 5.2 copy-start.32
  980.7 5.2 copy-start.34
  981.2 4.7 copy-start.17
  981.2 4.7 copy-start.55
  989.8 2.9 copy-start.56
  989.8 2.9 copy-start.65
  992.7 8.3 copy-start.63
  1000.9 8.3 copy-start.57
  1000.9 8.3 copy-start.61
  1066.1 6.2 copy-start.21
  1689.6 3.4 copy-start.20
  1693.1 2.9 copy-start.19
  1695.1 2.6 copy-start.8
  1697.7 3.0 copy-start.7
  1721.4 4.8 copy-start.33
  1721.4 4.8 copy-start.35
  1721.4 109.5 %all-to-all-start = ((bf16[288,8,1024]{2,0,1:T(8,128)(2,1)}), bf16[288,8,1024]{2,0,1:T(8,128)(2,1)}, u32[]{:S(2)}, u32[]{:S(2)}) async-start(bf16[288,8,1024]{2,0,1:T(8,128)(2,1)} %copy.270), calls=%async_computation.4 | async-start | bytes 9437184 | tf_op jit(solution)/shard_map/all_to_all | solution.py:353
  1726.1 2.3 copy-start.18
  1726.1 2.3 copy-start.22
  1726.1 279.8 %reduce-scatter.14.cloned.1.call-start = ((), (), s32[]{:S(2)}) async-start(), calls=%async_computation.21 | async-start | bytes 5898240 | tf_op jit(solution)/shard_map/reduce_scatter | solution.py:111
  1848.6 10.2 slice-start
  1852.1 6.7 slice-start.1
  1905.3 8.8 copy-start.1
  1955.6 16.7 copy-start
  2001.0 4.9 copy-start.47
  2001.0 4.9 copy-start.48
  2001.0 4.9 copy-start.49
  2001.0 5.0 copy-start.4
  2001.0 5.0 copy-start.46
  2001.0 5.0 copy-start.51
  2001.0 199.6 %all-to-all-start.1 = ((bf16[8,288,1024]{2,1,0:T(8,128)(2,1)}), bf16[8,288,1024]{2,1,0:T(8,128)(2,1)}, u32[]{:S(2)}, u32[]{:S(2)}) async-start(bf16[8,288,1024]{2,1,0:T(8,128)(2,1)} %convert_element_type.178), calls=%async_computation.5 | async-start | bytes 9437184 | tf_op jit(solution)/shard_map/all_to_all | solution.py:357
  2005.8 126.5 %copy-start.11 = (f32[128,2304]{1,0:T(8,128)S(1)}, f32[128,2304]{1,0:T(8,128)}, u32[]{:S(2)}) copy-start(f32[128,2304]{1,0:T(8,128)} %copy-done.10) | copy-start | bytes 3538948
  2005.8 126.4 %copy-start.52 = (f32[128]{0:T(128)S(1)}, f32[128]{0:T(128)}, u32[]{:S(2)}) copy-start(f32[128]{0:T(128)} %get-tuple-element.209) | copy-start | bytes 1540
  2005.8 167.4 %all-gather.35.cloned.1.call-start = ((), (), s32[]{:S(2)}) async-start(), calls=%async_computation.22 | async-start | bytes 1327104 | tf_op jit(solution)/shard_map/all_gather | solution.py:360
  2006.0 126.3 %copy-start.15 = (f32[128,2304]{1,0:T(8,128)S(1)}, f32[128,2304]{1,0:T(8,128)}, u32[]{:S(2)}) copy-start(f32[128,2304]{1,0:T(8,128)} %reduce-scatter.14.cloned.1.call-done) | copy-start | bytes 3538948
  2155.6 8.2 copy-start.6
  2166.2 3.7 copy-start.5
  (23 other events, 31.7 us)
Sparse Core Ops, SparseCore 0:
  10.2 43.7 all-gather.16
  56.1 22.8 all-gather.12
  81.2 41.0 all-gather.14
  124.3 50.8 all-gather.18
  177.2 50.6 all-gather.20
  233.3 46.3 reduce-scatter.7
  284.0 24.0 all-gather.22
  310.5 152.4 all-gather.24
  465.4 150.6 all-gather.26
  618.3 150.6 all-gather.28
  780.9 46.0 reduce-scatter.9
  832.6 24.0 all-gather.30
  892.3 47.8 reduce-scatter.11
  946.1 24.0 all-gather.32
  1065.2 616.1 reduce-scatter.15
  1733.1 49.1 reduce-scatter.13
  2132.3 40.8 all-gather.34
where the time goes:
time: 2230 us; the launch traced here: 2220 us
  waiting for transfers between devices  1550 us (70%)
  matrix products  292 us (13%)
  local copies, waits for them, and re-layouts  172 us (8%)
  blocking collectives  123 us (6%)
  other arithmetic  59.4 us (3%)
    unnamed x18, waiting for transfers between devices  605 us
    all_gather x1, waiting for transfers between devices, shards(): lax.all_gather(local_weights[4], 'dp', axis=0, tiled=True)  155 us
    all_gather x1, waiting for transfers between devices, shards(): lax.all_gather(local_weights[5], 'dp', axis=0, tiled=True)  141 us
    reduce_scatter x4, waiting for transfers between devices, sum_rows(): return lax.psum_scatter(values, 'tensor', scatter_dimension=0, tiled=True)  141 us
    all_gather x1, waiting for transfers between devices, shards(): lax.all_gather(local_weights[6], 'dp', axis=0, tiled=True)  140 us
    psum x1, blocking collectives, shards(): gain_grads = lax.psum(gain_rows, ('dp', 'tensor'))  123 us
    unnamed x161, local copies, waits for them, and re-layouts  106 us
    all_to_all x1, waiting for transfers between devices, shards(): lax.all_to_all(as_sent(stacked[:, :main_cols]), 'dp', split_axis=1, conca...  97.9 us
  transfers between devices with their start and end apart: 19, of which 17 were waited for; matrix products, arithmetic and copies ran while one was open for 14% of the time, Pallas kernels for 0%

commit v1 on v0

v1 whole, which is shorter than its diff:
```python
from functools import partial

import jax
import jax.numpy as jnp
from jax import lax
from jax.experimental import pallas as pl
from jax.experimental.pallas import tpu as pltpu
from jax.sharding import Mesh
from jax.sharding import PartitionSpec as P

MODEL_WIDTH = 2304
QUERY_HEADS = 8
KEY_VALUE_HEADS = 4
HEAD_SIZE = 256
WINDOW = 4096
BLK = 128
NS_STEPS = 5
GROUP_BLOCKS = 4
GROUP_SLOTS = 512


epsilon = 1e-06
softcap = 50.0
rope_base = 10000.0
coef_first = 3.4445
coef_second = -4.775
coef_third = 2.0315
momentum_decay = 0.95
learn_rate = 0.2
masked_value = -1e30


def slot_layout(lengths):
    blocks = (lengths + BLK - 1) // BLK
    block_ends = jnp.cumsum(blocks, dtype=jnp.int32) * BLK
    slot_index = jnp.arange(GROUP_SLOTS, dtype=jnp.int32)
    passed = slot_index[:, None] >= block_ends[None, :]
    segment = jnp.sum(passed.astype(jnp.int32), axis=1, dtype=jnp.int32)
    before = jnp.sum(jnp.where(passed, blocks[None, :] * BLK, 0), axis=1, dtype=jnp.int32)
    position = slot_index - before
    in_segment = segment[:, None] == jnp.arange(GROUP_BLOCKS, dtype=jnp.int32)[None, :]
    own_length = jnp.sum(jnp.where(in_segment, lengths[None, :], 0), axis=1, dtype=jnp.int32)
    is_alive = position < own_length
    return (segment, position, is_alive)


def allowed_pairs(segment, is_alive):
    slot_index = jnp.arange(GROUP_SLOTS, dtype=jnp.int32)
    distance = slot_index[:, None] - slot_index[None, :]
    same_segment = segment[:, None] == segment[None, :]
    inside = (
        is_alive[:, None] & is_alive[None, :] & same_segment & (distance >= 0) & (distance < WINDOW)
    )
    return (distance == 0) | inside


def rope_tables(position):
    half_width = HEAD_SIZE // 2
    frequency = rope_base ** (-2.0 * jnp.arange(half_width, dtype=jnp.float32) / HEAD_SIZE)
    angles = position.astype(jnp.float32)[:, None] * frequency[None, :]
    return (jnp.cos(angles), jnp.sin(angles))


def apply_rotary(values, rotary_cosines, rotary_sines):
    half_width = HEAD_SIZE // 2
    first_half = values[..., :half_width]
    second_half = values[..., half_width:]
    rotary_cosines = rotary_cosines[:, None, :]
    rotary_sines = rotary_sines[:, None, :]
    return jnp.concatenate(
        [
            first_half * rotary_cosines - second_half * rotary_sines,
            second_half * rotary_cosines + first_half * rotary_sines,
        ],
        axis=-1,
    )


def norm_forward(values, gain):
    inverse = lax.rsqrt(jnp.mean(values * values, axis=-1, keepdims=True) + epsilon)
    return (values * inverse * gain, inverse)


def norm_backward(values, inverse, gain, upstream):
    scaled = upstream * gain
    row_inner = jnp.mean(scaled * values, axis=-1, keepdims=True)
    return (
        inverse * scaled - values * inverse**3 * row_inner,
        jnp.sum(upstream * values * inverse, axis=0),
    )


def contract_last(left_side, right_side):
    return lax.dot_general(
        left_side, right_side, (((1,), (1,)), ((), ())), preferred_element_type=jnp.float32
    )


def contract_first(left_side, right_side):
    return lax.dot_general(
        left_side, right_side, (((0,), (0,)), ((), ())), preferred_element_type=jnp.float32
    )


def attention_scores(query_rows_rotated, key_vectors, allowed):
    raw_scores = jnp.einsum(
        "tkgd,skd->kgts", query_rows_rotated, key_vectors, preferred_element_type=jnp.float32
    )
    tanh_part = jnp.tanh(raw_scores / softcap)
    masked = jnp.where(allowed[None, None], softcap * tanh_part, masked_value)
    return (tanh_part, masked)


HALF = HEAD_SIZE // 2


def two_terms(values):
    high = values.astype(jnp.bfloat16)
    low = (values - high.astype(jnp.float32)).astype(jnp.bfloat16)
    return high, low


def product(left_side, right_side):
    return jnp.dot(left_side, right_side, preferred_element_type=jnp.float32)


def product_f32(left_terms, right_terms):
    left_high, left_low = left_terms
    right_high, right_low = right_terms
    return product(left_high, right_high) + (
        product(left_high, right_low) + product(left_low, right_high)
    )


def gram_body(counts, *refs):
    out_ref = refs[-1]
    step = pl.program_id(0)
    start = 0
    for ref, count in zip(refs[:-1], counts):

        @pl.when((step >= start) & (step < start + count))
        def _(ref=ref):
            high, low = two_terms(ref[...])
            mixed = contract_first(high, low)
            gram = contract_first(high, high) + (mixed + mixed.T)
            out_ref[0, 0] = gram[:HALF, :HALF]
            out_ref[0, 1] = gram[:HALF, HALF:]
            out_ref[0, 2] = gram[HALF:, HALF:]

        start += count

    @pl.when(step >= start)
    def _():
        out_ref[...] = jnp.zeros(out_ref.shape, out_ref.dtype)


def clamped(start, count):
    return lambda step: (0, jnp.clip(step - start, 0, count - 1))


def spans(states):
    counts = [state.shape[1] // HEAD_SIZE for state in states]
    starts = [sum(counts[:i]) for i in range(len(counts))]
    return counts, starts


def grams(states, slots):
    counts, starts = spans(states)
    rows = states[0].shape[0]
    return pl.pallas_call(
        partial(gram_body, counts),
        grid=(slots,),
        in_specs=[
            pl.BlockSpec((rows, HEAD_SIZE), clamped(s, c)) for s, c in zip(starts, counts)
        ],
        out_specs=pl.BlockSpec((1, 3, HALF, HALF), lambda step: (step, 0, 0, 0)),
        out_shape=jax.ShapeDtypeStruct((slots, 3, HALF, HALF), jnp.float32),
        cost_estimate=pl.CostEstimate(
            flops=4 * sum(counts) * rows * HEAD_SIZE**2,
            bytes_accessed=sum(counts) * 4 * HEAD_SIZE * (rows + HEAD_SIZE),
            transcendentals=0,
        ),
        compiler_params=pltpu.CompilerParams(vmem_limit_bytes=40 * 1024 * 1024),
    )(*states)


def newton_body(count, *refs):
    out_ref = refs[-1]
    row = lax.broadcasted_iota(jnp.int32, (HEAD_SIZE, HEAD_SIZE), 0)
    col = lax.broadcasted_iota(jnp.int32, (HEAD_SIZE, HEAD_SIZE), 1)
    unit = (row == col).astype(jnp.float32)
    squares = []
    scales = []
    for i in range(count):
        parts = [sum(ref[i, j].astype(jnp.float32) for ref in refs[:-1]) for j in range(3)]
        gram = jnp.concatenate(
            [
                jnp.concatenate([parts[0], parts[1]], axis=1),
                jnp.concatenate([parts[1].T, parts[2]], axis=1),
            ],
            axis=0,
        )
        total = jnp.sum(jnp.sum(gram * unit, axis=1, keepdims=True), axis=0, keepdims=True)
        inverse = 1.0 / (jnp.sqrt(total) + 1e-07)
        squares.append(gram * inverse * inverse)
        scales.append(-learn_rate * (MODEL_WIDTH / HEAD_SIZE) ** 0.5 * inverse)
    totals = [None] * count
    for repeat in range(NS_STEPS):
        terms = [two_terms(square) for square in squares]
        seconds = [product_f32(t, t) for t in terms]
        steps = [
            coef_first * unit + (coef_second * square + coef_third * second)
            for square, second in zip(squares, seconds)
        ]
        step_terms = [two_terms(step) for step in steps]
        if repeat == 0:
            totals = steps
        else:
            totals = [
                product_f32(two_terms(total), s) for total, s in zip(totals, step_terms)
            ]
        if repeat < NS_STEPS - 1:
            inner = [product_f32(s, t) for s, t in zip(step_terms, terms)]
            squares = [product_f32(two_terms(v), s) for v, s in zip(inner, step_terms)]
    for i in range(count):
        result = (totals[i] * scales[i]).astype(out_ref.dtype)
        out_ref[i, 0] = result[:HALF, :HALF]
        out_ref[i, 1] = result[:HALF, HALF:]
        out_ref[i, 2] = result[HALF:, HALF:]


def newton(pieces):
    count = pieces[0].shape[0]
    return pl.pallas_call(
        partial(newton_body, count),
        out_shape=jax.ShapeDtypeStruct((count, 3, HALF, HALF), jnp.bfloat16),
        cost_estimate=pl.CostEstimate(
            flops=count * 17 * 6 * HEAD_SIZE**3, bytes_accessed=count * 2**20, transcendentals=0
        ),
        compiler_params=pltpu.CompilerParams(vmem_limit_bytes=40 * 1024 * 1024),
    )(*pieces)


def apply_body(state_ref, factor_ref, out_ref):
    upper = factor_ref[0, 1].astype(jnp.float32)
    factor = jnp.concatenate(
        [
            jnp.concatenate([factor_ref[0, 0], factor_ref[0, 1]], axis=1),
            jnp.concatenate([upper.T.astype(jnp.bfloat16), factor_ref[0, 2]], axis=1),
        ],
        axis=0,
    )
    high, low = two_terms(state_ref[...])
    out_ref[...] = product(high, factor) + product(low, factor)


def apply_factor(state, factors, start):
    rows, cols = state.shape
    return pl.pallas_call(
        apply_body,
        grid=(cols // HEAD_SIZE,),
        in_specs=[
            pl.BlockSpec((rows, HEAD_SIZE), lambda step: (0, step)),
            pl.BlockSpec((1, 3, HALF, HALF), lambda step: (step + start, 0, 0, 0)),
        ],
        out_specs=pl.BlockSpec((rows, HEAD_SIZE), lambda step: (0, step)),
        out_shape=jax.ShapeDtypeStruct((rows, cols), jnp.float32),
        cost_estimate=pl.CostEstimate(
            flops=4 * rows * cols * HEAD_SIZE, bytes_accessed=8 * rows * cols, transcendentals=0
        ),
        compiler_params=pltpu.CompilerParams(vmem_limit_bytes=40 * 1024 * 1024),
    )(state, factors)


VMEM_BYTES = 50 * 1024 * 1024


def dense_call(body, grid, in_specs, out_specs, out_shape, flops, *operands):
    outs = out_shape if isinstance(out_shape, (list, tuple)) else [out_shape]
    moved = sum(v.size * v.dtype.itemsize for v in operands) + sum(
        v.size * v.dtype.itemsize for v in outs
    )
    return pl.pallas_call(
        body,
        grid=grid,
        in_specs=in_specs,
        out_specs=out_specs,
        out_shape=out_shape,
        cost_estimate=pl.CostEstimate(flops=flops, bytes_accessed=moved, transcendentals=0),
        compiler_params=pltpu.CompilerParams(vmem_limit_bytes=VMEM_BYTES),
    )(*operands)


def column_tile(width):
    return width if width % 768 else 768


def enter_body(rows_ref, gate_ref, up_ref, hidden_ref, gelu_ref, pull_ref):
    rows = rows_ref[...]
    gate = product(rows, gate_ref[...])
    up = product(rows, up_ref[...])
    factor = (2.0 / jnp.pi) ** 0.5
    squared = gate * gate
    bend = jnp.tanh(factor * (gate + 0.044715 * gate * squared))
    upper = 0.5 * (1.0 + bend)
    gelu = gate * upper
    slope = upper + 0.5 * gate * (1.0 - bend * bend) * (factor * (1.0 + 0.134145 * squared))
    hidden_ref[...] = (gelu * up).astype(jnp.bfloat16)
    gelu_ref[...] = gelu.astype(jnp.bfloat16)
    pull_ref[...] = (up * slope).astype(jnp.bfloat16)


def enter(rows, gate, up):
    count, width = rows.shape
    pieces, _, cols = gate.shape
    tile = column_tile(cols)
    weight = pl.BlockSpec((None, width, tile), lambda p, j, i: (p, 0, j))
    out = pl.BlockSpec((None, 256, tile), lambda p, j, i: (p, i, j))
    return dense_call(
        enter_body,
        (pieces, cols // tile, count // 256),
        [pl.BlockSpec((256, width), lambda p, j, i: (i, 0)), weight, weight],
        [out] * 3,
        [jax.ShapeDtypeStruct((pieces, count, cols), jnp.bfloat16)] * 3,
        4 * count * width * cols * pieces,
        rows,
        gate,
        up,
    )


def leave_body(rows_ref, down_ref, gelu_ref, pull_ref, gate_ref, up_ref):
    delta = product(rows_ref[...], down_ref[...])
    gate_ref[...] = (delta * pull_ref[...].astype(jnp.float32)).astype(jnp.bfloat16)
    up_ref[...] = (delta * gelu_ref[...].astype(jnp.float32)).astype(jnp.bfloat16)


def leave(rows, down, gelu, pull):
    count, width = rows.shape
    pieces, _, cols = down.shape
    tile = column_tile(cols)
    out = pl.BlockSpec((None, 256, tile), lambda p, j, i: (p, i, j))
    return dense_call(
        leave_body,
        (pieces, cols // tile, count // 256),
        [
            pl.BlockSpec((256, width), lambda p, j, i: (i, 0)),
            pl.BlockSpec((None, width, tile), lambda p, j, i: (p, 0, j)),
            out,
            out,
        ],
        [out] * 2,
        [jax.ShapeDtypeStruct((pieces, count, cols), jnp.bfloat16)] * 2,
        2 * count * width * cols * pieces,
        rows,
        down,
        gelu,
        pull,
    )


def shrink_body(count, *refs):
    pieces = refs[0].shape[0]
    total = None
    for i in range(count):
        for p in range(pieces):
            term = contract_last(refs[i][p], refs[count + i][p])
            total = term if total is None else total + term
    refs[-1][...] = total.astype(refs[-1].dtype)


def shrink(lefts, rights, rows, part, dtype):
    pieces, width, cols = rights[0].shape
    count = len(lefts)
    tile = 768 if cols < 768 else 256
    return dense_call(
        partial(shrink_body, count),
        (width // tile,),
        [pl.BlockSpec((pieces, rows, cols), lambda j: (0, part, 0))] * count
        + [pl.BlockSpec((pieces, tile, cols), lambda j: (0, j, 0))] * count,
        pl.BlockSpec((rows, tile), lambda j: (0, j)),
        jax.ShapeDtypeStruct((rows, width), dtype),
        2 * rows * width * cols * pieces * count,
        *lefts,
        *rights,
    )


def outer_body(left_ref, right_ref, out_ref):
    left = left_ref[...]
    for p in range(out_ref.shape[0]):
        out_ref[p] = contract_first(left, right_ref[p]).astype(jnp.bfloat16)


def outer(left, right):
    rows, width = left.shape
    pieces, _, cols = right.shape
    tile = 384 if cols < 768 else 256
    return dense_call(
        outer_body,
        (width // tile,),
        [
            pl.BlockSpec((rows, tile), lambda j: (0, j)),
            pl.BlockSpec((pieces, rows, cols), lambda j: (0, 0, 0)),
        ],
        pl.BlockSpec((pieces, tile, cols), lambda j: (0, j, 0)),
        jax.ShapeDtypeStruct((pieces, width, cols), jnp.bfloat16),
        2 * pieces * rows * width * cols,
        left,
        right,
    )


def fence(*values):
    return lax.optimization_barrier(values)


def after(value, *others):
    return lax.optimization_barrier((value,) + others)[0]


class Plain:
    def __init__(self, sizes):
        self.owners = sizes["dp"]
        self.token_spec = P(("dp", "tensor"), None)
        self.length_spec = P("dp", None)
        self.weight_spec = P("dp", "tensor")
        self.every = ("dp", "tensor")

    def setup(self):
        self.part = lax.axis_index("tensor")

    def gather_dp(self, shard):
        return lax.all_gather(shard, "dp", axis=0, tiled=True)

    def scatter_dp(self, partial_sum):
        return wide(lax.psum_scatter(partial_sum, "dp", scatter_dimension=0, tiled=True))

    def open(self, normed, mixed, out, gate, up, down, moments):
        self.later = {"up": up, "down": down}
        return (
            self.attn_rows(normed),
            self.gather_dp(mixed),
            self.gather_dp(out),
            self.gather_dp(gate)[None],
        )

    def beside(self, values, name):
        return values, self.gather_dp(self.later[name])[None]

    def beside_hidden(self, values):
        return values

    def attn_rows(self, values):
        return lax.all_gather(values, "tensor", axis=0, tiled=True)

    def attn_sum(self, values):
        return lax.psum_scatter(values, "tensor", scatter_dimension=0, tiled=True)

    def features_in(self, values):
        return values

    def features_out(self, values):
        return values

    def mlp_sum_rows(self, partial_sums):
        return self.scatter_dp(partial_sums[0])

    def close(self, partial_out, attention_backward, totals, moments):
        partial_mixed, partial_normed = attention_backward(partial_out)[:2]
        cuts = (moments[0].shape[1], moments[0].shape[1] + moments[1].shape[1])
        grads = jnp.split(self.scatter_dp(partial_mixed), cuts, axis=1)
        grads = (*grads, self.scatter_dp(partial_out), totals[1], totals[2], totals[0])
        states = [momentum_decay * m + g for m, g in zip(moments, grads)]
        first = muon(self, states[6:] + states[4:5])
        last = muon(self, states[5:6] + states[:4])
        updates = (*last[1:], first[1], last[0], first[0])
        return grads, states, updates, self.attn_sum(partial_normed)

    def finish_gains(self, gains):
        return self.sum_every(gains)

    def sum_every(self, values):
        return lax.psum(values, self.every)

    def mlp_rows(self, values):
        return self.attn_rows(values)

    def mlp_sum(self, lefts, rights):
        values = shrink(lefts, rights, lefts[0].shape[1], 0, jnp.float32)
        return self.attn_sum(values), values

    def gram_sum(self, values):
        return [lax.psum_scatter(values, "dp", scatter_dimension=0, tiled=True)]

    def factor_gather(self, values):
        return lax.all_gather(values, "dp", axis=0, tiled=True)


def shift(values, axis, distance):
    size = lax.axis_size(axis)
    return lax.ppermute(values, axis, [(i, (i + distance) % size) for i in range(size)])


def pick(stacked, index):
    return lax.dynamic_index_in_dim(stacked, index, 0, keepdims=False)


def wide(values):
    return values.astype(jnp.float32)


def narrow(values):
    return values.astype(jnp.bfloat16)


def place(buffer, values, *index):
    fresh = values.reshape((1,) * len(index) + values.shape)
    zero = jnp.zeros((), jnp.int32)
    return lax.dynamic_update_slice(buffer, fresh, tuple(index) + (zero,) * values.ndim)


class Grid:
    def __init__(self, sizes):
        self.depth = sizes["z"]
        self.owners = sizes["z"] * sizes["x"]
        self.token_spec = P(("z", "x", "y", "c"), None)
        self.length_spec = P(("z", "x"), None)
        self.weight_spec = P(("z", "x"), ("y", "c"))
        self.every = ("z", "x", "y", "c")

    def setup(self):
        self.z, self.x, self.y, self.c = (lax.axis_index(a) for a in self.every)
        self.part = self.y * 2 + self.c


    def features_in(self, values):
        split = values.reshape(values.shape[:-1] + (self.depth, 2, -1))
        return jnp.swapaxes(split, -3, -2).reshape(values.shape)

    def features_out(self, values):
        split = values.reshape(values.shape[:-1] + (2, self.depth, -1))
        return jnp.swapaxes(split, -3, -2).reshape(values.shape)

    def back(self, distance):
        return lax.rem(self.z + self.depth - distance, self.depth)

    def ahead(self, distance):
        return lax.rem(self.z + distance, self.depth)

    def open(self, normed, mixed, out, gate, up, down, moments):
        attn = jnp.concatenate([mixed, out], axis=1)
        line = [attn, shift(attn, "z", 1)]
        across = [shift(attn, "x", 1)]
        over = shift(normed, "y", 1)
        across[0], line[1], over, gate, up = fence(across[0], line[1], over, gate, up)

        across.append(shift(line[1], "x", 1))
        line.append(shift(line[1], "z", 1))
        pair = shift(jnp.concatenate([normed, over], axis=0), "c", 1)
        gate_sent = self.send(self.quarters(gate))
        across[1], line[2], pair, up, down, *gate_sent = fence(
            across[1], line[2], pair, up, down, *gate_sent
        )

        across.append(shift(line[2], "x", 1))
        line.append(shift(line[2], "z", 1))
        up_sent = self.send(self.quarters(up))
        across[2], line[3], down, gate_sent, up_sent, moments = lax.optimization_barrier(
            (across[2], line[3], down, gate_sent, up_sent, moments)
        )

        across.append(shift(line[3], "x", 1))
        gate_arrived = self.arrive(gate_sent)
        down_sent = self.send(self.quarters(down))
        inner = [self.main_quarters(narrow(m)) for m in moments]
        inner_sent = [
            self.send(jnp.concatenate([inner[0], inner[1]], axis=2)),
            self.send(inner[2]),
        ]
        across[3], gate_arrived, up_sent, down_sent, inner_sent = lax.optimization_barrier(
            (across[3], gate_arrived, up_sent, down_sent, inner_sent)
        )
        self.sent = {"up": up_sent, "down": down_sent}
        self.inner_sent = inner_sent

        mixed_cols = mixed.shape[1]
        full = jnp.zeros((2, self.depth) + attn.shape, attn.dtype)
        for k in range(self.depth):
            full = place(full, line[k], self.x, self.back(k))
            full = place(full, across[k], 1 - self.x, self.back(k))
        full, gate_column = fence(full.reshape((-1,) + attn.shape[1:]), self.column(gate_arrived))
        return (
            self.order_rows(normed, over, pair),
            full[:, :mixed_cols],
            full[:, mixed_cols:],
            self.gather_plane(gate_column),
        )

    def beside(self, values, name):
        arrived = self.arrive(self.sent[name])
        values, arrived = lax.optimization_barrier((values, arrived))
        values, column, self.sent = lax.optimization_barrier(
            (values, self.column(arrived), self.sent)
        )
        return values, self.gather_plane(column)

    def beside_hidden(self, values):
        arrived = self.arrive(self.inner_sent[0])
        values, arrived, last = lax.optimization_barrier((values, arrived, self.inner_sent[1]))
        self.inner_sent = last
        self.inner = jnp.split(self.column(arrived), 2, axis=2)
        return values


    def main_quarters(self, shard):
        rows, cols = shard.shape
        self.main = cols // (self.depth * HEAD_SIZE) * HEAD_SIZE
        main = shard[:, : self.depth * self.main]
        return main.reshape(rows, self.depth, self.main).transpose(1, 0, 2)

    def quarters(self, shard):
        main = self.main_quarters(shard)
        rest = shard[:, self.depth * self.main :]
        rest = rest.reshape(shard.shape[0], self.depth, -1).transpose(1, 0, 2)
        return jnp.concatenate([main, rest], axis=2)

    def send(self, chunks):
        return [pick(chunks, self.ahead(k)) for k in range(self.depth)]

    def arrive(self, sent):
        return [sent[0]] + [shift(sent[k], "z", k) for k in range(1, self.depth)]

    def column(self, arrived):
        column = jnp.zeros((self.depth,) + arrived[0].shape, arrived[0].dtype)
        for k, values in enumerate(arrived):
            column = place(column, values, self.back(k))
        return column

    def gather_plane(self, column):
        full = lax.all_gather(column, ("y", "x"), axis=0, tiled=True)
        return full.reshape(2, 2 * self.depth * column.shape[1], -1)

    def order_rows(self, own, over, pair):
        rows = own.shape[0]
        near, far = pair[:rows], pair[rows:]
        first = self.y == 0
        low_own, high_own = jnp.where(first, own, over), jnp.where(first, over, own)
        low_near, high_near = jnp.where(first, near, far), jnp.where(first, far, near)
        core = self.c == 0
        return jnp.concatenate(
            [
                jnp.where(core, low_own, low_near),
                jnp.where(core, low_near, low_own),
                jnp.where(core, high_own, high_near),
                jnp.where(core, high_near, high_own),
            ],
            axis=0,
        )

    def attn_rows(self, values):
        over = shift(values, "y", 1)
        pair = shift(jnp.concatenate([values, over], axis=0), "c", 1)
        return self.order_rows(values, over, pair)

    def core_half(self, values):
        stacked = values.reshape(2, 2, -1, values.shape[1]).transpose(1, 0, 2, 3)
        return pick(stacked, self.c), narrow(pick(stacked, 1 - self.c))

    def attn_sum(self, values):
        kept, sent = self.core_half(values)
        mine = kept + wide(shift(sent, "c", 1))
        return pick(mine, self.y) + wide(shift(narrow(pick(mine, 1 - self.y)), "y", 1))

    def mlp_sum_rows(self, partial_sums):
        stacked = partial_sums.reshape(4 * self.depth, -1, partial_sums.shape[-1])
        return lax.psum_scatter(stacked, ("y", "x"), scatter_dimension=0, tiled=True)

    def mlp_finish(self, arrived):
        column = self.column(arrived)
        rows = column.shape[1]
        main = column[:, :, : self.main].transpose(1, 0, 2).reshape(rows, -1)
        rest = column[:, :, self.main :].transpose(1, 0, 2).reshape(rows, -1)
        return wide(jnp.concatenate([main, rest], axis=1))

    def mlp_rows(self, values):
        line = jnp.concatenate([shift(values, "z", k) for k in range(1, self.depth)], axis=0)
        return jnp.concatenate([values, line, shift(values, "c", 1), shift(line, "c", 1)], axis=0)

    def mlp_sum(self, lefts, rights):
        rows = lefts[0].shape[1] // 2
        away = shrink(lefts, rights, rows, 1, jnp.bfloat16)
        received = shift(away, "c", 1)
        kept = shrink([after(v, away) for v in lefts], rights, rows, 0, jnp.bfloat16)
        mine = (wide(kept) + wide(received)).reshape(self.depth, -1, kept.shape[1])
        sent = [narrow(mine[k]) for k in range(1, self.depth)]
        own, *sent = fence(mine[0], *sent)
        arrived = [shift(v, "z", self.depth - k) for k, v in enumerate(sent, 1)]
        return own + sum(wide(v) for v in arrived), own

    def halves(self, values):
        stacked = values.reshape((2, -1) + values.shape[1:])
        return pick(stacked, self.x), pick(stacked, 1 - self.x)

    def main_grams(self, total, inner):
        state = momentum_decay * wide(inner) + wide(total[:, :, : self.main])
        return self.halves(grams([state.reshape(-1, self.main)], self.main // HEAD_SIZE))

    def close(self, partial_out, attention_backward, totals, moments):
        total_down, total_gate, total_up = totals

        stacked = partial_out.reshape(2, -1, partial_out.shape[1])
        kept_out, sent_out = pick(stacked, self.x), pick(stacked, 1 - self.x)
        down_sent = self.send(total_down)
        partial_out, sent_out, down_sent = lax.optimization_barrier(
            (partial_out, sent_out, down_sent)
        )
        received = shift(sent_out, "x", 1)
        turned_down = self.arrive(down_sent)
        backward = attention_backward(partial_out)
        backward, received, turned_down, total_gate = lax.optimization_barrier(
            (backward, received, turned_down, total_gate)
        )
        partial_mixed, partial_normed = backward
        out_rows = (wide(kept_out) + wide(received)).reshape(self.depth, -1, kept_out.shape[1])
        out_sent = self.send(narrow(out_rows))
        stacked = partial_mixed.reshape(2, -1, partial_mixed.shape[1])
        kept_mixed, sent_mixed = pick(stacked, self.x), pick(stacked, 1 - self.x)
        kept_normed, sent_normed = self.core_half(partial_normed)
        out_sent, sent_mixed, sent_normed = lax.optimization_barrier(
            (out_sent, sent_mixed, sent_normed)
        )

        received = shift(sent_mixed, "x", 1)
        out_arrived = self.arrive(out_sent)
        normed_received = shift(sent_normed, "c", 1)
        grad_down = self.mlp_finish(turned_down)
        kept_grams, sent_grams = zip(
            self.main_grams(total_down, self.inner[0]), self.main_grams(total_gate, self.inner[1])
        )
        kept_grams, sent_grams = jnp.concatenate(kept_grams), jnp.concatenate(sent_grams)
        received, out_arrived, normed_received, sent_grams, total_up = lax.optimization_barrier(
            (received, out_arrived, normed_received, sent_grams, total_up)
        )

        mixed_rows = (wide(kept_mixed) + wide(received)).reshape(
            self.depth, -1, kept_mixed.shape[1]
        )
        mixed_arrived = self.arrive(self.send(narrow(mixed_rows)))
        received_grams = shift(sent_grams, "x", 1)
        mine = kept_normed + wide(normed_received)
        normed_received = shift(narrow(pick(mine, 1 - self.y)), "y", 1)
        inner_arrived = self.arrive(self.inner_sent)
        grad_out = sum(wide(v) for v in out_arrived)
        both_sent = [jnp.concatenate(v, axis=0) for v in zip(self.send(total_gate), self.send(total_up))]
        (
            mixed_arrived,
            received_grams,
            normed_received,
            both_sent,
            inner_arrived,
        ) = lax.optimization_barrier(
            (mixed_arrived, received_grams, normed_received, both_sent, inner_arrived)
        )
        summed_normed = pick(mine, self.y) + wide(normed_received)

        both_arrived = self.arrive(both_sent)
        grad_mixed = sum(wide(v) for v in mixed_arrived)
        cuts = (moments[0].shape[1], moments[0].shape[1] + moments[1].shape[1])
        grads = [*jnp.split(grad_mixed, cuts, axis=1), grad_out]
        states = [momentum_decay * m + g for m, g in zip(moments, grads)]
        kept_attn, sent_attn = self.halves(grams(states, self.owners))
        received_attn = shift(sent_attn, "x", 1)
        kept_last, sent_last = self.main_grams(total_up, self.column(inner_arrived))
        received_last = shift(sent_last, "x", 1)
        both_arrived, received_attn, received_last = lax.optimization_barrier(
            (both_arrived, received_attn, received_last)
        )

        rows = both_arrived[0].shape[0] // 2
        grad_gate = self.mlp_finish([v[:rows] for v in both_arrived])
        grad_up = self.mlp_finish([v[rows:] for v in both_arrived])
        grads += [grad_gate, grad_up, grad_down]
        states += [momentum_decay * m + g for m, g in zip(moments[4:], grads[4:])]
        attn_arrived = self.arrive(self.send((kept_attn + received_attn)[:, None]))
        kept_rest, sent_rest = self.halves(
            grams([v[:, -HEAD_SIZE:] for v in states[4:]], self.owners)
        )
        received_rest = shift(sent_rest, "x", 1)
        main_factors = newton(
            [
                jnp.concatenate([kept_grams, kept_last]),
                jnp.concatenate([received_grams, received_last]),
            ]
        )
        attn_arrived, received_rest, main_factors = lax.optimization_barrier(
            (attn_arrived, received_rest, main_factors)
        )

        rest_arrived = self.arrive(self.send((kept_rest + received_rest)[:, None]))
        factors = jnp.concatenate([main_factors, newton(attn_arrived)])
        rest_arrived, factors = lax.optimization_barrier((rest_arrived, factors))

        line = self.along(factors)
        rest_factors = newton(rest_arrived)
        line, rest_factors = fence(line, rest_factors)

        across = shift(line, "x", 1)
        rest_line = self.along(rest_factors)
        across, rest_line = fence(across, rest_line)

        rest = self.both(rest_line, shift(rest_line, "x", 1))[:, :, 0]
        rest = rest.reshape((-1,) + rest.shape[2:])
        full = self.both(line, across)
        attn_factors = full[:, :, 3].reshape((-1,) + full.shape[3:])
        main = full[:, :, :3].transpose(2, 1, 0, 3, 4, 5).reshape((3, -1) + full.shape[3:])
        counts, starts = spans(states[:4])
        updates = [apply_factor(v, attn_factors, s) for v, s in zip(states[:4], starts)]
        for i, order in enumerate((1, 2, 0)):
            updates.append(
                apply_factor(
                    states[4 + i], jnp.concatenate([main[order], rest[i : i + 1]], axis=0), 0
                )
            )
        self.last = line
        return grads, states, updates, summed_normed

    def along(self, values):
        line = jnp.zeros((self.depth,) + values.shape, values.dtype)
        for k in range(self.depth):
            line = place(line, shift(values, "z", k) if k else values, self.back(k))
        return line

    def both(self, line, across):
        full = jnp.zeros((2,) + line.shape, line.dtype)
        return place(place(full, line, self.x), across, 1 - self.x)

    def finish_gains(self, gains):
        for axis in ("c", "y", "x"):
            gains = gains + shift(gains, axis, 1)
        return gains + sum(shift(gains, "z", k) for k in range(1, self.depth))


def muon(ways, states):
    counts, starts = spans(states)
    slots = -(-sum(counts) // ways.owners) * ways.owners
    factors = ways.factor_gather(newton(ways.gram_sum(grams(states, slots))))
    return [apply_factor(state, factors, start) for state, start in zip(states, starts)]


def shards(
    ways,
    tokens,
    cotangent,
    dealt_lengths,
    norm_gains,
    query_weight,
    key_matrix,
    value_matrix,
    out_weight,
    gate_weight,
    up_weight,
    down_weight,
    moment_query,
    moment_key,
    moment_value,
    moment_out,
    moment_gate,
    moment_up,
    moment_down,
):
    ways.setup()
    local_rows = tokens.shape[0]
    segment, position, is_alive = slot_layout(dealt_lengths[0])
    allowed = allowed_pairs(segment, is_alive)
    rotary_cosines, rotary_sines = rope_tables(position)
    my_alive = lax.dynamic_slice_in_dim(is_alive, ways.part * local_rows, local_rows)
    query_cols = query_weight.shape[1]
    kv_cols = key_matrix.shape[1]
    kv_heads = kv_cols // HEAD_SIZE
    group_width = QUERY_HEADS // KEY_VALUE_HEADS
    cuts = (query_cols, query_cols + kv_cols)

    norm_gains = ways.features_in(norm_gains)
    inputs = ways.features_in(tokens).astype(jnp.float32)
    normalized_input, inverse_in = norm_forward(inputs, norm_gains[0])
    normed_full, mixed_full, out_full, gate_full = ways.open(
        normalized_input.astype(jnp.bfloat16),
        jnp.concatenate([query_weight, key_matrix, value_matrix], axis=1),
        out_weight,
        gate_weight,
        up_weight,
        down_weight,
        (moment_down, moment_gate, moment_up),
    )
    projected = jnp.dot(normed_full, mixed_full, preferred_element_type=jnp.float32)
    projected_queries, projected_keys, projected_values = jnp.split(projected, cuts, axis=1)
    projected_queries = projected_queries.reshape(GROUP_SLOTS, -1, HEAD_SIZE)
    projected_keys = projected_keys.reshape(GROUP_SLOTS, kv_heads, HEAD_SIZE)
    value_rows_packed = projected_values.astype(jnp.bfloat16).reshape(
        GROUP_SLOTS, kv_heads, HEAD_SIZE
    )
    query_rows_rotated = (
        (apply_rotary(projected_queries, rotary_cosines, rotary_sines) * HEAD_SIZE ** (-0.5))
        .astype(jnp.bfloat16)
        .reshape(GROUP_SLOTS, kv_heads, group_width, HEAD_SIZE)
    )
    key_vectors = apply_rotary(projected_keys, rotary_cosines, rotary_sines).astype(jnp.bfloat16)
    tanh_part, masked = attention_scores(query_rows_rotated, key_vectors, allowed)
    row_max = jnp.max(masked, axis=-1, keepdims=True)
    exponent = jnp.exp(masked - row_max)
    row_total = jnp.sum(exponent, axis=-1, keepdims=True)
    prob_exact = exponent / row_total
    prob_low = prob_exact.astype(jnp.bfloat16)
    mixed_heads = (
        jnp.einsum(
            "kgts,skd->tkgd", prob_low, value_rows_packed, preferred_element_type=jnp.float32
        )
        .reshape(GROUP_SLOTS, query_cols)
        .astype(jnp.bfloat16)
    )
    partial_attended, up_full = ways.beside(contract_last(mixed_heads, out_full), "up")
    attended, down_full = ways.beside(ways.attn_sum(partial_attended), "down")
    normed_attn, inverse_attn = norm_forward(attended, norm_gains[1])
    middle = inputs + normed_attn
    normed_mid, inverse_mid = norm_forward(middle, norm_gains[2])
    mid_full = ways.mlp_rows(normed_mid.astype(jnp.bfloat16))
    hidden, activated, pulled = enter(mid_full, gate_full, up_full)
    hidden = ways.beside_hidden(hidden)
    feed_out, _ = ways.mlp_sum([hidden], [down_full])
    normed_feed, inverse_feed = norm_forward(feed_out, norm_gains[3])
    block_output = (middle + normed_feed).astype(jnp.bfloat16)

    upstream = jnp.where(my_alive[:, None], ways.features_in(cotangent).astype(jnp.float32), 0.0)
    delta_feed, gain_feed = norm_backward(feed_out, inverse_feed, norm_gains[3], upstream)
    feed_grad = ways.mlp_rows(delta_feed.astype(jnp.bfloat16))
    partial_down = outer(feed_grad, hidden)
    total_down = ways.mlp_sum_rows(partial_down)
    feed_grad = after(feed_grad, partial_down)
    delta_gate, delta_up = leave(feed_grad, down_full, activated, pulled)
    delta_mid, token = ways.mlp_sum([delta_gate, delta_up], [gate_full, up_full])
    mid_again = after(mid_full, token)
    total_gate = ways.mlp_sum_rows(outer(mid_again, delta_gate))
    total_up = ways.mlp_sum_rows(outer(mid_again, delta_up))

    mid_back, gain_mid = norm_backward(middle, inverse_mid, norm_gains[2], delta_mid)
    delta_middle = upstream + mid_back
    delta_attended, gain_attn = norm_backward(attended, inverse_attn, norm_gains[1], delta_middle)
    attn_grad = ways.attn_rows(delta_attended.astype(jnp.bfloat16))
    partial_out = narrow(contract_first(attn_grad, mixed_heads))

    def attention_backward(start):
        delta_mixed = (
            jnp.dot(after(attn_grad, start), out_full, preferred_element_type=jnp.float32)
            .astype(jnp.bfloat16)
            .reshape(GROUP_SLOTS, kv_heads, group_width, HEAD_SIZE)
        )
        delta_prob = jnp.einsum(
            "tkgd,skd->kgts", delta_mixed, value_rows_packed, preferred_element_type=jnp.float32
        )
        delta_values = (
            jnp.einsum("kgts,tkgd->skd", prob_low, delta_mixed, preferred_element_type=jnp.float32)
            .reshape(GROUP_SLOTS, kv_cols)
            .astype(jnp.bfloat16)
        )
        row_inner = jnp.sum(prob_exact * delta_prob, axis=-1, keepdims=True)
        delta_raw = (
            jnp.where(allowed[None, None], prob_exact * (delta_prob - row_inner), 0.0)
            * (1.0 - tanh_part * tanh_part)
        ).astype(jnp.bfloat16)
        delta_queries = jnp.einsum(
            "kgts,skd->tkgd", delta_raw, key_vectors, preferred_element_type=jnp.float32
        ).reshape(GROUP_SLOTS, -1, HEAD_SIZE) * HEAD_SIZE ** (-0.5)
        delta_query_proj = (
            apply_rotary(delta_queries, rotary_cosines, -rotary_sines)
            .reshape(GROUP_SLOTS, query_cols)
            .astype(jnp.bfloat16)
        )
        delta_keys = jnp.einsum(
            "kgts,tkgd->skd", delta_raw, query_rows_rotated, preferred_element_type=jnp.float32
        )
        delta_key_proj = (
            apply_rotary(delta_keys, rotary_cosines, -rotary_sines)
            .reshape(GROUP_SLOTS, kv_cols)
            .astype(jnp.bfloat16)
        )
        delta_mixed_proj = jnp.concatenate([delta_query_proj, delta_key_proj, delta_values], axis=1)
        partial_mixed = narrow(contract_first(normed_full, delta_mixed_proj))
        return partial_mixed, contract_last(delta_mixed_proj, mixed_full)

    moments = (
        moment_query,
        moment_key,
        moment_value,
        moment_out,
        moment_gate,
        moment_up,
        moment_down,
    )
    grads, states, updates, delta_normed = ways.close(
        partial_out, attention_backward, (total_down, total_gate, total_up), moments
    )
    in_back, gain_in = norm_backward(inputs, inverse_in, norm_gains[0], delta_normed)
    input_grad = delta_middle + in_back
    gain_grads = ways.finish_gains(jnp.stack([gain_in, gain_attn, gain_mid, gain_feed]))
    return (
        ways.features_out(block_output),
        ways.features_out(input_grad),
        ways.features_out(gain_grads),
        *grads,
        *states,
        *updates,
    )


def solution(mesh):
    sizes = dict(mesh.shape)
    if sizes == {"dp": 8, "tensor": 4}:
        mesh = Mesh(mesh.devices.reshape(4, 2, 2, 2), ("z", "x", "y", "c"))
        ways = Grid(dict(mesh.shape))
    else:
        ways = Plain(sizes)
    token_spec, weight_spec = ways.token_spec, ways.weight_spec
    return jax.shard_map(
        partial(shards, ways),
        mesh=mesh,
        in_specs=(token_spec, token_spec, ways.length_spec, P()) + (weight_spec,) * 14,
        out_specs=(token_spec, token_spec, P()) + (weight_spec,) * 21,
        check_vma=False,
    )
```

time: 2230 us -> 1110 us (0.50)
  waiting for transfers between devices: 1550 us -> 385 us
  matrix products: 292 us -> 37 us
  starting transfers between devices: 10.8 us -> 213 us
  Pallas kernels: 0 us -> 149 us
  blocking collectives: 123 us -> 0 us
  other arithmetic: 59.4 us -> 91.5 us
  local copies, waits for them, and re-layouts: 172 us -> 202 us
    all_gather x12 -> x3, waiting for transfers between devices: 702 us -> 24.1 us  [gather_plane(): full = lax.all_gather(column, ('y', 'x'), axis=0, tiled=True)]
    unnamed x18 -> x6, waiting for transfers between devices: 605 us -> 0.1 us
    ppermute x0 -> x86, waiting for transfers between devices: none -> 360 us  [shift(): lax.ppermute(values, axis, [(i, (i + distance) % size) for i in range(siz...]
    ppermute x0 -> x86, starting transfers between devices: none -> 213 us  [shift(): lax.ppermute(values, axis, [(i, (i + distance) % size) for i in range(siz...]
    dot_general x41 -> x6, matrix products: 209 us -> 15.1 us  [the longest x1 5.83 us: shards(): jnp.dot(normed_full, mixed_full, preferred_element_type=jnp.float32)]
    pallas_call x0 -> x24, Pallas kernels: none -> 149 us  [the longest x9 105 us: dense_call(): pl.pallas_call(body, grid=grid, in_specs=in_specs, out_specs=out_specs, o...]
    reduce_scatter x4 -> x3, waiting for transfers between devices: 141 us -> 0.01 us  [mlp_sum_rows(): lax.psum_scatter(stacked, ('y', 'x'), scatter_dimension=0, tiled=True)]
    psum x1 -> x0, blocking collectives: 123 us -> none  [shards(): gain_grads = lax.psum(gain_rows, ('dp', 'tensor'))]
  transfers between devices with their start and end apart: 19 -> 92, of which waited for: 17 -> 40; matrix products, arithmetic and copies ran while one was open for 14% -> 25% of each run, Pallas kernels for 0% -> 11%
where the time goes in v1:
time: 1110 us; the launch traced here: 1100 us
  waiting for transfers between devices  385 us (35%)
  starting transfers between devices  213 us (19%)
  local copies, waits for them, and re-layouts  202 us (18%)
  Pallas kernels  149 us (13%)
  other arithmetic  91.5 us (8%)
  matrix products  37 us (3%)
  between operations  17.2 us (2%)
    ppermute x86, waiting for transfers between devices, shift(): lax.ppermute(values, axis, [(i, (i + distance) % size) for i in range(siz...  360 us
    ppermute x86, starting transfers between devices, shift(): lax.ppermute(values, axis, [(i, (i + distance) % size) for i in range(siz...  213 us
    pallas_call x9, Pallas kernels, dense_call(): pl.pallas_call(body, grid=grid, in_specs=in_specs, out_specs=out_specs, o...  105 us
    unnamed x348, local copies, waits for them, and re-layouts  61.9 us
    dynamic_update_slice x49, local copies, waits for them, and re-layouts, place(): lax.dynamic_update_slice(buffer, fresh, tuple(index) + (zero,) * values.n...  41.4 us
    all_gather x3, waiting for transfers between devices, gather_plane(): full = lax.all_gather(column, ('y', 'x'), axis=0, tiled=True)  24.1 us
  transfers between devices with their start and end apart: 92, of which 40 were waited for; matrix products, arithmetic and copies ran while one was open for 25% of the time, Pallas kernels for 11%

profile of v1, /device:TPU:0, one launch (start us, length us, event | category | flops | bytes accessed | tf_op | source)
XLA Modules:
  0.0 1095.3 jit_solution(16646573264516202035)
XLA Ops:
  29.3 7.4 collective-permute-done.2
  46.7 4.8 fusion.48
  70.4 4.8 fusion.44
  96.2 4.8 fusion.40
  110.5 8.7 fusion.23
  148.1 5.8 fusion.3
  167.5 5.5 fusion.12
  173.1 7.4 collective-permute-done.13
  191.6 8.4 collective-permute-start.17
  202.3 16.3 %collective-permute-done.16 = bf16[128,2304]{1,0:T(8,128)(2,1)S(1)} collective-permute-done((bf16[128,2304]{1,0:T(8,128)(2,1)S(1)}, bf16[128,2304]{1,0:T(8,128)(2,1)S(1)}, u32[]{:S(2)}, u32[]{:S(2)}) %collective-permute-start.16) | collective-permute-done | bytes 589856 | tf_op jit(solution)/shard_map/ppermute | solution.py:502
  220.0 4.2 collective-permute-done.18
  232.2 8.4 collective-permute-start.20
  243.5 13.8 %collective-permute-done.20 = bf16[128,2304]{1,0:T(8,128)(2,1)S(1)} collective-permute-done((bf16[128,2304]{1,0:T(8,128)(2,1)S(1)}, bf16[128,2304]{1,0:T(8,128)(2,1)S(1)}, u32[]{:S(2)}, u32[]{:S(2)}) %collective-permute-start.20) | collective-permute-done | bytes 589856 | tf_op jit(solution)/shard_map/ppermute | solution.py:502
  257.3 23.8 %collective-permute-done.21 = bf16[128,2304]{1,0:T(8,128)(2,1)S(1)} collective-permute-done((bf16[128,2304]{1,0:T(8,128)(2,1)S(1)}, bf16[128,2304]{1,0:T(8,128)(2,1)S(1)}, u32[]{:S(2)}, u32[]{:S(2)}) %collective-permute-start.21) | collective-permute-done | bytes 589856 | tf_op jit(solution)/shard_map/ppermute | solution.py:502
  281.3 13.3 %collective-permute-start.25 = (bf16[288,1024]{1,0:T(8,128)(2,1)}, bf16[288,1024]{1,0:T(8,128)(2,1)}, u32[]{:S(2)}, u32[]{:S(2)}) collective-permute-start(bf16[288,1024]{1,0:T(8,128)(2,1)} %bitcast.448), channel_id=1, source_target_pairs={{0,8},{8,16},{16,24},{24,0},{1,9},{9,17},{17,25},{25,1},{2,10},{10... | collective-permute-start | bytes 1769480 | tf_op jit(solution)/shard_map/ppermute | solution.py:502
  301.9 21.7 %shard_map.361 = (bf16[2,1024,576]{2,1,0:T(8,128)(2,1)S(1)}, bf16[2,1024,576]{2,1,0:T(8,128)(2,1)}, bf16[2,1024,576]{2,1,0:T(8,128)(2,1)}) custom-call(bf16[1024,2304]{1,0:T(8,128)(2,1)} %constant_dynamic-update-slice_fusion.4.rows_ref.left_ref, bf16[2,2304,576]{2,1,0:T(8,128)(2,1)} %bitcast.540, bf16[2,2304,576]{2,1,0:T(8,128)(2,1)} %bitcast.543), custom_call_target="tpu_custom_call" | custom-call | flops 10871635968 | bytes 22413312 | tf_op jit(solution)/shard_map/pallas_call | solution.py:283
  325.0 9.4 collective-permute-done.26
  334.5 24.1 %all-gather.8.cloned.1.call-done = bf16[16,288,576]{2,1,0:T(8,128)(2,1)} async-done(((bf16[4,288,576]{2,1,0:T(8,128)(2,1)}), bf16[16,288,576]{2,1,0:T(8,128)(2,1)}) %all-gather.8.cloned.1.call-update) | async-done | bytes 5308432 | tf_op jit(solution)/shard_map/all_gather | solution.py:641
  358.6 6.4 shard_map.362
  365.1 6.4 shard_map.363
  385.4 7.3 collective-permute-done.31
  392.8 24.8 %collective-permute-done.30 = bf16[128,2304]{1,0:T(8,128)(2,1)} collective-permute-done((bf16[128,2304]{1,0:T(8,128)(2,1)}, bf16[128,2304]{1,0:T(8,128)(2,1)}, u32[]{:S(2)}, u32[]{:S(2)}) %collective-permute-start.30) | collective-permute-done | bytes 589856 | tf_op jit(solution)/shard_map/ppermute | solution.py:502
  422.1 13.2 %collective-permute-start.32 = (bf16[128,2304]{1,0:T(8,128)(2,1)S(1)}, bf16[128,2304]{1,0:T(8,128)(2,1)S(1)}, u32[]{:S(2)}, u32[]{:S(2)}) collective-permute-start(bf16[128,2304]{1,0:T(8,128)(2,1)S(1)} %get-tuple-element.463), channel_id=1, source_target_pairs={{0,8},{8,16},{16,24},{24,0},{1,9},{9,17},{17,25},{25,1},{2,10},{10... | collective-permute-start | bytes 1769480 | tf_op jit(solution)/shard_map/ppermute | solution.py:502
  437.7 12.8 %collective-permute-done.32 = bf16[128,2304]{1,0:T(8,128)(2,1)S(1)} collective-permute-done((bf16[128,2304]{1,0:T(8,128)(2,1)S(1)}, bf16[128,2304]{1,0:T(8,128)(2,1)S(1)}, u32[]{:S(2)}, u32[]{:S(2)}) %collective-permute-start.32) | collective-permute-done | bytes 589856 | tf_op jit(solution)/shard_map/ppermute | solution.py:502
  450.5 24.3 %collective-permute-done.33 = bf16[128,2304]{1,0:T(8,128)(2,1)S(1)} collective-permute-done((bf16[128,2304]{1,0:T(8,128)(2,1)S(1)}, bf16[128,2304]{1,0:T(8,128)(2,1)S(1)}, u32[]{:S(2)}, u32[]{:S(2)}) %collective-permute-start.33) | collective-permute-done | bytes 589856 | tf_op jit(solution)/shard_map/ppermute | solution.py:502
  475.6 3.9 collective-permute-done.35
  482.9 10.8 shard_map.364
  493.9 14.4 %shard_map.365 = (bf16[2,1024,576]{2,1,0:T(8,128)(2,1)S(1)}, bf16[2,1024,576]{2,1,0:T(8,128)(2,1)}) custom-call(bf16[1024,2304]{1,0:T(8,128)(2,1)} %copy-done.120, bf16[2,2304,576]{2,1,0:T(8,128)(2,1)} %bitcast.480, bf16[2,1024,576]{2,1,0:T(8,128)(2,1)} %get-tuple-element.259.gelu_ref, bf16[2,1024,576]{2,1,0:T(8,128)(2,1)} %get-tuple-element.260.pull_ref), custom_call_target="tpu_custom_call" | custom-call | flops 5435817984 | bytes 19464192 | tf_op jit(solution)/shard_map/pallas_call | solution.py:283
  509.8 11.9 %shard_map.366 = bf16[512,2304]{1,0:T(8,128)(2,1)S(1)} custom-call(bf16[2,1024,576]{2,1,0:T(8,128)(2,1)} %copy-done.20, bf16[2,1024,576]{2,1,0:T(8,128)(2,1)} %get-tuple-element.264.refs_1_.right_ref, bf16[2,2304,576]{2,1,0:T(8,128)(2,1)} %bitcast.541, bf16[2,2304,576]{2,1,0:T(8,128)(2,1)} %bitcast.544), custom_call_target="tpu_custom_call" | custom-call | flops 5435817984 | bytes 17694720 | tf_op jit(solution)/shard_map/pallas_call | solution.py:283
  522.0 11.4 %shard_map.367 = bf16[512,2304]{1,0:T(8,128)(2,1)S(1)} custom-call(bf16[2,1024,576]{2,1,0:T(8,128)(2,1)} %copy-done.20, bf16[2,1024,576]{2,1,0:T(8,128)(2,1)} %get-tuple-element.264.refs_1_.right_ref, bf16[2,2304,576]{2,1,0:T(8,128)(2,1)} %bitcast.542, bf16[2,2304,576]{2,1,0:T(8,128)(2,1)} %bitcast.545), custom_call_target="tpu_custom_call" | custom-call | flops 5435817984 | bytes 17694720 | tf_op jit(solution)/shard_map/pallas_call | solution.py:283
  537.4 10.8 shard_map.368
  548.3 12.7 %collective-permute-start.40 = (bf16[128,2304]{1,0:T(8,128)(2,1)}, bf16[128,2304]{1,0:T(8,128)(2,1)S(1)}, u32[]{:S(2)}, u32[]{:S(2)}) collective-permute-start(bf16[128,2304]{1,0:T(8,128)(2,1)} %get-tuple-element.268), channel_id=1, source_target_pairs={{0,8},{8,16},{16,24},{24,0},{1,9},{9,17},{17,25},{25,1},{2,10},{10... | collective-permute-start | bytes 1769480 | tf_op jit(solution)/shard_map/ppermute | solution.py:502
  563.4 13.7 %collective-permute-done.40 = bf16[128,2304]{1,0:T(8,128)(2,1)S(1)} collective-permute-done((bf16[128,2304]{1,0:T(8,128)(2,1)}, bf16[128,2304]{1,0:T(8,128)(2,1)S(1)}, u32[]{:S(2)}, u32[]{:S(2)}) %collective-permute-start.40) | collective-permute-done | bytes 589856 | tf_op jit(solution)/shard_map/ppermute | solution.py:502
  577.1 24.9 %collective-permute-done.39 = bf16[128,2304]{1,0:T(8,128)(2,1)S(1)} collective-permute-done((bf16[128,2304]{1,0:T(8,128)(2,1)}, bf16[128,2304]{1,0:T(8,128)(2,1)S(1)}, u32[]{:S(2)}, u32[]{:S(2)}) %collective-permute-start.39) | collective-permute-done | bytes 589856 | tf_op jit(solution)/shard_map/ppermute | solution.py:502
  608.2 20.0 %collective-permute-done.41 = bf16[128,2304]{1,0:T(8,128)(2,1)S(1)} collective-permute-done((bf16[128,2304]{1,0:T(8,128)(2,1)S(1)}, bf16[128,2304]{1,0:T(8,128)(2,1)S(1)}, u32[]{:S(2)}, u32[]{:S(2)}) %collective-permute-start.41) | collective-permute-done | bytes 589856 | tf_op jit(solution)/shard_map/ppermute | solution.py:502
  640.5 11.2 %shard_map.371 = bf16[2,2304,576]{2,1,0:T(8,128)(2,1)} custom-call(bf16[1024,2304]{1,0:T(8,128)(2,1)} %constant_dynamic-update-slice_fusion.4.rows_ref.left_ref, bf16[2,1024,576]{2,1,0:T(8,128)(2,1)S(1)} %copy-done.19), custom_call_target="tpu_custom_call" | custom-call | flops 5435817984 | bytes 12386304 | tf_op jit(solution)/shard_map/pallas_call | solution.py:283
  680.5 7.3 fusion.1
  687.9 13.9 %collective-permute-start.44 = (bf16[288,576]{1,0:T(8,128)(2,1)S(1)}, bf16[288,576]{1,0:T(8,128)(2,1)S(1)}, u32[]{:S(2)}, u32[]{:S(2)}) collective-permute-start(bf16[288,576]{1,0:T(8,128)(2,1)S(1)} %copy-done.102), channel_id=1, source_target_pairs={{0,8},{8,16},{16,24},{24,0},{1,9},{9,17},{17,25},{25,1},{2,10},{10... | collective-permute-start | bytes 995336 | tf_op jit(solution)/shard_map/ppermute | solution.py:502
  704.2 4.6 convolution_convert_fusion
  710.7 13.7 %collective-permute-done.45 = bf16[288,576]{1,0:T(8,128)(2,1)S(1)} collective-permute-done((bf16[288,576]{1,0:T(8,128)(2,1)S(1)}, bf16[288,576]{1,0:T(8,128)(2,1)S(1)}, u32[]{:S(2)}, u32[]{:S(2)}) %collective-permute-start.45) | collective-permute-done | bytes 331808 | tf_op jit(solution)/shard_map/ppermute | solution.py:502
  737.2 6.6 collective-permute-start.48
  761.8 5.8 collective-permute-done.49
  767.6 5.9 collective-permute-start.59
  773.5 25.3 %collective-permute-done.47 = bf16[1152,1024]{1,0:T(8,128)(2,1)} collective-permute-done((bf16[1152,1024]{1,0:T(8,128)(2,1)}, bf16[1152,1024]{1,0:T(8,128)(2,1)}, u32[]{:S(2)}, u32[]{:S(2)}) %collective-permute-start.47) | collective-permute-done | bytes 2359328 | tf_op jit(solution)/shard_map/ppermute | solution.py:502
  819.5 6.0 collective-permute-done.55
  825.4 19.4 %collective-permute-done.53 = bf16[288,1024]{1,0:T(8,128)(2,1)S(1)} collective-permute-done((bf16[288,1024]{1,0:T(8,128)(2,1)S(1)}, bf16[288,1024]{1,0:T(8,128)(2,1)S(1)}, u32[]{:S(2)}, u32[]{:S(2)}) %collective-permute-start.53) | collective-permute-done | bytes 589856 | tf_op jit(solution)/shard_map/ppermute | solution.py:502
  845.5 13.2 %collective-permute-start.66 = (bf16[576,576]{1,0:T(8,128)(2,1)}, bf16[576,576]{1,0:T(8,128)(2,1)}, u32[]{:S(2)}, u32[]{:S(2)}) collective-permute-start(bf16[576,576]{1,0:T(8,128)(2,1)} %pad_maximum_fusion.11), channel_id=1, source_target_pairs={{0,8},{8,16},{16,24},{24,0},{1,9},{9,17},{17,25},{25,1},{2,10},{10... | collective-permute-start | bytes 1990664 | tf_op jit(solution)/shard_map/ppermute | solution.py:502
  878.1 9.7 collective-permute-done.62
  903.2 5.6 collective-permute-done.67
  927.6 3.8 multiply_add_fusion.2
  938.7 16.4 %collective-permute-start.71 = (f32[1,3,128,128]{3,2,1,0:T(8,128)S(1)}, f32[1,3,128,128]{3,2,1,0:T(8,128)S(1)}, u32[]{:S(2)}, u32[]{:S(2)}) collective-permute-start(f32[1,3,128,128]{3,2,1,0:T(8,128)S(1)} %get-tuple-element.553), channel_id=1, source_target_pairs={{0,8},{8,16},{16,24},{24,0},{1,9},{9,17},{17,25},{25,1},{2,10},{10... | collective-permute-start | bytes 589832 | tf_op jit(solution)/shard_map/ppermute | solution.py:502
  958.8 6.0 shard_map.375
  966.4 3.7 collective-permute-done.72.refs_2_
  970.3 5.1 collective-permute-start.75
  977.8 4.2 shard_map.376
  982.9 5.3 collective-permute-done.76.refs_2_
  988.6 5.2 collective-permute-start.78
  999.6 4.2 shard_map.377
  1008.5 13.5 %collective-permute-done.79 = bf16[4,3,128,128]{3,2,1,0:T(8,128)(2,1)S(1)} collective-permute-done((bf16[4,3,128,128]{3,2,1,0:T(8,128)(2,1)S(1)}, bf16[4,3,128,128]{3,2,1,0:T(8,128)(2,1)S(1)}, u32[]{:S(2)}, u32[]{:S(2)}) %collective-permute-start.79) | collective-permute-done | bytes 393248 | tf_op jit(solution)/shard_map/ppermute | solution.py:502
  1031.7 7.6 collective-permute-start.82
  1047.2 13.0 %collective-permute-done.81 = bf16[4,4,3,128,128]{4,3,2,0,1:T(8,128)(2,1)} collective-permute-done((bf16[4,4,3,128,128]{4,3,2,0,1:T(8,128)(2,1)}, bf16[4,4,3,128,128]{4,3,2,0,1:T(8,128)(2,1)}, u32[]{:S(2)}, u32[]{:S(2)}) %collective-permute-start.81) | collective-permute-done | bytes 1572896 | tf_op jit(solution)/shard_map/ppermute | solution.py:502
  1071.8 5.3 shard_map.382
  1077.2 5.3 shard_map.383
  1082.6 5.3 shard_map.384
  (756 shorter events, 403.7 us)
Async XLA Ops:
  7.2 294.7 %all-gather.4.cloned.1.call-start = ((), (), s32[]{:S(2)}) async-start(), calls=%async_computation.3 | async-start | bytes 7372800 | tf_op jit(solution)/shard_map/all_gather | solution.py:641
  13.9 22.9 %collective-permute-start = (bf16[288,1536]{1,0:T(8,128)(2,1)}, bf16[288,1536]{1,0:T(8,128)(2,1)}, u32[]{:S(2)}, u32[]{:S(2)}) collective-permute-start(bf16[288,1536]{1,0:T(8,128)(2,1)} %constant_dynamic-update-slice_fusion), channel_id=1, source_target_pairs={{0,4},{4,0},{1,5},{5,1},{2,6},{6,2},{3,7},{7,3},{8,12},{12,8},{9,1... | collective-permute-start | bytes 2654216 | tf_op jit(solution)/shard_map/ppermute | solution.py:502
  16.8 23.3 %collective-permute-start.1 = (bf16[288,1536]{1,0:T(8,128)(2,1)}, bf16[288,1536]{1,0:T(8,128)(2,1)}, u32[]{:S(2)}, u32[]{:S(2)}) collective-permute-start(bf16[288,1536]{1,0:T(8,128)(2,1)} %constant_dynamic-update-slice_fusion), channel_id=1, source_target_pairs={{0,8},{8,16},{16,24},{24,0},{1,9},{9,17},{17,25},{25,1},{2,10},{10... | collective-permute-start | bytes 2654216 | tf_op jit(solution)/shard_map/ppermute | solution.py:502
  40.1 20.6 %collective-permute-start.3 = (bf16[288,1536]{1,0:T(8,128)(2,1)}, bf16[288,1536]{1,0:T(8,128)(2,1)}, u32[]{:S(2)}, u32[]{:S(2)}) collective-permute-start(bf16[288,1536]{1,0:T(8,128)(2,1)} %collective-permute-done.1), channel_id=1, source_target_pairs={{0,4},{4,0},{1,5},{5,1},{2,6},{6,2},{3,7},{7,3},{8,12},{12,8},{9,1... | collective-permute-start | bytes 2654216 | tf_op jit(solution)/shard_map/ppermute | solution.py:502
  40.6 22.4 %collective-permute-start.4 = (bf16[288,1536]{1,0:T(8,128)(2,1)}, bf16[288,1536]{1,0:T(8,128)(2,1)}, u32[]{:S(2)}, u32[]{:S(2)}) collective-permute-start(bf16[288,1536]{1,0:T(8,128)(2,1)} %collective-permute-done.1), channel_id=1, source_target_pairs={{0,8},{8,16},{16,24},{24,0},{1,9},{9,17},{17,25},{25,1},{2,10},{10... | collective-permute-start | bytes 2654216 | tf_op jit(solution)/shard_map/ppermute | solution.py:502
  64.3 20.9 %collective-permute-start.7 = (bf16[288,1536]{1,0:T(8,128)(2,1)}, bf16[288,1536]{1,0:T(8,128)(2,1)}, u32[]{:S(2)}, u32[]{:S(2)}) collective-permute-start(bf16[288,1536]{1,0:T(8,128)(2,1)} %collective-permute-done.4), channel_id=1, source_target_pairs={{0,8},{8,16},{16,24},{24,0},{1,9},{9,17},{17,25},{25,1},{2,10},{10... | collective-permute-start | bytes 2654216 | tf_op jit(solution)/shard_map/ppermute | solution.py:502
  88.0 47.7 %collective-permute-start.8 = (bf16[288,1536]{1,0:T(8,128)(2,1)}, bf16[288,1536]{1,0:T(8,128)(2,1)}, u32[]{:S(2)}, u32[]{:S(2)}) collective-permute-start(bf16[288,1536]{1,0:T(8,128)(2,1)} %collective-permute-done.7), channel_id=1, source_target_pairs={{0,4},{4,0},{1,5},{5,1},{2,6},{6,2},{3,7},{7,3},{8,12},{12,8},{9,1... | collective-permute-start | bytes 2654216 | tf_op jit(solution)/shard_map/ppermute | solution.py:502
  89.0 46.8 %collective-permute-start.9 = (bf16[288,576]{1,0:T(8,128)(2,1)}, bf16[288,576]{1,0:T(8,128)(2,1)}, u32[]{:S(2)}, u32[]{:S(2)}) collective-permute-start(bf16[288,576]{1,0:T(8,128)(2,1)} %bitcast.460), channel_id=1, source_target_pairs={{0,8},{8,16},{16,24},{24,0},{1,9},{9,17},{17,25},{25,1},{2,10},{10... | collective-permute-start | bytes 995336 | tf_op jit(solution)/shard_map/ppermute | solution.py:502
  89.0 46.8 %collective-permute-start.10 = (bf16[288,576]{1,0:T(8,128)(2,1)}, bf16[288,576]{1,0:T(8,128)(2,1)}, u32[]{:S(2)}, u32[]{:S(2)}) collective-permute-start(bf16[288,576]{1,0:T(8,128)(2,1)} %bitcast.459), channel_id=1, source_target_pairs={{0,16},{8,24},{16,0},{24,8},{1,17},{9,25},{17,1},{25,9},{2,18},{10... | collective-permute-start | bytes 995336 | tf_op jit(solution)/shard_map/ppermute | solution.py:502
  90.7 45.0 %collective-permute-start.11 = (bf16[288,576]{1,0:T(8,128)(2,1)}, bf16[288,576]{1,0:T(8,128)(2,1)}, u32[]{:S(2)}, u32[]{:S(2)}) collective-permute-start(bf16[288,576]{1,0:T(8,128)(2,1)} %bitcast.458), channel_id=1, source_target_pairs={{0,24},{8,0},{16,8},{24,16},{1,25},{9,1},{17,9},{25,17},{2,26},{10... | collective-permute-start | bytes 995336 | tf_op jit(solution)/shard_map/ppermute | solution.py:502
  142.6 159.3 %all-gather.6.cloned.1.call-start = ((), (), s32[]{:S(2)}) async-start(), calls=%async_computation.4 | async-start | bytes 7372800 | tf_op jit(solution)/shard_map/all_gather | solution.py:641
  156.2 24.2 %collective-permute-start.13 = (bf16[288,576]{1,0:T(8,128)(2,1)}, bf16[288,576]{1,0:T(8,128)(2,1)S(1)}, u32[]{:S(2)}, u32[]{:S(2)}) collective-permute-start(bf16[288,576]{1,0:T(8,128)(2,1)} %bitcast.535), channel_id=1, source_target_pairs={{0,16},{8,24},{16,0},{24,8},{1,17},{9,25},{17,1},{25,9},{2,18},{10... | collective-permute-start | bytes 995336 | tf_op jit(solution)/shard_map/ppermute | solution.py:502
  158.0 22.4 %collective-permute-start.14 = (bf16[288,576]{1,0:T(8,128)(2,1)}, bf16[288,576]{1,0:T(8,128)(2,1)S(1)}, u32[]{:S(2)}, u32[]{:S(2)}) collective-permute-start(bf16[288,576]{1,0:T(8,128)(2,1)} %bitcast.534), channel_id=1, source_target_pairs={{0,24},{8,0},{16,8},{24,16},{1,25},{9,1},{17,9},{25,17},{2,26},{10... | collective-permute-start | bytes 995336 | tf_op jit(solution)/shard_map/ppermute | solution.py:502
  181.9 176.7 %all-gather.8.cloned.1.call-start = ((), (), s32[]{:S(2)}) async-start(), calls=%async_computation.5 | async-start | bytes 7372800 | tf_op jit(solution)/shard_map/all_gather | solution.py:641
  190.0 28.6 %collective-permute-start.16 = (bf16[128,2304]{1,0:T(8,128)(2,1)S(1)}, bf16[128,2304]{1,0:T(8,128)(2,1)S(1)}, u32[]{:S(2)}, u32[]{:S(2)}) collective-permute-start(bf16[128,2304]{1,0:T(8,128)(2,1)S(1)} %fusion.52), channel_id=1, source_target_pairs={{0,2},{2,0},{1,3},{3,1},{4,6},{6,4},{5,7},{7,5},{8,10},{10,8},{9,1... | collective-permute-start | bytes 1769480 | tf_op jit(solution)/shard_map/ppermute | solution.py:502
  191.6 28.4 %collective-permute-start.17 = (bf16[288,576]{1,0:T(8,128)(2,1)}, bf16[288,576]{1,0:T(8,128)(2,1)S(1)}, u32[]{:S(2)}, u32[]{:S(2)}) collective-permute-start(bf16[288,576]{1,0:T(8,128)(2,1)} %bitcast.452), channel_id=1, source_target_pairs={{0,8},{8,16},{16,24},{24,0},{1,9},{9,17},{17,25},{25,1},{2,10},{10... | collective-permute-start | bytes 995336 | tf_op jit(solution)/shard_map/ppermute | solution.py:502
  200.0 24.2 %collective-permute-start.18 = (bf16[288,576]{1,0:T(8,128)(2,1)}, bf16[288,576]{1,0:T(8,128)(2,1)S(1)}, u32[]{:S(2)}, u32[]{:S(2)}) collective-permute-start(bf16[288,576]{1,0:T(8,128)(2,1)} %bitcast.451), channel_id=1, source_target_pairs={{0,16},{8,24},{16,0},{24,8},{1,17},{9,25},{17,1},{25,9},{2,18},{10... | collective-permute-start | bytes 995336 | tf_op jit(solution)/shard_map/ppermute | solution.py:502
  200.0 24.2 %collective-permute-start.19 = (bf16[288,576]{1,0:T(8,128)(2,1)}, bf16[288,576]{1,0:T(8,128)(2,1)S(1)}, u32[]{:S(2)}, u32[]{:S(2)}) collective-permute-start(bf16[288,576]{1,0:T(8,128)(2,1)} %bitcast.450), channel_id=1, source_target_pairs={{0,24},{8,0},{16,8},{24,16},{1,25},{9,1},{17,9},{25,17},{2,26},{10... | collective-permute-start | bytes 995336 | tf_op jit(solution)/shard_map/ppermute | solution.py:502
  228.5 447.9 %reduce-scatter.4.cloned.1.call-start = ((), (), s32[]{:S(2)}) async-start(), calls=%async_computation.6 | async-start | bytes 7372800 | tf_op jit(solution)/shard_map/reduce_scatter | solution.py:677
  232.2 25.0 %collective-permute-start.20 = (bf16[128,2304]{1,0:T(8,128)(2,1)S(1)}, bf16[128,2304]{1,0:T(8,128)(2,1)S(1)}, u32[]{:S(2)}, u32[]{:S(2)}) collective-permute-start(bf16[128,2304]{1,0:T(8,128)(2,1)S(1)} %get-tuple-element.467), channel_id=1, source_target_pairs={{0,8},{8,16},{16,24},{24,0},{1,9},{9,17},{17,25},{25,1},{2,10},{10... | collective-permute-start | bytes 1769480 | tf_op jit(solution)/shard_map/ppermute | solution.py:502
  240.6 40.5 %collective-permute-start.21 = (bf16[128,2304]{1,0:T(8,128)(2,1)S(1)}, bf16[128,2304]{1,0:T(8,128)(2,1)S(1)}, u32[]{:S(2)}, u32[]{:S(2)}) collective-permute-start(bf16[128,2304]{1,0:T(8,128)(2,1)S(1)} %get-tuple-element.467), channel_id=1, source_target_pairs={{0,16},{8,24},{16,0},{24,8},{1,17},{9,25},{17,1},{25,9},{2,18},{10... | collective-permute-start | bytes 1769480 | tf_op jit(solution)/shard_map/ppermute | solution.py:502
  243.5 37.7 %collective-permute-start.22 = (bf16[128,2304]{1,0:T(8,128)(2,1)S(1)}, bf16[128,2304]{1,0:T(8,128)(2,1)S(1)}, u32[]{:S(2)}, u32[]{:S(2)}) collective-permute-start(bf16[128,2304]{1,0:T(8,128)(2,1)S(1)} %get-tuple-element.467), channel_id=1, source_target_pairs={{0,24},{8,0},{16,8},{24,16},{1,25},{9,1},{17,9},{25,17},{2,26},{10... | collective-permute-start | bytes 1769480 | tf_op jit(solution)/shard_map/ppermute | solution.py:502
  281.3 43.7 %collective-permute-start.25 = (bf16[288,1024]{1,0:T(8,128)(2,1)}, bf16[288,1024]{1,0:T(8,128)(2,1)}, u32[]{:S(2)}, u32[]{:S(2)}) collective-permute-start(bf16[288,1024]{1,0:T(8,128)(2,1)} %bitcast.448), channel_id=1, source_target_pairs={{0,8},{8,16},{16,24},{24,0},{1,9},{9,17},{17,25},{25,1},{2,10},{10... | collective-permute-start | bytes 1769480 | tf_op jit(solution)/shard_map/ppermute | solution.py:502
  294.6 39.8 %collective-permute-start.26 = (bf16[288,1024]{1,0:T(8,128)(2,1)S(1)}, bf16[288,1024]{1,0:T(8,128)(2,1)}, u32[]{:S(2)}, u32[]{:S(2)}) collective-permute-start(bf16[288,1024]{1,0:T(8,128)(2,1)S(1)} %bitcast.529), channel_id=1, source_target_pairs={{0,16},{8,24},{16,0},{24,8},{1,17},{9,25},{17,1},{25,9},{2,18},{10... | collective-permute-start | bytes 1769480 | tf_op jit(solution)/shard_map/ppermute | solution.py:502
  295.4 39.1 %collective-permute-start.27 = (bf16[288,1024]{1,0:T(8,128)(2,1)S(1)}, bf16[288,1024]{1,0:T(8,128)(2,1)}, u32[]{:S(2)}, u32[]{:S(2)}) collective-permute-start(bf16[288,1024]{1,0:T(8,128)(2,1)S(1)} %bitcast.528), channel_id=1, source_target_pairs={{0,24},{8,0},{16,8},{24,16},{1,25},{9,1},{17,9},{25,17},{2,26},{10... | collective-permute-start | bytes 1769480 | tf_op jit(solution)/shard_map/ppermute | solution.py:502
  375.9 41.7 %collective-permute-start.30 = (bf16[128,2304]{1,0:T(8,128)(2,1)}, bf16[128,2304]{1,0:T(8,128)(2,1)}, u32[]{:S(2)}, u32[]{:S(2)}) collective-permute-start(bf16[128,2304]{1,0:T(8,128)(2,1)} %get-tuple-element.256), channel_id=1, source_target_pairs={{0,16},{8,24},{16,0},{24,8},{1,17},{9,25},{17,1},{25,9},{2,18},{10... | collective-permute-start | bytes 1769480 | tf_op jit(solution)/shard_map/ppermute | solution.py:502
  378.3 39.3 %collective-permute-start.29 = (bf16[128,2304]{1,0:T(8,128)(2,1)}, bf16[128,2304]{1,0:T(8,128)(2,1)}, u32[]{:S(2)}, u32[]{:S(2)}) collective-permute-start(bf16[128,2304]{1,0:T(8,128)(2,1)} %get-tuple-element.255), channel_id=1, source_target_pairs={{0,24},{8,0},{16,8},{24,16},{1,25},{9,1},{17,9},{25,17},{2,26},{10... | collective-permute-start | bytes 1769480 | tf_op jit(solution)/shard_map/ppermute | solution.py:502
  422.1 28.4 %collective-permute-start.32 = (bf16[128,2304]{1,0:T(8,128)(2,1)S(1)}, bf16[128,2304]{1,0:T(8,128)(2,1)S(1)}, u32[]{:S(2)}, u32[]{:S(2)}) collective-permute-start(bf16[128,2304]{1,0:T(8,128)(2,1)S(1)} %get-tuple-element.463), channel_id=1, source_target_pairs={{0,8},{8,16},{16,24},{24,0},{1,9},{9,17},{17,25},{25,1},{2,10},{10... | collective-permute-start | bytes 1769480 | tf_op jit(solution)/shard_map/ppermute | solution.py:502
  435.3 39.5 %collective-permute-start.33 = (bf16[128,2304]{1,0:T(8,128)(2,1)S(1)}, bf16[128,2304]{1,0:T(8,128)(2,1)S(1)}, u32[]{:S(2)}, u32[]{:S(2)}) collective-permute-start(bf16[128,2304]{1,0:T(8,128)(2,1)S(1)} %get-tuple-element.463), channel_id=1, source_target_pairs={{0,16},{8,24},{16,0},{24,8},{1,17},{9,25},{17,1},{25,9},{2,18},{10... | collective-permute-start | bytes 1769480 | tf_op jit(solution)/shard_map/ppermute | solution.py:502
  436.7 38.0 %collective-permute-start.34 = (bf16[128,2304]{1,0:T(8,128)(2,1)S(1)}, bf16[128,2304]{1,0:T(8,128)(2,1)S(1)}, u32[]{:S(2)}, u32[]{:S(2)}) collective-permute-start(bf16[128,2304]{1,0:T(8,128)(2,1)S(1)} %get-tuple-element.463), channel_id=1, source_target_pairs={{0,24},{8,0},{16,8},{24,16},{1,25},{9,1},{17,9},{25,17},{2,26},{10... | collective-permute-start | bytes 1769480 | tf_op jit(solution)/shard_map/ppermute | solution.py:502
  493.7 235.2 %reduce-scatter.6.cloned.1.call-start = ((), (), s32[]{:S(2)}) async-start(), calls=%async_computation.7 | async-start | bytes 7372800 | tf_op jit(solution)/shard_map/reduce_scatter | solution.py:677
  548.2 225.3 %reduce-scatter.8.cloned.1.call-start = ((), (), s32[]{:S(2)}) async-start(), calls=%async_computation.8 | async-start | bytes 7372800 | tf_op jit(solution)/shard_map/reduce_scatter | solution.py:677
  548.3 28.8 %collective-permute-start.40 = (bf16[128,2304]{1,0:T(8,128)(2,1)}, bf16[128,2304]{1,0:T(8,128)(2,1)S(1)}, u32[]{:S(2)}, u32[]{:S(2)}) collective-permute-start(bf16[128,2304]{1,0:T(8,128)(2,1)} %get-tuple-element.268), channel_id=1, source_target_pairs={{0,8},{8,16},{16,24},{24,0},{1,9},{9,17},{17,25},{25,1},{2,10},{10... | collective-permute-start | bytes 1769480 | tf_op jit(solution)/shard_map/ppermute | solution.py:502
  561.0 41.1 %collective-permute-start.39 = (bf16[128,2304]{1,0:T(8,128)(2,1)}, bf16[128,2304]{1,0:T(8,128)(2,1)S(1)}, u32[]{:S(2)}, u32[]{:S(2)}) collective-permute-start(bf16[128,2304]{1,0:T(8,128)(2,1)} %get-tuple-element.267), channel_id=1, source_target_pairs={{0,16},{8,24},{16,0},{24,8},{1,17},{9,25},{17,1},{25,9},{2,18},{10... | collective-permute-start | bytes 1769480 | tf_op jit(solution)/shard_map/ppermute | solution.py:502
  563.2 38.8 %collective-permute-start.38 = (bf16[128,2304]{1,0:T(8,128)(2,1)}, bf16[128,2304]{1,0:T(8,128)(2,1)S(1)}, u32[]{:S(2)}, u32[]{:S(2)}) collective-permute-start(bf16[128,2304]{1,0:T(8,128)(2,1)} %get-tuple-element.266), channel_id=1, source_target_pairs={{0,24},{8,0},{16,8},{24,16},{1,25},{9,1},{17,9},{25,17},{2,26},{10... | collective-permute-start | bytes 1769480 | tf_op jit(solution)/shard_map/ppermute | solution.py:502
  606.2 21.9 %collective-permute-start.41 = (bf16[128,2304]{1,0:T(8,128)(2,1)S(1)}, bf16[128,2304]{1,0:T(8,128)(2,1)S(1)}, u32[]{:S(2)}, u32[]{:S(2)}) collective-permute-start(bf16[128,2304]{1,0:T(8,128)(2,1)S(1)} %subtract_convert_fusion), channel_id=1, source_target_pairs={{0,2},{2,0},{1,3},{3,1},{4,6},{6,4},{5,7},{7,5},{8,10},{10,8},{9,1... | collective-permute-start | bytes 1769480 | tf_op jit(solution)/shard_map/ppermute | solution.py:502
  629.3 24.3 %collective-permute-start.42 = (bf16[256,2304]{1,0:T(8,128)(2,1)}, bf16[256,2304]{1,0:T(8,128)(2,1)}, u32[]{:S(2)}, u32[]{:S(2)}) collective-permute-start(bf16[256,2304]{1,0:T(8,128)(2,1)} %pad_maximum_fusion.5), channel_id=1, source_target_pairs={{0,1},{1,0},{2,3},{3,2},{4,5},{5,4},{6,7},{7,6},{8,9},{9,8},{10,11... | collective-permute-start | bytes 3538952 | tf_op jit(solution)/shard_map/ppermute | solution.py:502
  678.8 50.1 %collective-permute-start.43 = (bf16[1152,512]{1,0:T(8,128)(2,1)}, bf16[1152,512]{1,0:T(8,128)(2,1)}, u32[]{:S(2)}, u32[]{:S(2)}) collective-permute-start(bf16[1152,512]{1,0:T(8,128)(2,1)} %dynamic-slice_bitcast_fusion.1), channel_id=1, source_target_pairs={{0,4},{4,0},{1,5},{5,1},{2,6},{6,2},{3,7},{7,3},{8,12},{12,8},{9,1... | collective-permute-start | bytes 3538952 | tf_op jit(solution)/shard_map/ppermute | solution.py:502
  687.9 22.8 %collective-permute-start.44 = (bf16[288,576]{1,0:T(8,128)(2,1)S(1)}, bf16[288,576]{1,0:T(8,128)(2,1)S(1)}, u32[]{:S(2)}, u32[]{:S(2)}) collective-permute-start(bf16[288,576]{1,0:T(8,128)(2,1)S(1)} %copy-done.102), channel_id=1, source_target_pairs={{0,8},{8,16},{16,24},{24,0},{1,9},{9,17},{17,25},{25,1},{2,10},{10... | collective-permute-start | bytes 995336 | tf_op jit(solution)/shard_map/ppermute | solution.py:502
  701.7 22.6 %collective-permute-start.45 = (bf16[288,576]{1,0:T(8,128)(2,1)S(1)}, bf16[288,576]{1,0:T(8,128)(2,1)S(1)}, u32[]{:S(2)}, u32[]{:S(2)}) collective-permute-start(bf16[288,576]{1,0:T(8,128)(2,1)S(1)} %copy-done.101), channel_id=1, source_target_pairs={{0,16},{8,24},{16,0},{24,8},{1,17},{9,25},{17,1},{25,9},{2,18},{10... | collective-permute-start | bytes 995336 | tf_op jit(solution)/shard_map/ppermute | solution.py:502
  701.7 24.2 %collective-permute-start.46 = (bf16[288,576]{1,0:T(8,128)(2,1)S(1)}, bf16[288,576]{1,0:T(8,128)(2,1)S(1)}, u32[]{:S(2)}, u32[]{:S(2)}) collective-permute-start(bf16[288,576]{1,0:T(8,128)(2,1)S(1)} %copy-done.100), channel_id=1, source_target_pairs={{0,24},{8,0},{16,8},{24,16},{1,25},{9,1},{17,9},{25,17},{2,26},{10... | collective-permute-start | bytes 995336 | tf_op jit(solution)/shard_map/ppermute | solution.py:502
  737.2 61.7 %collective-permute-start.47 = (bf16[1152,1024]{1,0:T(8,128)(2,1)}, bf16[1152,1024]{1,0:T(8,128)(2,1)}, u32[]{:S(2)}, u32[]{:S(2)}) collective-permute-start(bf16[1152,1024]{1,0:T(8,128)(2,1)} %dynamic-slice_bitcast_fusion), channel_id=1, source_target_pairs={{0,4},{4,0},{1,5},{5,1},{2,6},{6,2},{3,7},{7,3},{8,12},{12,8},{9,1... | collective-permute-start | bytes 7077896 | tf_op jit(solution)/shard_map/ppermute | solution.py:502
  737.2 22.5 %collective-permute-start.48 = (bf16[288,512]{1,0:T(8,128)(2,1)}, bf16[288,512]{1,0:T(8,128)(2,1)}, u32[]{:S(2)}, u32[]{:S(2)}) collective-permute-start(bf16[288,512]{1,0:T(8,128)(2,1)} %get-tuple-element.280), channel_id=1, source_target_pairs={{0,8},{8,16},{16,24},{24,0},{1,9},{9,17},{17,25},{25,1},{2,10},{10... | collective-permute-start | bytes 884744 | tf_op jit(solution)/shard_map/ppermute | solution.py:502
  743.8 23.8 %collective-permute-start.49 = (bf16[288,512]{1,0:T(8,128)(2,1)}, bf16[288,512]{1,0:T(8,128)(2,1)}, u32[]{:S(2)}, u32[]{:S(2)}) collective-permute-start(bf16[288,512]{1,0:T(8,128)(2,1)} %get-tuple-element.281), channel_id=1, source_target_pairs={{0,16},{8,24},{16,0},{24,8},{1,17},{9,25},{17,1},{25,9},{2,18},{10... | collective-permute-start | bytes 884744 | tf_op jit(solution)/shard_map/ppermute | solution.py:502
  747.2 26.3 %collective-permute-start.51 = (bf16[2,128,2304]{2,1,0:T(8,128)(2,1)}, bf16[2,128,2304]{2,1,0:T(8,128)(2,1)}, u32[]{:S(2)}, u32[]{:S(2)}) collective-permute-start(bf16[2,128,2304]{2,1,0:T(8,128)(2,1)} %fusion.22), channel_id=1, source_target_pairs={{0,1},{1,0},{2,3},{3,2},{4,5},{5,4},{6,7},{7,6},{8,9},{9,8},{10,11... | collective-permute-start | bytes 3538952 | tf_op jit(solution)/shard_map/ppermute | solution.py:502
  759.6 51.2 %collective-permute-start.57 = (bf16[288,512]{1,0:T(8,128)(2,1)}, bf16[288,512]{1,0:T(8,128)(2,1)}, u32[]{:S(2)}, u32[]{:S(2)}) collective-permute-start(bf16[288,512]{1,0:T(8,128)(2,1)} %bitcast.464), channel_id=1, source_target_pairs={{0,8},{8,16},{16,24},{24,0},{1,9},{9,17},{17,25},{25,1},{2,10},{10... | collective-permute-start | bytes 884744 | tf_op jit(solution)/shard_map/ppermute | solution.py:502
  767.5 44.7 %collective-permute-start.58 = (bf16[288,512]{1,0:T(8,128)(2,1)}, bf16[288,512]{1,0:T(8,128)(2,1)}, u32[]{:S(2)}, u32[]{:S(2)}) collective-permute-start(bf16[288,512]{1,0:T(8,128)(2,1)} %bitcast.463), channel_id=1, source_target_pairs={{0,16},{8,24},{16,0},{24,8},{1,17},{9,25},{17,1},{25,9},{2,18},{10... | collective-permute-start | bytes 884744 | tf_op jit(solution)/shard_map/ppermute | solution.py:502
  767.6 48.1 %collective-permute-start.59 = (bf16[288,512]{1,0:T(8,128)(2,1)}, bf16[288,512]{1,0:T(8,128)(2,1)}, u32[]{:S(2)}, u32[]{:S(2)}) collective-permute-start(bf16[288,512]{1,0:T(8,128)(2,1)} %bitcast.462), channel_id=1, source_target_pairs={{0,24},{8,0},{16,8},{24,16},{1,25},{9,1},{17,9},{25,17},{2,26},{10... | collective-permute-start | bytes 884744 | tf_op jit(solution)/shard_map/ppermute | solution.py:502
  802.5 22.9 %collective-permute-start.52 = (bf16[288,1024]{1,0:T(8,128)(2,1)S(1)}, bf16[288,1024]{1,0:T(8,128)(2,1)S(1)}, u32[]{:S(2)}, u32[]{:S(2)}) collective-permute-start(bf16[288,1024]{1,0:T(8,128)(2,1)S(1)} %get-tuple-element.481), channel_id=1, source_target_pairs={{0,8},{8,16},{16,24},{24,0},{1,9},{9,17},{17,25},{25,1},{2,10},{10... | collective-permute-start | bytes 1769480 | tf_op jit(solution)/shard_map/ppermute | solution.py:502
  804.1 40.7 %collective-permute-start.53 = (bf16[288,1024]{1,0:T(8,128)(2,1)S(1)}, bf16[288,1024]{1,0:T(8,128)(2,1)S(1)}, u32[]{:S(2)}, u32[]{:S(2)}) collective-permute-start(bf16[288,1024]{1,0:T(8,128)(2,1)S(1)} %get-tuple-element.480), channel_id=1, source_target_pairs={{0,16},{8,24},{16,0},{24,8},{1,17},{9,25},{17,1},{25,9},{2,18},{10... | collective-permute-start | bytes 1769480 | tf_op jit(solution)/shard_map/ppermute | solution.py:502
  810.9 34.0 %collective-permute-start.54 = (bf16[288,1024]{1,0:T(8,128)(2,1)S(1)}, bf16[288,1024]{1,0:T(8,128)(2,1)S(1)}, u32[]{:S(2)}, u32[]{:S(2)}) collective-permute-start(bf16[288,1024]{1,0:T(8,128)(2,1)S(1)} %get-tuple-element.479), channel_id=1, source_target_pairs={{0,24},{8,0},{16,8},{24,16},{1,25},{9,1},{17,9},{25,17},{2,26},{10... | collective-permute-start | bytes 1769480 | tf_op jit(solution)/shard_map/ppermute | solution.py:502
  812.3 32.5 %collective-permute-start.56 = (bf16[128,2304]{1,0:T(8,128)(2,1)S(1)}, bf16[128,2304]{1,0:T(8,128)(2,1)S(1)}, u32[]{:S(2)}, u32[]{:S(2)}) collective-permute-start(bf16[128,2304]{1,0:T(8,128)(2,1)S(1)} %fusion.53), channel_id=1, source_target_pairs={{0,2},{2,0},{1,3},{3,1},{4,6},{6,4},{5,7},{7,5},{8,10},{10,8},{9,1... | collective-permute-start | bytes 1769480 | tf_op jit(solution)/shard_map/ppermute | solution.py:502
  845.4 26.1 %collective-permute-start.60 = (f32[4,2304]{1,0:T(4,128)S(1)}, f32[4,2304]{1,0:T(4,128)S(1)}, u32[]{:S(2)}, u32[]{:S(2)}) collective-permute-start(f32[4,2304]{1,0:T(4,128)S(1)} %pad_maximum_fusion.23), channel_id=1, source_target_pairs={{0,1},{1,0},{2,3},{3,2},{4,5},{5,4},{6,7},{7,6},{8,9},{9,8},{10,11... | collective-permute-start | bytes 110600 | tf_op jit(solution)/shard_map/ppermute | solution.py:502
  845.5 57.7 %collective-permute-start.66 = (bf16[576,576]{1,0:T(8,128)(2,1)}, bf16[576,576]{1,0:T(8,128)(2,1)}, u32[]{:S(2)}, u32[]{:S(2)}) collective-permute-start(bf16[576,576]{1,0:T(8,128)(2,1)} %pad_maximum_fusion.11), channel_id=1, source_target_pairs={{0,8},{8,16},{16,24},{24,0},{1,9},{9,17},{17,25},{25,1},{2,10},{10... | collective-permute-start | bytes 1990664 | tf_op jit(solution)/shard_map/ppermute | solution.py:502
  858.6 50.1 %collective-permute-start.67 = (bf16[576,576]{1,0:T(8,128)(2,1)}, bf16[576,576]{1,0:T(8,128)(2,1)}, u32[]{:S(2)}, u32[]{:S(2)}) collective-permute-start(bf16[576,576]{1,0:T(8,128)(2,1)} %pad_maximum_fusion.12), channel_id=1, source_target_pairs={{0,16},{8,24},{16,0},{24,8},{1,17},{9,25},{17,1},{25,9},{2,18},{10... | collective-permute-start | bytes 1990664 | tf_op jit(solution)/shard_map/ppermute | solution.py:502
  860.2 48.6 %collective-permute-start.68 = (bf16[576,576]{1,0:T(8,128)(2,1)}, bf16[576,576]{1,0:T(8,128)(2,1)}, u32[]{:S(2)}, u32[]{:S(2)}) collective-permute-start(bf16[576,576]{1,0:T(8,128)(2,1)} %pad_maximum_fusion.13), channel_id=1, source_target_pairs={{0,24},{8,0},{16,8},{24,16},{1,25},{9,1},{17,9},{25,17},{2,26},{10... | collective-permute-start | bytes 1990664 | tf_op jit(solution)/shard_map/ppermute | solution.py:502
  867.6 41.1 %collective-permute-start.69 = (f32[4,3,128,128]{3,2,1,0:T(8,128)}, f32[4,3,128,128]{3,2,1,0:T(8,128)}, u32[]{:S(2)}, u32[]{:S(2)}) collective-permute-start(f32[4,3,128,128]{3,2,1,0:T(8,128)} %dynamic-slice_bitcast_fusion.3), channel_id=1, source_target_pairs={{0,4},{4,0},{1,5},{5,1},{2,6},{6,2},{3,7},{7,3},{8,12},{12,8},{9,1... | collective-permute-start | bytes 2359304 | tf_op jit(solution)/shard_map/ppermute | solution.py:502
  901.4 124.3 %collective-permute-start.65 = (f32[4,2304]{1,0:T(4,128)}, f32[4,2304]{1,0:T(4,128)}, u32[]{:S(2)}, u32[]{:S(2)}) collective-permute-start(f32[4,2304]{1,0:T(4,128)} %add.526), channel_id=1, source_target_pairs={{0,24},{8,0},{16,8},{24,16},{1,25},{9,1},{17,9},{25,17},{2,26},{10... | collective-permute-start | bytes 110600 | tf_op jit(solution)/shard_map/ppermute | solution.py:502
  936.9 33.2 %collective-permute-start.74 = (f32[4,3,128,128]{3,2,1,0:T(8,128)S(1)}, f32[4,3,128,128]{3,2,1,0:T(8,128)S(1)}, u32[]{:S(2)}, u32[]{:S(2)}) collective-permute-start(f32[4,3,128,128]{3,2,1,0:T(8,128)S(1)} %dynamic-slice_bitcast_fusion.2), channel_id=1, source_target_pairs={{0,4},{4,0},{1,5},{5,1},{2,6},{6,2},{3,7},{7,3},{8,12},{12,8},{9,1... | collective-permute-start | bytes 2359304 | tf_op jit(solution)/shard_map/ppermute | solution.py:502
  938.7 26.0 %collective-permute-start.71 = (f32[1,3,128,128]{3,2,1,0:T(8,128)S(1)}, f32[1,3,128,128]{3,2,1,0:T(8,128)S(1)}, u32[]{:S(2)}, u32[]{:S(2)}) collective-permute-start(f32[1,3,128,128]{3,2,1,0:T(8,128)S(1)} %get-tuple-element.553), channel_id=1, source_target_pairs={{0,8},{8,16},{16,24},{24,0},{1,9},{9,17},{17,25},{25,1},{2,10},{10... | collective-permute-start | bytes 589832 | tf_op jit(solution)/shard_map/ppermute | solution.py:502
  964.8 61.0 %collective-permute-start.63 = (f32[4,2304]{1,0:T(4,128)}, f32[4,2304]{1,0:T(4,128)S(1)}, u32[]{:S(2)}, u32[]{:S(2)}) collective-permute-start(f32[4,2304]{1,0:T(4,128)} %add.526), channel_id=1, source_target_pairs={{0,8},{8,16},{16,24},{24,0},{1,9},{9,17},{17,25},{25,1},{2,10},{10... | collective-permute-start | bytes 110600 | tf_op jit(solution)/shard_map/ppermute | solution.py:502
  982.1 43.7 %collective-permute-start.64 = (f32[4,2304]{1,0:T(4,128)}, f32[4,2304]{1,0:T(4,128)S(1)}, u32[]{:S(2)}, u32[]{:S(2)}) collective-permute-start(f32[4,2304]{1,0:T(4,128)} %add.526), channel_id=1, source_target_pairs={{0,16},{8,24},{16,0},{24,8},{1,17},{9,25},{17,1},{25,9},{2,18},{10... | collective-permute-start | bytes 110600 | tf_op jit(solution)/shard_map/ppermute | solution.py:502
  993.9 28.2 %collective-permute-start.79 = (bf16[4,3,128,128]{3,2,1,0:T(8,128)(2,1)S(1)}, bf16[4,3,128,128]{3,2,1,0:T(8,128)(2,1)S(1)}, u32[]{:S(2)}, u32[]{:S(2)}) collective-permute-start(bf16[4,3,128,128]{3,2,1,0:T(8,128)(2,1)S(1)} %pad_maximum_fusion.22), channel_id=1, source_target_pairs={{0,16},{8,24},{16,0},{24,8},{1,17},{9,25},{17,1},{25,9},{2,18},{10... | collective-permute-start | bytes 1179656 | tf_op jit(solution)/shard_map/ppermute | solution.py:502
  1024.2 36.0 %collective-permute-start.81 = (bf16[4,4,3,128,128]{4,3,2,0,1:T(8,128)(2,1)}, bf16[4,4,3,128,128]{4,3,2,0,1:T(8,128)(2,1)}, u32[]{:S(2)}, u32[]{:S(2)}) collective-permute-start(bf16[4,4,3,128,128]{4,3,2,0,1:T(8,128)(2,1)} %bitcast_dynamic-update-slice_fusion.15), channel_id=1, source_target_pairs={{0,4},{4,0},{1,5},{5,1},{2,6},{6,2},{3,7},{7,3},{8,12},{12,8},{9,1... | collective-permute-start | bytes 4718600 | tf_op jit(solution)/shard_map/ppermute | solution.py:502
  (186 other events, 2918.6 us)
Sparse Core Ops, SparseCore 0:
  142.7 78.6 all-gather.3
  223.8 65.3 all-gather.5
  291.7 66.8 all-gather.7
  493.8 77.8 reduce-scatter.3
  574.6 70.2 reduce-scatter.5
  651.8 106.0 reduce-scatter.7

commit v2 on v1

--- a/solution.py
+++ b/solution.py
@@ -102,16 +102,9 @@
     )
 
 
-def attention_scores(query_rows_rotated, key_vectors, allowed):
-    raw_scores = jnp.einsum(
-        "tkgd,skd->kgts", query_rows_rotated, key_vectors, preferred_element_type=jnp.float32
-    )
-    tanh_part = jnp.tanh(raw_scores / softcap)
-    masked = jnp.where(allowed[None, None], softcap * tanh_part, masked_value)
-    return (tanh_part, masked)
-
-
 HALF = HEAD_SIZE // 2
+
+BRIEF = pl.CostEstimate(flops=1024, bytes_accessed=1024, transcendentals=0)
 
 
 def two_terms(values):
@@ -175,13 +168,140 @@
         ],
         out_specs=pl.BlockSpec((1, 3, HALF, HALF), lambda step: (step, 0, 0, 0)),
         out_shape=jax.ShapeDtypeStruct((slots, 3, HALF, HALF), jnp.float32),
-        cost_estimate=pl.CostEstimate(
-            flops=4 * sum(counts) * rows * HEAD_SIZE**2,
-            bytes_accessed=sum(counts) * 4 * HEAD_SIZE * (rows + HEAD_SIZE),
-            transcendentals=0,
-        ),
+        cost_estimate=BRIEF,
         compiler_params=pltpu.CompilerParams(vmem_limit_bytes=40 * 1024 * 1024),
     )(*states)
+
+
+def add_gram(out_ref, index, values):
+    high, low = two_terms(values)
+    mixed = contract_first(high, low)
+    gram = contract_first(high, high) + (mixed + mixed.T)
+    out_ref[index, 0] += gram[:HALF, :HALF]
+    out_ref[index, 1] += gram[:HALF, HALF:]
+    out_ref[index, 2] += gram[HALF:, HALF:]
+
+
+def inner_body(total_ref, moment_ref, out_ref):
+    out_ref[...] = jnp.zeros(out_ref.shape, out_ref.dtype)
+    gradient = total_ref[...].astype(jnp.float32)
+    add_gram(out_ref, 0, momentum_decay * moment_ref[...].astype(jnp.float32) + gradient)
+
+
+def inner_grams(total, moment, blocks, first):
+    rows = total.shape[0]
+    return pl.pallas_call(
+        inner_body,
+        grid=(blocks,),
+        in_specs=[
+            pl.BlockSpec((rows, HEAD_SIZE), lambda step: (0, step)),
+            pl.BlockSpec((rows, HEAD_SIZE), lambda step: (0, step + first)),
+        ],
+        out_specs=pl.BlockSpec((1, 3, HALF, HALF), lambda step: (step, 0, 0, 0)),
+        out_shape=jax.ShapeDtypeStruct((blocks, 3, HALF, HALF), jnp.float32),
+        cost_estimate=BRIEF,
+        compiler_params=pltpu.CompilerParams(vmem_limit_bytes=40 * 1024 * 1024),
+    )(total, moment)
+
+
+ROW_TILE = 96
+
+
+def finish_body(main, place_ref, *refs):
+    depth = len(refs) - 4
+    moment_ref, grad_ref, state_ref, gram_ref = refs[depth:]
+    rest = refs[0].shape[1] - main
+    for j in range(depth):
+        turn = lax.rem(place_ref[0] + depth - j, depth)
+        for k in range(depth):
+
+            @pl.when(turn == k)
+            def _(piece=refs[k], j=j):
+                grad_ref[:, main * j : main * (j + 1)] = piece[:, :main].astype(jnp.float32)
+                start = main * depth + rest * j
+                grad_ref[:, start : start + rest] = piece[:, main:].astype(jnp.float32)
+
+    state_ref[...] = momentum_decay * moment_ref[...] + grad_ref[...]
+
+    @pl.when(pl.program_id(0) == 0)
+    def _():
+        gram_ref[...] = jnp.zeros(gram_ref.shape, gram_ref.dtype)
+
+    add_gram(gram_ref, 0, state_ref[:, main * depth :])
+
+
+def finish(pieces, position, moment, main):
+    rows, cols = moment.shape
+    wide_spec = pl.BlockSpec((ROW_TILE, cols), lambda step, place: (step, 0))
+    piece_spec = pl.BlockSpec((ROW_TILE, pieces[0].shape[1]), lambda step, place: (step, 0))
+    return pl.pallas_call(
+        partial(finish_body, main),
+        grid_spec=pltpu.PrefetchScalarGridSpec(
+            num_scalar_prefetch=1,
+            grid=(rows // ROW_TILE,),
+            in_specs=[piece_spec] * len(pieces) + [wide_spec],
+            out_specs=[
+                wide_spec,
+                wide_spec,
+                pl.BlockSpec((1, 3, HALF, HALF), lambda step, place: (0, 0, 0, 0)),
+            ],
+        ),
+        out_shape=[
+            jax.ShapeDtypeStruct((rows, cols), jnp.float32),
+            jax.ShapeDtypeStruct((rows, cols), jnp.float32),
+            jax.ShapeDtypeStruct((1, 3, HALF, HALF), jnp.float32),
+        ],
+        cost_estimate=BRIEF,
+        compiler_params=pltpu.CompilerParams(vmem_limit_bytes=40 * 1024 * 1024),
+    )(position.reshape(1), *pieces, moment)
+
+
+def attn_finish_body(depth, *refs):
+    sums = refs[: 2 * depth]
+    moments, grads, states = (refs[2 * depth + 4 * i : 2 * depth + 4 * i + 4] for i in range(3))
+    gram_ref = refs[-1]
+
+    @pl.when(pl.program_id(0) == 0)
+    def _():
+        gram_ref[...] = jnp.zeros(gram_ref.shape, gram_ref.dtype)
+
+    mixed = sum(ref[...].astype(jnp.float32) for ref in sums[:depth])
+    out = sum(ref[...].astype(jnp.float32) for ref in sums[depth:])
+    slot = 0
+    start = 0
+    for moment_ref, grad_ref, state_ref in zip(moments, grads, states):
+        cols = moment_ref.shape[1]
+        if grad_ref is grads[-1]:
+            gradient = out
+        else:
+            gradient = mixed[:, start : start + cols]
+        start += cols
+        grad_ref[...] = gradient
+        state = momentum_decay * moment_ref[...] + gradient
+        state_ref[...] = state
+        for block in range(cols // HEAD_SIZE):
+            add_gram(gram_ref, slot, state[:, block * HEAD_SIZE : (block + 1) * HEAD_SIZE])
+            slot += 1
+
+
+def attn_finish(mixed, out, moments, slots):
+    rows = moments[0].shape[0]
+
+    def spec(v):
+        return pl.BlockSpec((ROW_TILE, v.shape[1]), lambda step: (step, 0))
+
+    outs = [jax.ShapeDtypeStruct(m.shape, jnp.float32) for m in moments]
+    results = pl.pallas_call(
+        partial(attn_finish_body, len(mixed)),
+        grid=(rows // ROW_TILE,),
+        in_specs=[spec(v) for v in (*mixed, *out, *moments)],
+        out_specs=[spec(v) for v in outs + outs]
+        + [pl.BlockSpec((slots, 3, HALF, HALF), lambda step: (0, 0, 0, 0))],
+        out_shape=outs + outs + [jax.ShapeDtypeStruct((slots, 3, HALF, HALF), jnp.float32)],
+        cost_estimate=BRIEF,
+        compiler_params=pltpu.CompilerParams(vmem_limit_bytes=40 * 1024 * 1024),
+    )(*mixed, *out, *moments)
+    return list(results[:4]), list(results[4:8]), results[8]
 
 
 def newton_body(count, *refs):
@@ -234,14 +354,13 @@
     return pl.pallas_call(
         partial(newton_body, count),
         out_shape=jax.ShapeDtypeStruct((count, 3, HALF, HALF), jnp.bfloat16),
-        cost_estimate=pl.CostEstimate(
-            flops=count * 17 * 6 * HEAD_SIZE**3, bytes_accessed=count * 2**20, transcendentals=0
-        ),
+        cost_estimate=BRIEF,
         compiler_params=pltpu.CompilerParams(vmem_limit_bytes=40 * 1024 * 1024),
     )(*pieces)
 
 
-def apply_body(state_ref, factor_ref, out_ref):
+def apply_body(state_ref, factor_ref, *refs):
+    out_ref = refs[-1]
     upper = factor_ref[0, 1].astype(jnp.float32)
     factor = jnp.concatenate(
         [
@@ -254,39 +373,34 @@
     out_ref[...] = product(high, factor) + product(low, factor)
 
 
-def apply_factor(state, factors, start):
+def apply_factor(state, factors, start, low=0, high=None, into=None):
     rows, cols = state.shape
+    high = cols // HEAD_SIZE if high is None else high
+    block = pl.BlockSpec((rows, HEAD_SIZE), lambda step: (0, step + low))
     return pl.pallas_call(
         apply_body,
-        grid=(cols // HEAD_SIZE,),
-        in_specs=[
-            pl.BlockSpec((rows, HEAD_SIZE), lambda step: (0, step)),
-            pl.BlockSpec((1, 3, HALF, HALF), lambda step: (step + start, 0, 0, 0)),
-        ],
-        out_specs=pl.BlockSpec((rows, HEAD_SIZE), lambda step: (0, step)),
+        grid=(high - low,),
+        in_specs=[block, pl.BlockSpec((1, 3, HALF, HALF), lambda step: (step + start, 0, 0, 0))]
+        + ([] if into is None else [pl.BlockSpec(memory_space=pl.ANY)]),
+        out_specs=block,
         out_shape=jax.ShapeDtypeStruct((rows, cols), jnp.float32),
-        cost_estimate=pl.CostEstimate(
-            flops=4 * rows * cols * HEAD_SIZE, bytes_accessed=8 * rows * cols, transcendentals=0
-        ),
+        input_output_aliases={} if into is None else {2: 0},
+        cost_estimate=BRIEF,
         compiler_params=pltpu.CompilerParams(vmem_limit_bytes=40 * 1024 * 1024),
-    )(state, factors)
+    )(state, factors, *([] if into is None else [into]))
 
 
 VMEM_BYTES = 50 * 1024 * 1024
 
 
-def dense_call(body, grid, in_specs, out_specs, out_shape, flops, *operands):
-    outs = out_shape if isinstance(out_shape, (list, tuple)) else [out_shape]
-    moved = sum(v.size * v.dtype.itemsize for v in operands) + sum(
-        v.size * v.dtype.itemsize for v in outs
-    )
+def dense_call(body, grid, in_specs, out_specs, out_shape, *operands):
     return pl.pallas_call(
         body,
         grid=grid,
         in_specs=in_specs,
         out_specs=out_specs,
         out_shape=out_shape,
-        cost_estimate=pl.CostEstimate(flops=flops, bytes_accessed=moved, transcendentals=0),
+        cost_estimate=BRIEF,
         compiler_params=pltpu.CompilerParams(vmem_limit_bytes=VMEM_BYTES),
     )(*operands)
 
@@ -297,32 +411,32 @@
 
 def enter_body(rows_ref, gate_ref, up_ref, hidden_ref, gelu_ref, pull_ref):
     rows = rows_ref[...]
-    gate = product(rows, gate_ref[...])
-    up = product(rows, up_ref[...])
     factor = (2.0 / jnp.pi) ** 0.5
-    squared = gate * gate
-    bend = jnp.tanh(factor * (gate + 0.044715 * gate * squared))
-    upper = 0.5 * (1.0 + bend)
-    gelu = gate * upper
-    slope = upper + 0.5 * gate * (1.0 - bend * bend) * (factor * (1.0 + 0.134145 * squared))
-    hidden_ref[...] = (gelu * up).astype(jnp.bfloat16)
-    gelu_ref[...] = gelu.astype(jnp.bfloat16)
-    pull_ref[...] = (up * slope).astype(jnp.bfloat16)
+    for p in range(gate_ref.shape[0]):
+        gate = product(rows, gate_ref[p])
+        up = product(rows, up_ref[p])
+        squared = gate * gate
+        bend = jnp.tanh(factor * (gate + 0.044715 * gate * squared))
+        upper = 0.5 * (1.0 + bend)
+        gelu = gate * upper
+        slope = upper + 0.5 * gate * (1.0 - bend * bend) * (factor * (1.0 + 0.134145 * squared))
+        hidden_ref[p] = (gelu * up).astype(jnp.bfloat16)
+        gelu_ref[p] = gelu.astype(jnp.bfloat16)
+        pull_ref[p] = (up * slope).astype(jnp.bfloat16)
 
 
 def enter(rows, gate, up):
     count, width = rows.shape
     pieces, _, cols = gate.shape
     tile = column_tile(cols)
-    weight = pl.BlockSpec((None, width, tile), lambda p, j, i: (p, 0, j))
-    out = pl.BlockSpec((None, 256, tile), lambda p, j, i: (p, i, j))
+    weight = pl.BlockSpec((pieces, width, tile), lambda j, i: (0, 0, j))
+    out = pl.BlockSpec((pieces, 256, tile), lambda j, i: (0, i, j))
     return dense_call(
         enter_body,
-        (pieces, cols // tile, count // 256),
-        [pl.BlockSpec((256, width), lambda p, j, i: (i, 0)), weight, weight],
+        (cols // tile, count // 256),
+        [pl.BlockSpec((256, width), lambda j, i: (i, 0)), weight, weight],
         [out] * 3,
         [jax.ShapeDtypeStruct((pieces, count, cols), jnp.bfloat16)] * 3,
-        4 * count * width * cols * pieces,
         rows,
         gate,
         up,
@@ -330,28 +444,29 @@
 
 
 def leave_body(rows_ref, down_ref, gelu_ref, pull_ref, gate_ref, up_ref):
-    delta = product(rows_ref[...], down_ref[...])
-    gate_ref[...] = (delta * pull_ref[...].astype(jnp.float32)).astype(jnp.bfloat16)
-    up_ref[...] = (delta * gelu_ref[...].astype(jnp.float32)).astype(jnp.bfloat16)
+    rows = rows_ref[...]
+    for p in range(down_ref.shape[0]):
+        delta = product(rows, down_ref[p])
+        gate_ref[p] = (delta * pull_ref[p].astype(jnp.float32)).astype(jnp.bfloat16)
+        up_ref[p] = (delta * gelu_ref[p].astype(jnp.float32)).astype(jnp.bfloat16)
 
 
 def leave(rows, down, gelu, pull):
     count, width = rows.shape
     pieces, _, cols = down.shape
     tile = column_tile(cols)
-    out = pl.BlockSpec((None, 256, tile), lambda p, j, i: (p, i, j))
+    out = pl.BlockSpec((pieces, 256, tile), lambda j, i: (0, i, j))
     return dense_call(
         leave_body,
-        (pieces, cols // tile, count // 256),
+        (cols // tile, count // 256),
         [
-            pl.BlockSpec((256, width), lambda p, j, i: (i, 0)),
-            pl.BlockSpec((None, width, tile), lambda p, j, i: (p, 0, j)),
+            pl.BlockSpec((256, width), lambda j, i: (i, 0)),
+            pl.BlockSpec((pieces, width, tile), lambda j, i: (0, 0, j)),
             out,
             out,
         ],
         [out] * 2,
         [jax.ShapeDtypeStruct((pieces, count, cols), jnp.bfloat16)] * 2,
-        2 * count * width * cols * pieces,
         rows,
         down,
         gelu,
@@ -380,7 +495,6 @@
         + [pl.BlockSpec((pieces, tile, cols), lambda j: (0, j, 0))] * count,
         pl.BlockSpec((rows, tile), lambda j: (0, j)),
         jax.ShapeDtypeStruct((rows, width), dtype),
-        2 * rows * width * cols * pieces * count,
         *lefts,
         *rights,
     )
@@ -405,10 +519,93 @@
         ],
         pl.BlockSpec((pieces, tile, cols), lambda j: (0, j, 0)),
         jax.ShapeDtypeStruct((pieces, width, cols), jnp.bfloat16),
-        2 * pieces * rows * width * cols,
         left,
         right,
     )
+
+
+def rotated(values, cosines, sines):
+    first, second = values[:, :HALF], values[:, HALF:]
+    return jnp.concatenate(
+        [first * cosines - second * sines, second * cosines + first * sines], axis=1
+    )
+
+
+def head(index):
+    return slice(index * HEAD_SIZE, (index + 1) * HEAD_SIZE)
+
+
+def pair_mask(segment_rows, segment_cols, alive_rows, alive_cols):
+    shape = (segment_rows.shape[0], segment_cols.shape[1])
+    distance = lax.broadcasted_iota(jnp.int32, shape, 0) - lax.broadcasted_iota(
+        jnp.int32, shape, 1
+    )
+    inside = (
+        (alive_rows * alive_cols > 0)
+        & (segment_rows == segment_cols)
+        & (distance >= 0)
+        & (distance < WINDOW)
+    )
+    return (distance == 0) | inside
+
+
+def attend_body(kv_heads, width, *refs):
+    projected, cosines, sines = (ref[...] for ref in refs[:3])
+    query_ref, key_ref, value_ref, prob_ref, tanh_ref, mixed_ref = refs[7:]
+    allowed = pair_mask(*(ref[...] for ref in refs[3:7]))
+    query_heads = kv_heads * width
+    for j in range(kv_heads):
+        key = rotated(projected[:, head(query_heads + j)], cosines, sines).astype(jnp.bfloat16)
+        value = projected[:, head(query_heads + kv_heads + j)].astype(jnp.bfloat16)
+        key_ref[:, head(j)] = key
+        value_ref[:, head(j)] = value
+        for i in range(j * width, (j + 1) * width):
+            query = rotated(projected[:, head(i)], cosines, sines) * HEAD_SIZE ** (-0.5)
+            query = query.astype(jnp.bfloat16)
+            query_ref[:, head(i)] = query
+            tanh_part = jnp.tanh(contract_last(query, key) / softcap)
+            masked = jnp.where(allowed, softcap * tanh_part, masked_value)
+            exponent = jnp.exp(masked - jnp.max(masked, axis=-1, keepdims=True))
+            prob = exponent / jnp.sum(exponent, axis=-1, keepdims=True)
+            prob_ref[i] = prob
+            tanh_ref[i] = tanh_part
+            mixed_ref[:, head(i)] = product(prob.astype(jnp.bfloat16), value).astype(jnp.bfloat16)
+
+
+def attend_back_body(kv_heads, width, *refs):
+    delta_mixed, cosines, sines = (ref[...] for ref in refs[:3])
+    query_ref, key_ref, value_ref, prob_ref, tanh_ref, out_ref = refs[7:]
+    allowed = pair_mask(*(ref[...] for ref in refs[3:7]))
+    query_heads = kv_heads * width
+    for j in range(kv_heads):
+        key, value = key_ref[:, head(j)], value_ref[:, head(j)]
+        delta_key = delta_value = None
+        for i in range(j * width, (j + 1) * width):
+            delta = delta_mixed[:, head(i)]
+            prob, tanh_part = prob_ref[i], tanh_ref[i]
+            delta_prob = contract_last(delta, value)
+            inner = jnp.sum(prob * delta_prob, axis=-1, keepdims=True)
+            raw = jnp.where(allowed, prob * (delta_prob - inner), 0.0)
+            raw = (raw * (1.0 - tanh_part * tanh_part)).astype(jnp.bfloat16)
+            delta_query = product(raw, key) * HEAD_SIZE ** (-0.5)
+            out_ref[:, head(i)] = rotated(delta_query, cosines, -sines).astype(jnp.bfloat16)
+            key_term = contract_first(raw, query_ref[:, head(i)])
+            value_term = contract_first(prob.astype(jnp.bfloat16), delta)
+            delta_key = key_term if delta_key is None else delta_key + key_term
+            delta_value = value_term if delta_value is None else delta_value + value_term
+        out_ref[:, head(query_heads + j)] = rotated(delta_key, cosines, -sines).astype(
+            jnp.bfloat16
+        )
+        out_ref[:, head(query_heads + kv_heads + j)] = delta_value.astype(jnp.bfloat16)
+
+
+def whole_call(body, out_shape, *operands):
+    return pl.pallas_call(
+        body,
+        out_shape=out_shape,
+        cost_estimate=BRIEF,
+        compiler_params=pltpu.CompilerParams(vmem_limit_bytes=VMEM_BYTES),
+    )(*operands)
 
 
 def fence(*values):
@@ -445,11 +642,17 @@
             self.gather_dp(gate)[None],
         )
 
-    def beside(self, values, name):
-        return values, self.gather_dp(self.later[name])[None]
+    def beside_attention(self, values):
+        return values, self.gather_dp(self.later["up"])[None]
+
+    def beside_sum(self, values):
+        return self.attn_sum(values)
+
+    def beside_rows(self, values):
+        return self.attn_rows(values)
 
     def beside_hidden(self, values):
-        return values
+        return values, self.gather_dp(self.later["down"])[None]
 
     def attn_rows(self, values):
         return lax.all_gather(values, "tensor", axis=0, tiled=True)
@@ -466,8 +669,8 @@
     def mlp_sum_rows(self, partial_sums):
         return self.scatter_dp(partial_sums[0])
 
-    def close(self, partial_out, attention_backward, totals, moments):
-        partial_mixed, partial_normed = attention_backward(partial_out)[:2]
+    def close(self, partial_out, attention_backward, totals, moments, end_norm):
+        partial_mixed, partial_normed = attention_backward(partial_out)
         cuts = (moments[0].shape[1], moments[0].shape[1] + moments[1].shape[1])
         grads = jnp.split(self.scatter_dp(partial_mixed), cuts, axis=1)
         grads = (*grads, self.scatter_dp(partial_out), totals[1], totals[2], totals[0])
@@ -475,10 +678,8 @@
         first = muon(self, states[6:] + states[4:5])
         last = muon(self, states[5:6] + states[:4])
         updates = (*last[1:], first[1], last[0], first[0])
-        return grads, states, updates, self.attn_sum(partial_normed)
-
-    def finish_gains(self, gains):
-        return self.sum_every(gains)
+        input_grad, gains = end_norm(self.attn_sum(partial_normed))
+        return grads, states, updates, input_grad, self.sum_every(gains)
 
     def sum_every(self, values):
         return lax.psum(values, self.every)
@@ -489,6 +690,9 @@
     def mlp_sum(self, lefts, rights):
         values = shrink(lefts, rights, lefts[0].shape[1], 0, jnp.float32)
         return self.attn_sum(values), values
+
+    def attn_rows_beside(self, values):
+        return self.attn_rows(values)
 
     def gram_sum(self, values):
         return [lax.psum_scatter(values, "dp", scatter_dimension=0, tiled=True)]
@@ -573,16 +777,10 @@
         across.append(shift(line[3], "x", 1))
         gate_arrived = self.arrive(gate_sent)
         down_sent = self.send(self.quarters(down))
-        inner = [self.main_quarters(narrow(m)) for m in moments]
-        inner_sent = [
-            self.send(jnp.concatenate([inner[0], inner[1]], axis=2)),
-            self.send(inner[2]),
-        ]
-        across[3], gate_arrived, up_sent, down_sent, inner_sent = lax.optimization_barrier(
-            (across[3], gate_arrived, up_sent, down_sent, inner_sent)
-        )
-        self.sent = {"up": up_sent, "down": down_sent}
-        self.inner_sent = inner_sent
+        across[3], gate_arrived, up_sent, down_sent, moments = lax.optimization_barrier(
+            (across[3], gate_arrived, up_sent, down_sent, moments)
+        )
+        self.up_sent, self.down_sent, self.moments = up_sent, down_sent, moments
 
         mixed_cols = mixed.shape[1]
         full = jnp.zeros((2, self.depth) + attn.shape, attn.dtype)
@@ -597,20 +795,49 @@
             self.gather_plane(gate_column),
         )
 
-    def beside(self, values, name):
-        arrived = self.arrive(self.sent[name])
-        values, arrived = lax.optimization_barrier((values, arrived))
-        values, column, self.sent = lax.optimization_barrier(
-            (values, self.column(arrived), self.sent)
-        )
+    def beside_attention(self, values):
+        arrived = self.arrive(self.up_sent)
+        values, arrived, down_sent = lax.optimization_barrier((values, arrived, self.down_sent))
+        values, column, moments, down_sent = lax.optimization_barrier(
+            (values, self.column(arrived), self.moments, down_sent)
+        )
+        self.down_sent, self.moments = down_sent, moments
         return values, self.gather_plane(column)
+
+    def beside_sum(self, values):
+        kept, sent = self.core_half(values)
+        received = shift(sent, "c", 1)
+        arrived = self.arrive(self.down_sent)
+        mine = kept + wide(received)
+        total = pick(mine, self.y) + wide(shift(narrow(pick(mine, 1 - self.y)), "y", 1))
+        total, arrived = lax.optimization_barrier((total, arrived))
+        total, column, moments = lax.optimization_barrier(
+            (total, self.column(arrived), self.moments)
+        )
+        self.down_full = self.gather_plane(column)
+        self.moments = moments
+        return total
+
+    def beside_rows(self, values):
+        values, moments = lax.optimization_barrier((values, self.moments))
+        line = [shift(values, "z", k) for k in range(1, self.depth)]
+        inner = [self.main_quarters(narrow(m)) for m in moments]
+        inner_sent = [
+            self.send(jnp.concatenate([inner[0], inner[1]], axis=2)),
+            self.send(inner[2]),
+        ]
+        line, inner_sent = lax.optimization_barrier((line, inner_sent))
+        line = jnp.concatenate(line, axis=0)
+        pair = shift(values, "c", 1), shift(line, "c", 1)
+        values, line, pair, inner_sent = lax.optimization_barrier((values, line, pair, inner_sent))
+        self.inner_sent = inner_sent
+        return jnp.concatenate([values, line, *pair], axis=0)
 
     def beside_hidden(self, values):
         arrived = self.arrive(self.inner_sent[0])
-        values, arrived, last = lax.optimization_barrier((values, arrived, self.inner_sent[1]))
-        self.inner_sent = last
-        self.inner = jnp.split(self.column(arrived), 2, axis=2)
-        return values
+        values, arrived = lax.optimization_barrier((values, arrived))
+        self.inner = self.column(arrived).reshape(-1, 2 * self.main)
+        return values, self.down_full
 
 
     def main_quarters(self, shard):
@@ -676,13 +903,6 @@
         stacked = partial_sums.reshape(4 * self.depth, -1, partial_sums.shape[-1])
         return lax.psum_scatter(stacked, ("y", "x"), scatter_dimension=0, tiled=True)
 
-    def mlp_finish(self, arrived):
-        column = self.column(arrived)
-        rows = column.shape[1]
-        main = column[:, :, : self.main].transpose(1, 0, 2).reshape(rows, -1)
-        rest = column[:, :, self.main :].transpose(1, 0, 2).reshape(rows, -1)
-        return wide(jnp.concatenate([main, rest], axis=1))
-
     def mlp_rows(self, values):
         line = jnp.concatenate([shift(values, "z", k) for k in range(1, self.depth)], axis=0)
         return jnp.concatenate([values, line, shift(values, "c", 1), shift(line, "c", 1)], axis=0)
@@ -698,49 +918,68 @@
         arrived = [shift(v, "z", self.depth - k) for k, v in enumerate(sent, 1)]
         return own + sum(wide(v) for v in arrived), own
 
+    def attn_rows_beside(self, values):
+        values, sent = lax.optimization_barrier((values, self.inner_sent[1]))
+        arrived = self.arrive(sent)
+        over = shift(values, "y", 1)
+        values, over, arrived = lax.optimization_barrier((values, over, arrived))
+        self.inner_last = arrived
+        pair = shift(jnp.concatenate([values, over], axis=0), "c", 1)
+        return self.order_rows(values, over, pair)
+
     def halves(self, values):
         stacked = values.reshape((2, -1) + values.shape[1:])
         return pick(stacked, self.x), pick(stacked, 1 - self.x)
 
-    def main_grams(self, total, inner):
-        state = momentum_decay * wide(inner) + wide(total[:, :, : self.main])
-        return self.halves(grams([state.reshape(-1, self.main)], self.main // HEAD_SIZE))
-
-    def close(self, partial_out, attention_backward, totals, moments):
+    def main_grams(self, total, inner, first):
+        blocks = self.main // HEAD_SIZE
+        rows = total.reshape(-1, total.shape[-1])
+        return self.halves(inner_grams(rows, inner, blocks, first * blocks))
+
+    def close(self, partial_out, attention_backward, totals, moments, end_norm):
         total_down, total_gate, total_up = totals
 
         stacked = partial_out.reshape(2, -1, partial_out.shape[1])
         kept_out, sent_out = pick(stacked, self.x), pick(stacked, 1 - self.x)
-        down_sent = self.send(total_down)
         partial_out, sent_out, down_sent = lax.optimization_barrier(
-            (partial_out, sent_out, down_sent)
+            (partial_out, sent_out, self.send(total_down))
         )
         received = shift(sent_out, "x", 1)
         turned_down = self.arrive(down_sent)
-        backward = attention_backward(partial_out)
-        backward, received, turned_down, total_gate = lax.optimization_barrier(
-            (backward, received, turned_down, total_gate)
-        )
-        partial_mixed, partial_normed = backward
+        partial_mixed, partial_normed = attention_backward(partial_out)
+        partial_mixed, partial_normed, received, turned_down, total_gate = (
+            lax.optimization_barrier(
+                (partial_mixed, partial_normed, received, turned_down, total_gate)
+            )
+        )
         out_rows = (wide(kept_out) + wide(received)).reshape(self.depth, -1, kept_out.shape[1])
         out_sent = self.send(narrow(out_rows))
+        gate_sent = self.send(total_gate)
         stacked = partial_mixed.reshape(2, -1, partial_mixed.shape[1])
         kept_mixed, sent_mixed = pick(stacked, self.x), pick(stacked, 1 - self.x)
         kept_normed, sent_normed = self.core_half(partial_normed)
-        out_sent, sent_mixed, sent_normed = lax.optimization_barrier(
-            (out_sent, sent_mixed, sent_normed)
+        out_sent, gate_sent, sent_mixed, sent_normed = lax.optimization_barrier(
+            (out_sent, gate_sent, sent_mixed, sent_normed)
         )
 
         received = shift(sent_mixed, "x", 1)
         out_arrived = self.arrive(out_sent)
+        turned_gate = self.arrive(gate_sent)
         normed_received = shift(sent_normed, "c", 1)
-        grad_down = self.mlp_finish(turned_down)
-        kept_grams, sent_grams = zip(
-            self.main_grams(total_down, self.inner[0]), self.main_grams(total_gate, self.inner[1])
-        )
-        kept_grams, sent_grams = jnp.concatenate(kept_grams), jnp.concatenate(sent_grams)
-        received, out_arrived, normed_received, sent_grams, total_up = lax.optimization_barrier(
-            (received, out_arrived, normed_received, sent_grams, total_up)
+        kept_down, sent_down = self.main_grams(total_down, self.inner, 0)
+        kept_gate, sent_gate = self.main_grams(total_gate, self.inner, 1)
+        sent_grams = jnp.concatenate([sent_down, sent_gate])
+        received, out_arrived, turned_gate, normed_received, sent_grams, turned_down = (
+            lax.optimization_barrier(
+                (
+                    received,
+                    out_arrived,
+                    turned_gate,
+                    normed_received,
+                    sent_grams,
+                    turned_down,
+                )
+            )
         )
 
         mixed_rows = (wide(kept_mixed) + wide(received)).reshape(
@@ -750,95 +989,99 @@
         received_grams = shift(sent_grams, "x", 1)
         mine = kept_normed + wide(normed_received)
         normed_received = shift(narrow(pick(mine, 1 - self.y)), "y", 1)
-        inner_arrived = self.arrive(self.inner_sent)
-        grad_out = sum(wide(v) for v in out_arrived)
-        both_sent = [jnp.concatenate(v, axis=0) for v in zip(self.send(total_gate), self.send(total_up))]
-        (
-            mixed_arrived,
-            received_grams,
-            normed_received,
-            both_sent,
-            inner_arrived,
-        ) = lax.optimization_barrier(
-            (mixed_arrived, received_grams, normed_received, both_sent, inner_arrived)
-        )
-        summed_normed = pick(mine, self.y) + wide(normed_received)
-
-        both_arrived = self.arrive(both_sent)
-        grad_mixed = sum(wide(v) for v in mixed_arrived)
-        cuts = (moments[0].shape[1], moments[0].shape[1] + moments[1].shape[1])
-        grads = [*jnp.split(grad_mixed, cuts, axis=1), grad_out]
-        states = [momentum_decay * m + g for m, g in zip(moments, grads)]
-        kept_attn, sent_attn = self.halves(grams(states, self.owners))
+        finished_down = finish(turned_down, self.z, moments[6], self.main)
+        finished_gate = finish(turned_gate, self.z, moments[4], self.main)
+        inner_last = self.column(self.inner_last).reshape(-1, self.main)
+        mixed_arrived, received_grams, normed_received, inner_last, total_up = (
+            lax.optimization_barrier(
+                (mixed_arrived, received_grams, normed_received, inner_last, total_up)
+            )
+        )
+        input_grad, gains = end_norm(pick(mine, self.y) + wide(normed_received))
+
+        turned_up = self.arrive(self.send(total_up))
+        kept_last, sent_last = self.main_grams(total_up, inner_last, 0)
+        received_last = shift(sent_last, "x", 1)
+        grads, states, attn_grams = attn_finish(
+            mixed_arrived, out_arrived, moments[:4], self.owners
+        )
+        kept_attn, sent_attn = self.halves(attn_grams)
         received_attn = shift(sent_attn, "x", 1)
-        kept_last, sent_last = self.main_grams(total_up, self.column(inner_arrived))
-        received_last = shift(sent_last, "x", 1)
-        both_arrived, received_attn, received_last = lax.optimization_barrier(
-            (both_arrived, received_attn, received_last)
-        )
-
-        rows = both_arrived[0].shape[0] // 2
-        grad_gate = self.mlp_finish([v[:rows] for v in both_arrived])
-        grad_up = self.mlp_finish([v[rows:] for v in both_arrived])
-        grads += [grad_gate, grad_up, grad_down]
-        states += [momentum_decay * m + g for m, g in zip(moments[4:], grads[4:])]
+        main_factors = newton([jnp.concatenate([kept_down, kept_gate]), received_grams])
+        turned_up, received_attn, received_last, main_factors, gains = lax.optimization_barrier(
+            (turned_up, received_attn, received_last, main_factors, gains)
+        )
+
         attn_arrived = self.arrive(self.send((kept_attn + received_attn)[:, None]))
-        kept_rest, sent_rest = self.halves(
-            grams([v[:, -HEAD_SIZE:] for v in states[4:]], self.owners)
-        )
+        finished_up = finish(turned_up, self.z, moments[5], self.main)
+        finished = finished_gate, finished_up, finished_down
+        edges = jnp.zeros((self.owners, 3, HALF, HALF), jnp.float32)
+        edges = lax.dynamic_update_slice_in_dim(
+            edges, jnp.concatenate([v[2] for v in finished]), 0, 0
+        )
+        kept_rest, sent_rest = self.halves(edges)
         received_rest = shift(sent_rest, "x", 1)
-        main_factors = newton(
-            [
-                jnp.concatenate([kept_grams, kept_last]),
-                jnp.concatenate([received_grams, received_last]),
-            ]
-        )
-        attn_arrived, received_rest, main_factors = lax.optimization_barrier(
-            (attn_arrived, received_rest, main_factors)
+        last_factor = newton([kept_last, received_last])
+        main_line = self.along_sent(main_factors)
+        gains = gains + shift(gains, "c", 1)
+        attn_arrived, received_rest, last_factor, main_line, gains = lax.optimization_barrier(
+            (attn_arrived, received_rest, last_factor, main_line, gains)
         )
 
         rest_arrived = self.arrive(self.send((kept_rest + received_rest)[:, None]))
-        factors = jnp.concatenate([main_factors, newton(attn_arrived)])
-        rest_arrived, factors = lax.optimization_barrier((rest_arrived, factors))
-
-        line = self.along(factors)
+        main_line = self.in_order(main_line)
+        main_across = shift(main_line, "x", 1)
+        factors = jnp.concatenate([last_factor, newton(attn_arrived)])
+        gains = gains + shift(gains, "y", 1)
+        rest_arrived, main_across, factors, gains = lax.optimization_barrier(
+            (rest_arrived, main_across, factors, gains)
+        )
+
+        grads += [v[0] for v in finished]
+        states += [v[1] for v in finished]
+        line = self.along_sent(factors)
         rest_factors = newton(rest_arrived)
-        line, rest_factors = fence(line, rest_factors)
-
+        gains = gains + shift(gains, "x", 1)
+        line, rest_factors, gains = lax.optimization_barrier((line, rest_factors, gains))
+
+        line = self.in_order(line)
         across = shift(line, "x", 1)
-        rest_line = self.along(rest_factors)
-        across, rest_line = fence(across, rest_line)
-
-        rest = self.both(rest_line, shift(rest_line, "x", 1))[:, :, 0]
-        rest = rest.reshape((-1,) + rest.shape[2:])
-        full = self.both(line, across)
-        attn_factors = full[:, :, 3].reshape((-1,) + full.shape[3:])
-        main = full[:, :, :3].transpose(2, 1, 0, 3, 4, 5).reshape((3, -1) + full.shape[3:])
+        rest_line = self.along_sent(rest_factors)
+        main = self.main_blocks(main_line, main_across)
+        across, rest_line = lax.optimization_barrier((across, rest_line))
+
+        gains = gains + sum(shift(gains, "z", k) for k in range(1, self.depth))
+        rest_line = self.in_order(rest_line)
+        rest = self.both(rest_line, shift(rest_line, "x", 1))
+        rest = rest.reshape((-1,) + rest.shape[3:])
+        main = jnp.concatenate([main, self.main_blocks(line[:, :1], across[:, :1])])
+        attn_factors = self.both(line[:, 1], across[:, 1])
+        attn_factors = attn_factors.reshape((-1,) + attn_factors.shape[2:])
         counts, starts = spans(states[:4])
         updates = [apply_factor(v, attn_factors, s) for v, s in zip(states[:4], starts)]
         for i, order in enumerate((1, 2, 0)):
-            updates.append(
-                apply_factor(
-                    states[4 + i], jnp.concatenate([main[order], rest[i : i + 1]], axis=0), 0
-                )
-            )
-        self.last = line
-        return grads, states, updates, summed_normed
-
-    def along(self, values):
-        line = jnp.zeros((self.depth,) + values.shape, values.dtype)
-        for k in range(self.depth):
-            line = place(line, shift(values, "z", k) if k else values, self.back(k))
+            blocks = main.shape[1]
+            partly = apply_factor(states[4 + i], main[order], 0, 0, blocks)
+            updates.append(apply_factor(states[4 + i], rest, i, blocks, blocks + 1, partly))
+        return grads, states, updates, input_grad, gains
+
+    def along_sent(self, values):
+        return [values] + [shift(values, "z", k) for k in range(1, self.depth)]
+
+    def in_order(self, arrived):
+        line = jnp.zeros((self.depth,) + arrived[0].shape, arrived[0].dtype)
+        for k, values in enumerate(arrived):
+            line = place(line, values, self.back(k))
         return line
+
+    def main_blocks(self, line, across):
+        full = self.both(line, across)
+        full = full.transpose(2, 1, 0, 3, 4, 5)
+        return full.reshape(full.shape[:1] + (-1,) + full.shape[3:])
 
     def both(self, line, across):
         full = jnp.zeros((2,) + line.shape, line.dtype)
         return place(place(full, line, self.x), across, 1 - self.x)
-
-    def finish_gains(self, gains):
-        for axis in ("c", "y", "x"):
-            gains = gains + shift(gains, axis, 1)
-        return gains + sum(shift(gains, "z", k) for k in range(1, self.depth))
 
 
 def muon(ways, states):
@@ -872,7 +1115,6 @@
     ways.setup()
     local_rows = tokens.shape[0]
     segment, position, is_alive = slot_layout(dealt_lengths[0])
-    allowed = allowed_pairs(segment, is_alive)
     rotary_cosines, rotary_sines = rope_tables(position)
     my_alive = lax.dynamic_slice_in_dim(is_alive, ways.part * local_rows, local_rows)
     query_cols = query_weight.shape[1]
@@ -894,39 +1136,30 @@
         (moment_down, moment_gate, moment_up),
     )
     projected = jnp.dot(normed_full, mixed_full, preferred_element_type=jnp.float32)
-    projected_queries, projected_keys, projected_values = jnp.split(projected, cuts, axis=1)
-    projected_queries = projected_queries.reshape(GROUP_SLOTS, -1, HEAD_SIZE)
-    projected_keys = projected_keys.reshape(GROUP_SLOTS, kv_heads, HEAD_SIZE)
-    value_rows_packed = projected_values.astype(jnp.bfloat16).reshape(
-        GROUP_SLOTS, kv_heads, HEAD_SIZE
-    )
-    query_rows_rotated = (
-        (apply_rotary(projected_queries, rotary_cosines, rotary_sines) * HEAD_SIZE ** (-0.5))
-        .astype(jnp.bfloat16)
-        .reshape(GROUP_SLOTS, kv_heads, group_width, HEAD_SIZE)
-    )
-    key_vectors = apply_rotary(projected_keys, rotary_cosines, rotary_sines).astype(jnp.bfloat16)
-    tanh_part, masked = attention_scores(query_rows_rotated, key_vectors, allowed)
-    row_max = jnp.max(masked, axis=-1, keepdims=True)
-    exponent = jnp.exp(masked - row_max)
-    row_total = jnp.sum(exponent, axis=-1, keepdims=True)
-    prob_exact = exponent / row_total
-    prob_low = prob_exact.astype(jnp.bfloat16)
-    mixed_heads = (
-        jnp.einsum(
-            "kgts,skd->tkgd", prob_low, value_rows_packed, preferred_element_type=jnp.float32
-        )
-        .reshape(GROUP_SLOTS, query_cols)
-        .astype(jnp.bfloat16)
-    )
-    partial_attended, up_full = ways.beside(contract_last(mixed_heads, out_full), "up")
-    attended, down_full = ways.beside(ways.attn_sum(partial_attended), "down")
+    alive_flags = is_alive.astype(jnp.int32)
+    marks = (segment[:, None], segment[None, :], alive_flags[:, None], alive_flags[None, :])
+    heads = query_cols // HEAD_SIZE
+    square = jax.ShapeDtypeStruct((heads, GROUP_SLOTS, GROUP_SLOTS), jnp.float32)
+    narrow_rows = [
+        jax.ShapeDtypeStruct((GROUP_SLOTS, c), jnp.bfloat16)
+        for c in (query_cols, kv_cols, kv_cols, query_cols)
+    ]
+    *kept_attention, mixed_heads = whole_call(
+        partial(attend_body, kv_heads, group_width),
+        [*narrow_rows[:3], square, square, narrow_rows[3]],
+        projected,
+        rotary_cosines,
+        rotary_sines,
+        *marks,
+    )
+    partial_attended, up_full = ways.beside_attention(contract_last(mixed_heads, out_full))
+    attended = ways.beside_sum(partial_attended)
     normed_attn, inverse_attn = norm_forward(attended, norm_gains[1])
     middle = inputs + normed_attn
     normed_mid, inverse_mid = norm_forward(middle, norm_gains[2])
-    mid_full = ways.mlp_rows(normed_mid.astype(jnp.bfloat16))
+    mid_full = ways.beside_rows(normed_mid.astype(jnp.bfloat16))
     hidden, activated, pulled = enter(mid_full, gate_full, up_full)
-    hidden = ways.beside_hidden(hidden)
+    hidden, down_full = ways.beside_hidden(hidden)
     feed_out, _ = ways.mlp_sum([hidden], [down_full])
     normed_feed, inverse_feed = norm_forward(feed_out, norm_gains[3])
     block_output = (middle + normed_feed).astype(jnp.bfloat16)
@@ -939,52 +1172,26 @@
     feed_grad = after(feed_grad, partial_down)
     delta_gate, delta_up = leave(feed_grad, down_full, activated, pulled)
     delta_mid, token = ways.mlp_sum([delta_gate, delta_up], [gate_full, up_full])
-    mid_again = after(mid_full, token)
-    total_gate = ways.mlp_sum_rows(outer(mid_again, delta_gate))
-    total_up = ways.mlp_sum_rows(outer(mid_again, delta_up))
+    total_gate = ways.mlp_sum_rows(outer(after(mid_full, token), delta_gate))
 
     mid_back, gain_mid = norm_backward(middle, inverse_mid, norm_gains[2], delta_mid)
     delta_middle = upstream + mid_back
     delta_attended, gain_attn = norm_backward(attended, inverse_attn, norm_gains[1], delta_middle)
-    attn_grad = ways.attn_rows(delta_attended.astype(jnp.bfloat16))
+    attn_grad = ways.attn_rows_beside(delta_attended.astype(jnp.bfloat16))
+    total_up = ways.mlp_sum_rows(outer(after(mid_full, attn_grad), delta_up))
     partial_out = narrow(contract_first(attn_grad, mixed_heads))
 
     def attention_backward(start):
-        delta_mixed = (
-            jnp.dot(after(attn_grad, start), out_full, preferred_element_type=jnp.float32)
-            .astype(jnp.bfloat16)
-            .reshape(GROUP_SLOTS, kv_heads, group_width, HEAD_SIZE)
-        )
-        delta_prob = jnp.einsum(
-            "tkgd,skd->kgts", delta_mixed, value_rows_packed, preferred_element_type=jnp.float32
-        )
-        delta_values = (
-            jnp.einsum("kgts,tkgd->skd", prob_low, delta_mixed, preferred_element_type=jnp.float32)
-            .reshape(GROUP_SLOTS, kv_cols)
-            .astype(jnp.bfloat16)
-        )
-        row_inner = jnp.sum(prob_exact * delta_prob, axis=-1, keepdims=True)
-        delta_raw = (
-            jnp.where(allowed[None, None], prob_exact * (delta_prob - row_inner), 0.0)
-            * (1.0 - tanh_part * tanh_part)
-        ).astype(jnp.bfloat16)
-        delta_queries = jnp.einsum(
-            "kgts,skd->tkgd", delta_raw, key_vectors, preferred_element_type=jnp.float32
-        ).reshape(GROUP_SLOTS, -1, HEAD_SIZE) * HEAD_SIZE ** (-0.5)
-        delta_query_proj = (
-            apply_rotary(delta_queries, rotary_cosines, -rotary_sines)
-            .reshape(GROUP_SLOTS, query_cols)
-            .astype(jnp.bfloat16)
-        )
-        delta_keys = jnp.einsum(
-            "kgts,tkgd->skd", delta_raw, query_rows_rotated, preferred_element_type=jnp.float32
-        )
-        delta_key_proj = (
-            apply_rotary(delta_keys, rotary_cosines, -rotary_sines)
-            .reshape(GROUP_SLOTS, kv_cols)
-            .astype(jnp.bfloat16)
-        )
-        delta_mixed_proj = jnp.concatenate([delta_query_proj, delta_key_proj, delta_values], axis=1)
+        delta_mixed = narrow(product(after(attn_grad, start), out_full))
+        delta_mixed_proj = whole_call(
+            partial(attend_back_body, kv_heads, group_width),
+            jax.ShapeDtypeStruct((GROUP_SLOTS, query_cols + 2 * kv_cols), jnp.bfloat16),
+            delta_mixed,
+            rotary_cosines,
+            rotary_sines,
+            *marks,
+            *kept_attention,
+        )
         partial_mixed = narrow(contract_first(normed_full, delta_mixed_proj))
         return partial_mixed, contract_last(delta_mixed_proj, mixed_full)
 
@@ -997,12 +1204,14 @@
         moment_up,
         moment_down,
     )
-    grads, states, updates, delta_normed = ways.close(
-        partial_out, attention_backward, (total_down, total_gate, total_up), moments
-    )
-    in_back, gain_in = norm_backward(inputs, inverse_in, norm_gains[0], delta_normed)
-    input_grad = delta_middle + in_back
-    gain_grads = ways.finish_gains(jnp.stack([gain_in, gain_attn, gain_mid, gain_feed]))
+    def end_norm(delta_normed):
+        in_back, gain_in = norm_backward(inputs, inverse_in, norm_gains[0], delta_normed)
+        gains = jnp.stack([gain_in, gain_attn, gain_mid, gain_feed])
+        return delta_middle + in_back, gains
+
+    grads, states, updates, input_grad, gain_grads = ways.close(
+        partial_out, attention_backward, (total_down, total_gate, total_up), moments, end_norm
+    )
     return (
         ways.features_out(block_output),
         ways.features_out(input_grad),

time: 1110 us -> 1040 us (0.937)
  waiting for transfers between devices: 385 us -> 338 us
  other arithmetic: 91.5 us -> 69.1 us
  Pallas kernels: 149 us -> 171 us
  local copies, waits for them, and re-layouts: 202 us -> 181 us
  starting transfers between devices: 213 us -> 227 us
    ppermute x86 -> x93, waiting for transfers between devices: 360 us -> 313 us  [shift(): lax.ppermute(values, axis, [(i, (i + distance) % size) for i in range(siz...]
    pallas_call x12 -> x19, Pallas kernels: 29.7 us -> 49.3 us  [the longest x10 21.8 us: apply_factor(): pl.pallas_call(apply_body, grid=(high - low,), in_specs=[block, pl.BlockS...]
    add x16 -> x7, other arithmetic: 21.2 us -> 8.08 us  [the longest x1 2.84 us: end_norm(): return (delta_middle + in_back, gains)]
    ppermute x86 -> x93, starting transfers between devices: 213 us -> 226 us  [shift(): lax.ppermute(values, axis, [(i, (i + distance) % size) for i in range(siz...]
    dynamic_update_slice x49 -> x48, local copies, waits for them, and re-layouts: 41.4 us -> 36.3 us  [place(): lax.dynamic_update_slice(buffer, fresh, tuple(index) + (zero,) * values.n...]
    unnamed x348 -> x302, local copies, waits for them, and re-layouts: 61.9 us -> 58.2 us
  transfers between devices with their start and end apart: 92 -> 99, of which waited for: 40 -> 42; matrix products, arithmetic and copies ran while one was open for 25% -> 22% of each run, Pallas kernels for 11% -> 13%
where the time goes in v2:
time: 1040 us; the launch traced here: 1030 us
  waiting for transfers between devices  338 us (32%)
  starting transfers between devices  227 us (22%)
  local copies, waits for them, and re-layouts  181 us (17%)
  Pallas kernels  171 us (16%)
  other arithmetic  69.1 us (7%)
  matrix products  28.9 us (3%)
  between operations  17 us (2%)
    ppermute x93, waiting for transfers between devices, shift(): lax.ppermute(values, axis, [(i, (i + distance) % size) for i in range(siz...  313 us
    ppermute x93, starting transfers between devices, shift(): lax.ppermute(values, axis, [(i, (i + distance) % size) for i in range(siz...  226 us
    pallas_call x9, Pallas kernels, dense_call(): pl.pallas_call(body, grid=grid, in_specs=in_specs, out_specs=out_specs, o...  102 us
    unnamed x302, local copies, waits for them, and re-layouts  58.2 us
    dynamic_update_slice x48, local copies, waits for them, and re-layouts, place(): lax.dynamic_update_slice(buffer, fresh, tuple(index) + (zero,) * values.n...  36.3 us
    all_gather x3, waiting for transfers between devices, gather_plane(): full = lax.all_gather(column, ('y', 'x'), axis=0, tiled=True)  25.1 us
    pallas_call x10, Pallas kernels, apply_factor(): pl.pallas_call(apply_body, grid=(high - low,), in_specs=[block, pl.BlockS...  21.8 us
  transfers between devices with their start and end apart: 99, of which 42 were waited for; matrix products, arithmetic and copies ran while one was open for 22% of the time, Pallas kernels for 13%

profile of v2, /device:TPU:0, one launch (start us, length us, event | category | flops | bytes accessed | tf_op | source)
XLA Modules:
  0.0 1030.8 jit_solution(9331511338315065035)
XLA Ops:
  29.7 7.5 collective-permute-done.2
  46.7 4.8 fusion.27
  70.4 4.8 fusion.23
  96.2 4.8 fusion.19
  108.5 5.4 collective-permute-done.10
  124.4 7.6 collective-permute-start.12
  134.5 6.8 fusion.3.refs_0_
  141.3 4.6 shard_map.361
  145.9 5.9 fusion.8
  167.0 8.1 collective-permute-start.17
  178.5 15.4 %collective-permute-done.16 = bf16[128,2304]{1,0:T(8,128)(2,1)} collective-permute-done((bf16[128,2304]{1,0:T(8,128)(2,1)}, bf16[128,2304]{1,0:T(8,128)(2,1)}, u32[]{:S(2)}, u32[]{:S(2)}) %collective-permute-start.16) | collective-permute-done | bytes 589856 | tf_op jit(solution)/shard_map/ppermute | solution.py:706
  195.5 7.2 collective-permute-done.18
  209.2 8.4 collective-permute-start.20
  231.5 9.8 fusion.15
  251.9 5.3 constant_dynamic-slice_fusion.14
  268.2 8.6 collective-permute-start.25
  285.8 22.1 %shard_map.362 = (bf16[2,1024,576]{2,1,0:T(8,128)(2,1)S(1)}, bf16[2,1024,576]{2,1,0:T(8,128)(2,1)}, bf16[2,1024,576]{2,1,0:T(8,128)(2,1)}) custom-call(bf16[1024,2304]{1,0:T(8,128)(2,1)} %constant_dynamic-update-slice_fusion.7.rows_ref.left_ref, bf16[2,2304,576]{2,1,0:T(8,128)(2,1)} %bitcast.378, bf16[2,2304,576]{2,1,0:T(8,128)(2,1)} %bitcast.381), custom_call_target="tpu_custom_call" | custom-call | flops 1024 | bytes 1024 | tf_op jit(solution)/shard_map/pallas_call | solution.py:397
  309.4 9.6 collective-permute-done.26
  319.0 25.1 %all-gather.8.cloned.1.call-done = bf16[16,288,576]{2,1,0:T(8,128)(2,1)} async-done(((bf16[4,288,576]{2,1,0:T(8,128)(2,1)}), bf16[16,288,576]{2,1,0:T(8,128)(2,1)}) %all-gather.8.cloned.1.call-update) | async-done | bytes 5308432 | tf_op jit(solution)/shard_map/all_gather | solution.py:868
  344.1 6.4 shard_map.363
  350.6 6.4 shard_map.364
  374.1 5.8 collective-permute-done.31
  379.9 24.8 %collective-permute-done.30 = bf16[128,2304]{1,0:T(8,128)(2,1)} collective-permute-done((bf16[128,2304]{1,0:T(8,128)(2,1)}, bf16[128,2304]{1,0:T(8,128)(2,1)}, u32[]{:S(2)}, u32[]{:S(2)}) %collective-permute-start.30) | collective-permute-done | bytes 589856 | tf_op jit(solution)/shard_map/ppermute | solution.py:706
  408.7 13.2 %collective-permute-start.32 = (bf16[128,2304]{1,0:T(8,128)(2,1)S(1)}, bf16[128,2304]{1,0:T(8,128)(2,1)S(1)}, u32[]{:S(2)}, u32[]{:S(2)}) collective-permute-start(bf16[128,2304]{1,0:T(8,128)(2,1)S(1)} %get-tuple-element.643), channel_id=1, source_target_pairs={{0,8},{8,16},{16,24},{24,0},{1,9},{9,17},{17,25},{25,1},{2,10},{10... | collective-permute-start | bytes 1769480 | tf_op jit(solution)/shard_map/ppermute | solution.py:706
  424.3 12.8 %collective-permute-done.32 = bf16[128,2304]{1,0:T(8,128)(2,1)S(1)} collective-permute-done((bf16[128,2304]{1,0:T(8,128)(2,1)S(1)}, bf16[128,2304]{1,0:T(8,128)(2,1)S(1)}, u32[]{:S(2)}, u32[]{:S(2)}) %collective-permute-start.32) | collective-permute-done | bytes 589856 | tf_op jit(solution)/shard_map/ppermute | solution.py:706
  437.1 24.3 %collective-permute-done.33 = bf16[128,2304]{1,0:T(8,128)(2,1)S(1)} collective-permute-done((bf16[128,2304]{1,0:T(8,128)(2,1)S(1)}, bf16[128,2304]{1,0:T(8,128)(2,1)S(1)}, u32[]{:S(2)}, u32[]{:S(2)}) %collective-permute-start.33) | collective-permute-done | bytes 589856 | tf_op jit(solution)/shard_map/ppermute | solution.py:706
  469.4 10.8 %shard_map.365 = bf16[2,2304,576]{2,1,0:T(8,128)(2,1)} custom-call(bf16[1024,2304]{1,0:T(8,128)(2,1)} %copy-done.62, bf16[2,1024,576]{2,1,0:T(8,128)(2,1)S(1)} %copy-done.4), custom_call_target="tpu_custom_call" | custom-call | flops 1024 | bytes 1024 | tf_op jit(solution)/shard_map/pallas_call | solution.py:397
  480.5 12.7 %shard_map.366 = (bf16[2,1024,576]{2,1,0:T(8,128)(2,1)S(1)}, bf16[2,1024,576]{2,1,0:T(8,128)(2,1)}) custom-call(bf16[1024,2304]{1,0:T(8,128)(2,1)} %copy-done.62, bf16[2,2304,576]{2,1,0:T(8,128)(2,1)} %bitcast.386, bf16[2,1024,576]{2,1,0:T(8,128)(2,1)} %get-tuple-element.373.gelu_ref, bf16[2,1024,576]{2,1,0:T(8,128)(2,1)} %get-tuple-element.374.pull_ref), custom_call_target="tpu_custom_call" | custom-call | flops 1024 | bytes 1024 | tf_op jit(solution)/shard_map/pallas_call | solution.py:397
  494.7 11.0 %shard_map.367 = bf16[512,2304]{1,0:T(8,128)(2,1)S(1)} custom-call(bf16[2,1024,576]{2,1,0:T(8,128)(2,1)} %copy-done.1, bf16[2,1024,576]{2,1,0:T(8,128)(2,1)} %get-tuple-element.378.refs_1_.right_ref, bf16[2,2304,576]{2,1,0:T(8,128)(2,1)} %bitcast.379, bf16[2,2304,576]{2,1,0:T(8,128)(2,1)} %bitcast.382), custom_call_target="tpu_custom_call" | custom-call | flops 1024 | bytes 1024 | tf_op jit(solution)/shard_map/pallas_call | solution.py:397
  505.9 11.0 %shard_map.368 = bf16[512,2304]{1,0:T(8,128)(2,1)S(1)} custom-call(bf16[2,1024,576]{2,1,0:T(8,128)(2,1)} %copy-done.1, bf16[2,1024,576]{2,1,0:T(8,128)(2,1)} %get-tuple-element.378.refs_1_.right_ref, bf16[2,2304,576]{2,1,0:T(8,128)(2,1)} %bitcast.380, bf16[2,2304,576]{2,1,0:T(8,128)(2,1)} %bitcast.383), custom_call_target="tpu_custom_call" | custom-call | flops 1024 | bytes 1024 | tf_op jit(solution)/shard_map/pallas_call | solution.py:397
  522.9 10.9 %shard_map.370 = bf16[2,2304,576]{2,1,0:T(8,128)(2,1)} custom-call(bf16[1024,2304]{1,0:T(8,128)(2,1)} %constant_dynamic-update-slice_fusion.7.rows_ref.left_ref, bf16[2,1024,576]{2,1,0:T(8,128)(2,1)S(1)} %copy-done.2), custom_call_target="tpu_custom_call" | custom-call | flops 1024 | bytes 1024 | tf_op jit(solution)/shard_map/pallas_call | solution.py:397
  533.9 13.5 %collective-permute-start.40 = (bf16[128,2304]{1,0:T(8,128)(2,1)}, bf16[128,2304]{1,0:T(8,128)(2,1)S(1)}, u32[]{:S(2)}, u32[]{:S(2)}) collective-permute-start(bf16[128,2304]{1,0:T(8,128)(2,1)} %get-tuple-element.382), channel_id=1, source_target_pairs={{0,8},{8,16},{16,24},{24,0},{1,9},{9,17},{17,25},{25,1},{2,10},{10... | collective-permute-start | bytes 1769480 | tf_op jit(solution)/shard_map/ppermute | solution.py:706
  549.9 13.4 %collective-permute-done.40 = bf16[128,2304]{1,0:T(8,128)(2,1)S(1)} collective-permute-done((bf16[128,2304]{1,0:T(8,128)(2,1)}, bf16[128,2304]{1,0:T(8,128)(2,1)S(1)}, u32[]{:S(2)}, u32[]{:S(2)}) %collective-permute-start.40) | collective-permute-done | bytes 589856 | tf_op jit(solution)/shard_map/ppermute | solution.py:706
  563.2 24.8 %collective-permute-done.39 = bf16[128,2304]{1,0:T(8,128)(2,1)S(1)} collective-permute-done((bf16[128,2304]{1,0:T(8,128)(2,1)}, bf16[128,2304]{1,0:T(8,128)(2,1)S(1)}, u32[]{:S(2)}, u32[]{:S(2)}) %collective-permute-start.39) | collective-permute-done | bytes 589856 | tf_op jit(solution)/shard_map/ppermute | solution.py:706
  593.5 13.1 %collective-permute-start.42 = (bf16[288,512]{1,0:T(8,128)(2,1)S(1)}, bf16[288,512]{1,0:T(8,128)(2,1)S(1)}, u32[]{:S(2)}, u32[]{:S(2)}) collective-permute-start(bf16[288,512]{1,0:T(8,128)(2,1)S(1)} %bitcast.440), channel_id=1, source_target_pairs={{0,8},{8,16},{16,24},{24,0},{1,9},{9,17},{17,25},{25,1},{2,10},{10... | collective-permute-start | bytes 884744 | tf_op jit(solution)/shard_map/ppermute | solution.py:706
  609.4 5.8 collective-permute-done.42
  615.2 11.2 %collective-permute-done.43 = bf16[288,512]{1,0:T(8,128)(2,1)S(1)} collective-permute-done((bf16[288,512]{1,0:T(8,128)(2,1)S(1)}, bf16[288,512]{1,0:T(8,128)(2,1)S(1)}, u32[]{:S(2)}, u32[]{:S(2)}) %collective-permute-start.43) | collective-permute-done | bytes 294944 | tf_op jit(solution)/shard_map/ppermute | solution.py:706
  633.1 10.8 %shard_map.373 = bf16[2,2304,576]{2,1,0:T(8,128)(2,1)} custom-call(bf16[1024,2304]{1,0:T(8,128)(2,1)} %constant_dynamic-update-slice_fusion.7.rows_ref.left_ref, bf16[2,1024,576]{2,1,0:T(8,128)(2,1)S(1)} %copy-done), custom_call_target="tpu_custom_call" | custom-call | flops 1024 | bytes 1024 | tf_op jit(solution)/shard_map/pallas_call | solution.py:397
  647.9 4.4 shard_map.369
  660.1 6.7 fusion.1
  666.7 6.3 collective-permute-start.47
  675.4 4.3 convolution_convert_fusion
  679.8 4.3 collective-permute-done.47.refs_1_
  684.8 14.2 %collective-permute-done.48.refs_2_ = bf16[288,576]{1,0:T(8,128)(2,1)S(1)} collective-permute-done((bf16[288,576]{1,0:T(8,128)(2,1)S(1)}, bf16[288,576]{1,0:T(8,128)(2,1)S(1)}, u32[]{:S(2)}, u32[]{:S(2)}) %collective-permute-start.48) | collective-permute-done | bytes 331808 | tf_op jit(solution)/shard_map/ppermute | solution.py:706
  700.5 12.2 %collective-permute-done.46 = bf16[1152,512]{1,0:T(8,128)(2,1)} collective-permute-done((bf16[1152,512]{1,0:T(8,128)(2,1)S(1)}, bf16[1152,512]{1,0:T(8,128)(2,1)}, u32[]{:S(2)}, u32[]{:S(2)}) %collective-permute-start.46) | collective-permute-done | bytes 1179680 | tf_op jit(solution)/shard_map/ppermute | solution.py:706
  738.6 11.3 %collective-permute-start.54 = (bf16[288,576]{1,0:T(8,128)(2,1)}, bf16[288,576]{1,0:T(8,128)(2,1)S(1)}, u32[]{:S(2)}, u32[]{:S(2)}) collective-permute-start(bf16[288,576]{1,0:T(8,128)(2,1)} %get-tuple-element.415), channel_id=1, source_target_pairs={{0,8},{8,16},{16,24},{24,0},{1,9},{9,17},{17,25},{25,1},{2,10},{10... | collective-permute-start | bytes 995336 | tf_op jit(solution)/shard_map/ppermute | solution.py:706
  752.4 9.1 collective-permute-start.56
  765.6 15.5 %collective-permute-done.55.refs_2_ = bf16[288,576]{1,0:T(8,128)(2,1)S(1)} collective-permute-done((bf16[288,576]{1,0:T(8,128)(2,1)}, bf16[288,576]{1,0:T(8,128)(2,1)S(1)}, u32[]{:S(2)}, u32[]{:S(2)}) %collective-permute-start.55) | collective-permute-done | bytes 331808 | tf_op jit(solution)/shard_map/ppermute | solution.py:706
  781.1 7.8 collective-permute-done.56.refs_3_
  810.8 23.2 %collective-permute-done.59.refs_2_ = bf16[288,1024]{1,0:T(8,128)(2,1)} collective-permute-done((bf16[288,1024]{1,0:T(8,128)(2,1)}, bf16[288,1024]{1,0:T(8,128)(2,1)}, u32[]{:S(2)}, u32[]{:S(2)}) %collective-permute-start.59) | collective-permute-done | bytes 589856 | tf_op jit(solution)/shard_map/ppermute | solution.py:706
  834.2 4.4 shard_map.375
  840.2 13.0 %collective-permute-start.63 = (bf16[288,576]{1,0:T(8,128)(2,1)S(1)}, bf16[288,576]{1,0:T(8,128)(2,1)S(1)}, u32[]{:S(2)}, u32[]{:S(2)}) collective-permute-start(bf16[288,576]{1,0:T(8,128)(2,1)S(1)} %get-tuple-element.680), channel_id=1, source_target_pairs={{0,8},{8,16},{16,24},{24,0},{1,9},{9,17},{17,25},{25,1},{2,10},{10... | collective-permute-start | bytes 995336 | tf_op jit(solution)/shard_map/ppermute | solution.py:706
  858.3 6.6 shard_map.377
  867.9 9.6 collective-permute-done.64.refs_2_
  883.4 8.3 collective-permute-start.68
  903.1 12.4 %collective-permute-done.69.refs_2_ = f32[1,3,128,128]{3,2,1,0:T(8,128)S(1)} collective-permute-done((f32[1,3,128,128]{3,2,1,0:T(8,128)}, f32[1,3,128,128]{3,2,1,0:T(8,128)S(1)}, u32[]{:S(2)}, u32[]{:S(2)}) %collective-permute-start.69) | collective-permute-done | bytes 196640 | tf_op jit(solution)/shard_map/ppermute | solution.py:706
  916.1 4.2 shard_map.380
  935.5 4.8 collective-permute-start.76
  944.9 4.2 shard_map.381
  952.8 4.7 collective-permute-start.81
  964.2 4.6 shard_map.387.refs_0_
  968.8 4.6 shard_map.391.refs_0_
  973.4 4.2 shard_map.382
  1015.2 4.6 shard_map.389.refs_0_
  (684 shorter events, 390.1 us)
Async XLA Ops:
  7.2 278.6 %all-gather.4.cloned.1.call-start = ((), (), s32[]{:S(2)}) async-start(), calls=%async_computation.3 | async-start | bytes 7372800 | tf_op jit(solution)/shard_map/all_gather | solution.py:868
  13.8 23.4 %collective-permute-start = (bf16[288,1536]{1,0:T(8,128)(2,1)}, bf16[288,1536]{1,0:T(8,128)(2,1)}, u32[]{:S(2)}, u32[]{:S(2)}) collective-permute-start(bf16[288,1536]{1,0:T(8,128)(2,1)} %constant_dynamic-update-slice_fusion), channel_id=1, source_target_pairs={{0,4},{4,0},{1,5},{5,1},{2,6},{6,2},{3,7},{7,3},{8,12},{12,8},{9,1... | collective-permute-start | bytes 2654216 | tf_op jit(solution)/shard_map/ppermute | solution.py:706
  16.8 23.3 %collective-permute-start.1 = (bf16[288,1536]{1,0:T(8,128)(2,1)}, bf16[288,1536]{1,0:T(8,128)(2,1)}, u32[]{:S(2)}, u32[]{:S(2)}) collective-permute-start(bf16[288,1536]{1,0:T(8,128)(2,1)} %constant_dynamic-update-slice_fusion), channel_id=1, source_target_pairs={{0,8},{8,16},{16,24},{24,0},{1,9},{9,17},{17,25},{25,1},{2,10},{10... | collective-permute-start | bytes 2654216 | tf_op jit(solution)/shard_map/ppermute | solution.py:706
  40.1 20.6 %collective-permute-start.3 = (bf16[288,1536]{1,0:T(8,128)(2,1)}, bf16[288,1536]{1,0:T(8,128)(2,1)}, u32[]{:S(2)}, u32[]{:S(2)}) collective-permute-start(bf16[288,1536]{1,0:T(8,128)(2,1)} %collective-permute-done.1), channel_id=1, source_target_pairs={{0,4},{4,0},{1,5},{5,1},{2,6},{6,2},{3,7},{7,3},{8,12},{12,8},{9,1... | collective-permute-start | bytes 2654216 | tf_op jit(solution)/shard_map/ppermute | solution.py:706
  40.6 22.4 %collective-permute-start.4 = (bf16[288,1536]{1,0:T(8,128)(2,1)}, bf16[288,1536]{1,0:T(8,128)(2,1)}, u32[]{:S(2)}, u32[]{:S(2)}) collective-permute-start(bf16[288,1536]{1,0:T(8,128)(2,1)} %collective-permute-done.1), channel_id=1, source_target_pairs={{0,8},{8,16},{16,24},{24,0},{1,9},{9,17},{17,25},{25,1},{2,10},{10... | collective-permute-start | bytes 2654216 | tf_op jit(solution)/shard_map/ppermute | solution.py:706
  63.0 19.7 %collective-permute-start.6 = (bf16[288,1536]{1,0:T(8,128)(2,1)}, bf16[288,1536]{1,0:T(8,128)(2,1)}, u32[]{:S(2)}, u32[]{:S(2)}) collective-permute-start(bf16[288,1536]{1,0:T(8,128)(2,1)} %collective-permute-done.4), channel_id=1, source_target_pairs={{0,4},{4,0},{1,5},{5,1},{2,6},{6,2},{3,7},{7,3},{8,12},{12,8},{9,1... | collective-permute-start | bytes 2654216 | tf_op jit(solution)/shard_map/ppermute | solution.py:706
  64.3 20.9 %collective-permute-start.7 = (bf16[288,1536]{1,0:T(8,128)(2,1)}, bf16[288,1536]{1,0:T(8,128)(2,1)}, u32[]{:S(2)}, u32[]{:S(2)}) collective-permute-start(bf16[288,1536]{1,0:T(8,128)(2,1)} %collective-permute-done.4), channel_id=1, source_target_pairs={{0,8},{8,16},{16,24},{24,0},{1,9},{9,17},{17,25},{25,1},{2,10},{10... | collective-permute-start | bytes 2654216 | tf_op jit(solution)/shard_map/ppermute | solution.py:706
  88.0 25.9 %collective-permute-start.8 = (bf16[288,1536]{1,0:T(8,128)(2,1)}, bf16[288,1536]{1,0:T(8,128)(2,1)}, u32[]{:S(2)}, u32[]{:S(2)}) collective-permute-start(bf16[288,1536]{1,0:T(8,128)(2,1)} %collective-permute-done.7), channel_id=1, source_target_pairs={{0,4},{4,0},{1,5},{5,1},{2,6},{6,2},{3,7},{7,3},{8,12},{12,8},{9,1... | collective-permute-start | bytes 2654216 | tf_op jit(solution)/shard_map/ppermute | solution.py:706
  89.0 24.9 %collective-permute-start.10 = (bf16[288,576]{1,0:T(8,128)(2,1)}, bf16[288,576]{1,0:T(8,128)(2,1)}, u32[]{:S(2)}, u32[]{:S(2)}) collective-permute-start(bf16[288,576]{1,0:T(8,128)(2,1)} %bitcast.349), channel_id=1, source_target_pairs={{0,16},{8,24},{16,0},{24,8},{1,17},{9,25},{17,1},{25,9},{2,18},{10... | collective-permute-start | bytes 995336 | tf_op jit(solution)/shard_map/ppermute | solution.py:706
  90.7 23.2 %collective-permute-start.11 = (bf16[288,576]{1,0:T(8,128)(2,1)}, bf16[288,576]{1,0:T(8,128)(2,1)}, u32[]{:S(2)}, u32[]{:S(2)}) collective-permute-start(bf16[288,576]{1,0:T(8,128)(2,1)} %bitcast.348), channel_id=1, source_target_pairs={{0,24},{8,0},{16,8},{24,16},{1,25},{9,1},{17,9},{25,17},{2,26},{10... | collective-permute-start | bytes 995336 | tf_op jit(solution)/shard_map/ppermute | solution.py:706
  120.6 165.2 %all-gather.6.cloned.1.call-start = ((), (), s32[]{:S(2)}) async-start(), calls=%async_computation.4 | async-start | bytes 7372800 | tf_op jit(solution)/shard_map/all_gather | solution.py:868
  124.4 27.3 %collective-permute-start.12 = (bf16[288,576]{1,0:T(8,128)(2,1)S(1)}, bf16[288,576]{1,0:T(8,128)(2,1)S(1)}, u32[]{:S(2)}, u32[]{:S(2)}) collective-permute-start(bf16[288,576]{1,0:T(8,128)(2,1)S(1)} %bitcast.437), channel_id=1, source_target_pairs={{0,8},{8,16},{16,24},{24,0},{1,9},{9,17},{17,25},{25,1},{2,10},{10... | collective-permute-start | bytes 995336 | tf_op jit(solution)/shard_map/ppermute | solution.py:706
  132.0 21.6 %collective-permute-start.13 = (bf16[288,576]{1,0:T(8,128)(2,1)S(1)}, bf16[288,576]{1,0:T(8,128)(2,1)S(1)}, u32[]{:S(2)}, u32[]{:S(2)}) collective-permute-start(bf16[288,576]{1,0:T(8,128)(2,1)S(1)} %bitcast.436), channel_id=1, source_target_pairs={{0,16},{8,24},{16,0},{24,8},{1,17},{9,25},{17,1},{25,9},{2,18},{10... | collective-permute-start | bytes 995336 | tf_op jit(solution)/shard_map/ppermute | solution.py:706
  132.3 22.8 %collective-permute-start.14 = (bf16[288,576]{1,0:T(8,128)(2,1)S(1)}, bf16[288,576]{1,0:T(8,128)(2,1)S(1)}, u32[]{:S(2)}, u32[]{:S(2)}) collective-permute-start(bf16[288,576]{1,0:T(8,128)(2,1)S(1)} %bitcast.435), channel_id=1, source_target_pairs={{0,24},{8,0},{16,8},{24,16},{1,25},{9,1},{17,9},{25,17},{2,26},{10... | collective-permute-start | bytes 995336 | tf_op jit(solution)/shard_map/ppermute | solution.py:706
  156.6 187.4 %all-gather.8.cloned.1.call-start = ((), (), s32[]{:S(2)}) async-start(), calls=%async_computation.5 | async-start | bytes 7372800 | tf_op jit(solution)/shard_map/all_gather | solution.py:868
  164.7 29.1 %collective-permute-start.16 = (bf16[128,2304]{1,0:T(8,128)(2,1)}, bf16[128,2304]{1,0:T(8,128)(2,1)}, u32[]{:S(2)}, u32[]{:S(2)}) collective-permute-start(bf16[128,2304]{1,0:T(8,128)(2,1)} %fusion.31), channel_id=1, source_target_pairs={{0,2},{2,0},{1,3},{3,1},{4,6},{6,4},{5,7},{7,5},{8,10},{10,8},{9,1... | collective-permute-start | bytes 1769480 | tf_op jit(solution)/shard_map/ppermute | solution.py:706
  167.0 28.5 %collective-permute-start.17 = (bf16[288,576]{1,0:T(8,128)(2,1)}, bf16[288,576]{1,0:T(8,128)(2,1)S(1)}, u32[]{:S(2)}, u32[]{:S(2)}) collective-permute-start(bf16[288,576]{1,0:T(8,128)(2,1)} %bitcast.434), channel_id=1, source_target_pairs={{0,8},{8,16},{16,24},{24,0},{1,9},{9,17},{17,25},{25,1},{2,10},{10... | collective-permute-start | bytes 995336 | tf_op jit(solution)/shard_map/ppermute | solution.py:706
  175.1 27.6 %collective-permute-start.18 = (bf16[288,576]{1,0:T(8,128)(2,1)}, bf16[288,576]{1,0:T(8,128)(2,1)S(1)}, u32[]{:S(2)}, u32[]{:S(2)}) collective-permute-start(bf16[288,576]{1,0:T(8,128)(2,1)} %bitcast.433), channel_id=1, source_target_pairs={{0,16},{8,24},{16,0},{24,8},{1,17},{9,25},{17,1},{25,9},{2,18},{10... | collective-permute-start | bytes 995336 | tf_op jit(solution)/shard_map/ppermute | solution.py:706
  178.5 24.2 %collective-permute-start.19 = (bf16[288,576]{1,0:T(8,128)(2,1)}, bf16[288,576]{1,0:T(8,128)(2,1)S(1)}, u32[]{:S(2)}, u32[]{:S(2)}) collective-permute-start(bf16[288,576]{1,0:T(8,128)(2,1)} %bitcast.432), channel_id=1, source_target_pairs={{0,24},{8,0},{16,8},{24,16},{1,25},{9,1},{17,9},{25,17},{2,26},{10... | collective-permute-start | bytes 995336 | tf_op jit(solution)/shard_map/ppermute | solution.py:706
  204.2 452.1 %reduce-scatter.4.cloned.1.call-start = ((), (), s32[]{:S(2)}) async-start(), calls=%async_computation.6 | async-start | bytes 7372800 | tf_op jit(solution)/shard_map/reduce_scatter | solution.py:904
  209.2 51.1 %collective-permute-start.20 = (bf16[128,2304]{1,0:T(8,128)(2,1)}, bf16[128,2304]{1,0:T(8,128)(2,1)}, u32[]{:S(2)}, u32[]{:S(2)}) collective-permute-start(bf16[128,2304]{1,0:T(8,128)(2,1)} %multiply_convert_fusion), channel_id=1, source_target_pairs={{0,8},{8,16},{16,24},{24,0},{1,9},{9,17},{17,25},{25,1},{2,10},{10... | collective-permute-start | bytes 1769480 | tf_op jit(solution)/shard_map/ppermute | solution.py:706
  217.5 42.7 %collective-permute-start.21 = (bf16[128,2304]{1,0:T(8,128)(2,1)}, bf16[128,2304]{1,0:T(8,128)(2,1)}, u32[]{:S(2)}, u32[]{:S(2)}) collective-permute-start(bf16[128,2304]{1,0:T(8,128)(2,1)} %multiply_convert_fusion), channel_id=1, source_target_pairs={{0,16},{8,24},{16,0},{24,8},{1,17},{9,25},{17,1},{25,9},{2,18},{10... | collective-permute-start | bytes 1769480 | tf_op jit(solution)/shard_map/ppermute | solution.py:706
  217.6 42.7 %collective-permute-start.22 = (bf16[128,2304]{1,0:T(8,128)(2,1)}, bf16[128,2304]{1,0:T(8,128)(2,1)}, u32[]{:S(2)}, u32[]{:S(2)}) collective-permute-start(bf16[128,2304]{1,0:T(8,128)(2,1)} %multiply_convert_fusion), channel_id=1, source_target_pairs={{0,24},{8,0},{16,8},{24,16},{1,25},{9,1},{17,9},{25,17},{2,26},{10... | collective-permute-start | bytes 1769480 | tf_op jit(solution)/shard_map/ppermute | solution.py:706
  268.2 41.2 %collective-permute-start.25 = (bf16[288,1024]{1,0:T(8,128)(2,1)}, bf16[288,1024]{1,0:T(8,128)(2,1)}, u32[]{:S(2)}, u32[]{:S(2)}) collective-permute-start(bf16[288,1024]{1,0:T(8,128)(2,1)} %bitcast.338), channel_id=1, source_target_pairs={{0,8},{8,16},{16,24},{24,0},{1,9},{9,17},{17,25},{25,1},{2,10},{10... | collective-permute-start | bytes 1769480 | tf_op jit(solution)/shard_map/ppermute | solution.py:706
  276.8 42.2 %collective-permute-start.26 = (bf16[288,1024]{1,0:T(8,128)(2,1)}, bf16[288,1024]{1,0:T(8,128)(2,1)}, u32[]{:S(2)}, u32[]{:S(2)}) collective-permute-start(bf16[288,1024]{1,0:T(8,128)(2,1)} %bitcast.337), channel_id=1, source_target_pairs={{0,16},{8,24},{16,0},{24,8},{1,17},{9,25},{17,1},{25,9},{2,18},{10... | collective-permute-start | bytes 1769480 | tf_op jit(solution)/shard_map/ppermute | solution.py:706
  280.1 38.9 %collective-permute-start.27 = (bf16[288,1024]{1,0:T(8,128)(2,1)}, bf16[288,1024]{1,0:T(8,128)(2,1)}, u32[]{:S(2)}, u32[]{:S(2)}) collective-permute-start(bf16[288,1024]{1,0:T(8,128)(2,1)} %bitcast.336), channel_id=1, source_target_pairs={{0,24},{8,0},{16,8},{24,16},{1,25},{9,1},{17,9},{25,17},{2,26},{10... | collective-permute-start | bytes 1769480 | tf_op jit(solution)/shard_map/ppermute | solution.py:706
  363.0 41.7 %collective-permute-start.30 = (bf16[128,2304]{1,0:T(8,128)(2,1)}, bf16[128,2304]{1,0:T(8,128)(2,1)}, u32[]{:S(2)}, u32[]{:S(2)}) collective-permute-start(bf16[128,2304]{1,0:T(8,128)(2,1)} %get-tuple-element.370), channel_id=1, source_target_pairs={{0,16},{8,24},{16,0},{24,8},{1,17},{9,25},{17,1},{25,9},{2,18},{10... | collective-permute-start | bytes 1769480 | tf_op jit(solution)/shard_map/ppermute | solution.py:706
  365.4 39.3 %collective-permute-start.29 = (bf16[128,2304]{1,0:T(8,128)(2,1)}, bf16[128,2304]{1,0:T(8,128)(2,1)}, u32[]{:S(2)}, u32[]{:S(2)}) collective-permute-start(bf16[128,2304]{1,0:T(8,128)(2,1)} %get-tuple-element.369), channel_id=1, source_target_pairs={{0,24},{8,0},{16,8},{24,16},{1,25},{9,1},{17,9},{25,17},{2,26},{10... | collective-permute-start | bytes 1769480 | tf_op jit(solution)/shard_map/ppermute | solution.py:706
  408.7 28.4 %collective-permute-start.32 = (bf16[128,2304]{1,0:T(8,128)(2,1)S(1)}, bf16[128,2304]{1,0:T(8,128)(2,1)S(1)}, u32[]{:S(2)}, u32[]{:S(2)}) collective-permute-start(bf16[128,2304]{1,0:T(8,128)(2,1)S(1)} %get-tuple-element.643), channel_id=1, source_target_pairs={{0,8},{8,16},{16,24},{24,0},{1,9},{9,17},{17,25},{25,1},{2,10},{10... | collective-permute-start | bytes 1769480 | tf_op jit(solution)/shard_map/ppermute | solution.py:706
  421.8 39.5 %collective-permute-start.33 = (bf16[128,2304]{1,0:T(8,128)(2,1)S(1)}, bf16[128,2304]{1,0:T(8,128)(2,1)S(1)}, u32[]{:S(2)}, u32[]{:S(2)}) collective-permute-start(bf16[128,2304]{1,0:T(8,128)(2,1)S(1)} %get-tuple-element.643), channel_id=1, source_target_pairs={{0,16},{8,24},{16,0},{24,8},{1,17},{9,25},{17,1},{25,9},{2,18},{10... | collective-permute-start | bytes 1769480 | tf_op jit(solution)/shard_map/ppermute | solution.py:706
  423.3 38.0 %collective-permute-start.34 = (bf16[128,2304]{1,0:T(8,128)(2,1)S(1)}, bf16[128,2304]{1,0:T(8,128)(2,1)S(1)}, u32[]{:S(2)}, u32[]{:S(2)}) collective-permute-start(bf16[128,2304]{1,0:T(8,128)(2,1)S(1)} %get-tuple-element.643), channel_id=1, source_target_pairs={{0,24},{8,0},{16,8},{24,16},{1,25},{9,1},{17,9},{25,17},{2,26},{10... | collective-permute-start | bytes 1769480 | tf_op jit(solution)/shard_map/ppermute | solution.py:706
  480.2 232.5 %reduce-scatter.6.cloned.1.call-start = ((), (), s32[]{:S(2)}) async-start(), calls=%async_computation.7 | async-start | bytes 7372800 | tf_op jit(solution)/shard_map/reduce_scatter | solution.py:904
  533.8 277.0 %reduce-scatter.8.cloned.1.call-start = ((), (), s32[]{:S(2)}) async-start(), calls=%async_computation.8 | async-start | bytes 7372800 | tf_op jit(solution)/shard_map/reduce_scatter | solution.py:904
  533.9 29.3 %collective-permute-start.40 = (bf16[128,2304]{1,0:T(8,128)(2,1)}, bf16[128,2304]{1,0:T(8,128)(2,1)S(1)}, u32[]{:S(2)}, u32[]{:S(2)}) collective-permute-start(bf16[128,2304]{1,0:T(8,128)(2,1)} %get-tuple-element.382), channel_id=1, source_target_pairs={{0,8},{8,16},{16,24},{24,0},{1,9},{9,17},{17,25},{25,1},{2,10},{10... | collective-permute-start | bytes 1769480 | tf_op jit(solution)/shard_map/ppermute | solution.py:706
  547.4 40.6 %collective-permute-start.39 = (bf16[128,2304]{1,0:T(8,128)(2,1)}, bf16[128,2304]{1,0:T(8,128)(2,1)S(1)}, u32[]{:S(2)}, u32[]{:S(2)}) collective-permute-start(bf16[128,2304]{1,0:T(8,128)(2,1)} %get-tuple-element.381), channel_id=1, source_target_pairs={{0,16},{8,24},{16,0},{24,8},{1,17},{9,25},{17,1},{25,9},{2,18},{10... | collective-permute-start | bytes 1769480 | tf_op jit(solution)/shard_map/ppermute | solution.py:706
  549.3 38.7 %collective-permute-start.38 = (bf16[128,2304]{1,0:T(8,128)(2,1)}, bf16[128,2304]{1,0:T(8,128)(2,1)S(1)}, u32[]{:S(2)}, u32[]{:S(2)}) collective-permute-start(bf16[128,2304]{1,0:T(8,128)(2,1)} %get-tuple-element.380), channel_id=1, source_target_pairs={{0,24},{8,0},{16,8},{24,16},{1,25},{9,1},{17,9},{25,17},{2,26},{10... | collective-permute-start | bytes 1769480 | tf_op jit(solution)/shard_map/ppermute | solution.py:706
  592.0 34.4 %collective-permute-start.41 = (bf16[128,2304]{1,0:T(8,128)(2,1)S(1)}, bf16[128,2304]{1,0:T(8,128)(2,1)S(1)}, u32[]{:S(2)}, u32[]{:S(2)}) collective-permute-start(bf16[128,2304]{1,0:T(8,128)(2,1)S(1)} %subtract_convert_fusion), channel_id=1, source_target_pairs={{0,2},{2,0},{1,3},{3,1},{4,6},{6,4},{5,7},{7,5},{8,10},{10,8},{9,1... | collective-permute-start | bytes 1769480 | tf_op jit(solution)/shard_map/ppermute | solution.py:706
  593.5 21.7 %collective-permute-start.42 = (bf16[288,512]{1,0:T(8,128)(2,1)S(1)}, bf16[288,512]{1,0:T(8,128)(2,1)S(1)}, u32[]{:S(2)}, u32[]{:S(2)}) collective-permute-start(bf16[288,512]{1,0:T(8,128)(2,1)S(1)} %bitcast.440), channel_id=1, source_target_pairs={{0,8},{8,16},{16,24},{24,0},{1,9},{9,17},{17,25},{25,1},{2,10},{10... | collective-permute-start | bytes 884744 | tf_op jit(solution)/shard_map/ppermute | solution.py:706
  606.6 19.8 %collective-permute-start.43 = (bf16[288,512]{1,0:T(8,128)(2,1)S(1)}, bf16[288,512]{1,0:T(8,128)(2,1)S(1)}, u32[]{:S(2)}, u32[]{:S(2)}) collective-permute-start(bf16[288,512]{1,0:T(8,128)(2,1)S(1)} %bitcast.439), channel_id=1, source_target_pairs={{0,16},{8,24},{16,0},{24,8},{1,17},{9,25},{17,1},{25,9},{2,18},{10... | collective-permute-start | bytes 884744 | tf_op jit(solution)/shard_map/ppermute | solution.py:706
  658.7 54.0 %collective-permute-start.46 = (bf16[1152,512]{1,0:T(8,128)(2,1)S(1)}, bf16[1152,512]{1,0:T(8,128)(2,1)}, u32[]{:S(2)}, u32[]{:S(2)}) collective-permute-start(bf16[1152,512]{1,0:T(8,128)(2,1)S(1)} %copy-done.94), channel_id=1, source_target_pairs={{0,4},{4,0},{1,5},{5,1},{2,6},{6,2},{3,7},{7,3},{8,12},{12,8},{9,1... | collective-permute-start | bytes 3538952 | tf_op jit(solution)/shard_map/ppermute | solution.py:706
  673.1 26.0 %collective-permute-start.48 = (bf16[288,576]{1,0:T(8,128)(2,1)S(1)}, bf16[288,576]{1,0:T(8,128)(2,1)S(1)}, u32[]{:S(2)}, u32[]{:S(2)}) collective-permute-start(bf16[288,576]{1,0:T(8,128)(2,1)S(1)} %get-tuple-element.402), channel_id=1, source_target_pairs={{0,16},{8,24},{16,0},{24,8},{1,17},{9,25},{17,1},{25,9},{2,18},{10... | collective-permute-start | bytes 995336 | tf_op jit(solution)/shard_map/ppermute | solution.py:706
  675.1 24.7 %collective-permute-start.49 = (bf16[288,576]{1,0:T(8,128)(2,1)S(1)}, bf16[288,576]{1,0:T(8,128)(2,1)S(1)}, u32[]{:S(2)}, u32[]{:S(2)}) collective-permute-start(bf16[288,576]{1,0:T(8,128)(2,1)S(1)} %get-tuple-element.403), channel_id=1, source_target_pairs={{0,24},{8,0},{16,8},{24,16},{1,25},{9,1},{17,9},{25,17},{2,26},{10... | collective-permute-start | bytes 995336 | tf_op jit(solution)/shard_map/ppermute | solution.py:706
  721.5 67.6 %collective-permute-start.50 = (bf16[1152,1024]{1,0:T(8,128)(2,1)}, bf16[1152,1024]{1,0:T(8,128)(2,1)S(1)}, u32[]{:S(2)}, u32[]{:S(2)}) collective-permute-start(bf16[1152,1024]{1,0:T(8,128)(2,1)} %dynamic-slice_bitcast_fusion), channel_id=1, source_target_pairs={{0,4},{4,0},{1,5},{5,1},{2,6},{6,2},{3,7},{7,3},{8,12},{12,8},{9,1... | collective-permute-start | bytes 7077896 | tf_op jit(solution)/shard_map/ppermute | solution.py:706
  724.5 64.4 %collective-permute-start.57 = (bf16[2,128,2304]{2,1,0:T(8,128)(2,1)}, bf16[2,128,2304]{2,1,0:T(8,128)(2,1)}, u32[]{:S(2)}, u32[]{:S(2)}) collective-permute-start(bf16[2,128,2304]{2,1,0:T(8,128)(2,1)} %fusion.14), channel_id=1, source_target_pairs={{0,1},{1,0},{2,3},{3,2},{4,5},{5,4},{6,7},{7,6},{8,9},{9,8},{10,11... | collective-permute-start | bytes 3538952 | tf_op jit(solution)/shard_map/ppermute | solution.py:706
  728.8 22.5 %collective-permute-start.52 = (bf16[288,512]{1,0:T(8,128)(2,1)S(1)}, bf16[288,512]{1,0:T(8,128)(2,1)S(1)}, u32[]{:S(2)}, u32[]{:S(2)}) collective-permute-start(bf16[288,512]{1,0:T(8,128)(2,1)S(1)} %get-tuple-element.412), channel_id=1, source_target_pairs={{0,16},{8,24},{16,0},{24,8},{1,17},{9,25},{17,1},{25,9},{2,18},{10... | collective-permute-start | bytes 884744 | tf_op jit(solution)/shard_map/ppermute | solution.py:706
  731.2 21.2 %collective-permute-start.53 = (bf16[288,512]{1,0:T(8,128)(2,1)S(1)}, bf16[288,512]{1,0:T(8,128)(2,1)S(1)}, u32[]{:S(2)}, u32[]{:S(2)}) collective-permute-start(bf16[288,512]{1,0:T(8,128)(2,1)S(1)} %get-tuple-element.413), channel_id=1, source_target_pairs={{0,24},{8,0},{16,8},{24,16},{1,25},{9,1},{17,9},{25,17},{2,26},{10... | collective-permute-start | bytes 884744 | tf_op jit(solution)/shard_map/ppermute | solution.py:706
  738.6 27.0 %collective-permute-start.54 = (bf16[288,576]{1,0:T(8,128)(2,1)}, bf16[288,576]{1,0:T(8,128)(2,1)S(1)}, u32[]{:S(2)}, u32[]{:S(2)}) collective-permute-start(bf16[288,576]{1,0:T(8,128)(2,1)} %get-tuple-element.415), channel_id=1, source_target_pairs={{0,8},{8,16},{16,24},{24,0},{1,9},{9,17},{17,25},{25,1},{2,10},{10... | collective-permute-start | bytes 995336 | tf_op jit(solution)/shard_map/ppermute | solution.py:706
  751.3 29.8 %collective-permute-start.55 = (bf16[288,576]{1,0:T(8,128)(2,1)}, bf16[288,576]{1,0:T(8,128)(2,1)S(1)}, u32[]{:S(2)}, u32[]{:S(2)}) collective-permute-start(bf16[288,576]{1,0:T(8,128)(2,1)} %get-tuple-element.416), channel_id=1, source_target_pairs={{0,16},{8,24},{16,0},{24,8},{1,17},{9,25},{17,1},{25,9},{2,18},{10... | collective-permute-start | bytes 995336 | tf_op jit(solution)/shard_map/ppermute | solution.py:706
  752.4 36.5 %collective-permute-start.56 = (bf16[288,576]{1,0:T(8,128)(2,1)S(1)}, bf16[288,576]{1,0:T(8,128)(2,1)S(1)}, u32[]{:S(2)}, u32[]{:S(2)}) collective-permute-start(bf16[288,576]{1,0:T(8,128)(2,1)S(1)} %get-tuple-element.417), channel_id=1, source_target_pairs={{0,24},{8,0},{16,8},{24,16},{1,25},{9,1},{17,9},{25,17},{2,26},{10... | collective-permute-start | bytes 995336 | tf_op jit(solution)/shard_map/ppermute | solution.py:706
  792.9 41.2 %collective-permute-start.59 = (bf16[288,1024]{1,0:T(8,128)(2,1)}, bf16[288,1024]{1,0:T(8,128)(2,1)}, u32[]{:S(2)}, u32[]{:S(2)}) collective-permute-start(bf16[288,1024]{1,0:T(8,128)(2,1)} %get-tuple-element.655), channel_id=1, source_target_pairs={{0,16},{8,24},{16,0},{24,8},{1,17},{9,25},{17,1},{25,9},{2,18},{10... | collective-permute-start | bytes 1769480 | tf_op jit(solution)/shard_map/ppermute | solution.py:706
  795.3 38.8 %collective-permute-start.60 = (bf16[288,1024]{1,0:T(8,128)(2,1)}, bf16[288,1024]{1,0:T(8,128)(2,1)}, u32[]{:S(2)}, u32[]{:S(2)}) collective-permute-start(bf16[288,1024]{1,0:T(8,128)(2,1)} %get-tuple-element.654), channel_id=1, source_target_pairs={{0,24},{8,0},{16,8},{24,16},{1,25},{9,1},{17,9},{25,17},{2,26},{10... | collective-permute-start | bytes 1769480 | tf_op jit(solution)/shard_map/ppermute | solution.py:706
  799.8 34.3 %collective-permute-start.62 = (bf16[128,2304]{1,0:T(8,128)(2,1)}, bf16[128,2304]{1,0:T(8,128)(2,1)}, u32[]{:S(2)}, u32[]{:S(2)}) collective-permute-start(bf16[128,2304]{1,0:T(8,128)(2,1)} %fusion.32), channel_id=1, source_target_pairs={{0,2},{2,0},{1,3},{3,1},{4,6},{6,4},{5,7},{7,5},{8,10},{10,8},{9,1... | collective-permute-start | bytes 1769480 | tf_op jit(solution)/shard_map/ppermute | solution.py:706
  838.7 38.8 %collective-permute-start.66 = (f32[4,3,128,128]{3,2,1,0:T(8,128)S(1)}, f32[4,3,128,128]{3,2,1,0:T(8,128)S(1)}, u32[]{:S(2)}, u32[]{:S(2)}) collective-permute-start(f32[4,3,128,128]{3,2,1,0:T(8,128)S(1)} %dynamic-slice_bitcast_fusion.3), channel_id=1, source_target_pairs={{0,4},{4,0},{1,5},{5,1},{2,6},{6,2},{3,7},{7,3},{8,12},{12,8},{9,1... | collective-permute-start | bytes 2359304 | tf_op jit(solution)/shard_map/ppermute | solution.py:706
  840.2 27.7 %collective-permute-start.63 = (bf16[288,576]{1,0:T(8,128)(2,1)S(1)}, bf16[288,576]{1,0:T(8,128)(2,1)S(1)}, u32[]{:S(2)}, u32[]{:S(2)}) collective-permute-start(bf16[288,576]{1,0:T(8,128)(2,1)S(1)} %get-tuple-element.680), channel_id=1, source_target_pairs={{0,8},{8,16},{16,24},{24,0},{1,9},{9,17},{17,25},{25,1},{2,10},{10... | collective-permute-start | bytes 995336 | tf_op jit(solution)/shard_map/ppermute | solution.py:706
  853.2 24.3 %collective-permute-start.64 = (bf16[288,576]{1,0:T(8,128)(2,1)S(1)}, bf16[288,576]{1,0:T(8,128)(2,1)S(1)}, u32[]{:S(2)}, u32[]{:S(2)}) collective-permute-start(bf16[288,576]{1,0:T(8,128)(2,1)S(1)} %get-tuple-element.679), channel_id=1, source_target_pairs={{0,16},{8,24},{16,0},{24,8},{1,17},{9,25},{17,1},{25,9},{2,18},{10... | collective-permute-start | bytes 995336 | tf_op jit(solution)/shard_map/ppermute | solution.py:706
  854.5 23.0 %collective-permute-start.65 = (bf16[288,576]{1,0:T(8,128)(2,1)S(1)}, bf16[288,576]{1,0:T(8,128)(2,1)S(1)}, u32[]{:S(2)}, u32[]{:S(2)}) collective-permute-start(bf16[288,576]{1,0:T(8,128)(2,1)S(1)} %get-tuple-element.678), channel_id=1, source_target_pairs={{0,24},{8,0},{16,8},{24,16},{1,25},{9,1},{17,9},{25,17},{2,26},{10... | collective-permute-start | bytes 995336 | tf_op jit(solution)/shard_map/ppermute | solution.py:706
  881.9 41.8 %collective-permute-start.71 = (f32[4,3,128,128]{3,2,1,0:T(8,128)}, f32[4,3,128,128]{3,2,1,0:T(8,128)}, u32[]{:S(2)}, u32[]{:S(2)}) collective-permute-start(f32[4,3,128,128]{3,2,1,0:T(8,128)} %dynamic-slice_bitcast_fusion.2), channel_id=1, source_target_pairs={{0,4},{4,0},{1,5},{5,1},{2,6},{6,2},{3,7},{7,3},{8,12},{12,8},{9,1... | collective-permute-start | bytes 2359304 | tf_op jit(solution)/shard_map/ppermute | solution.py:706
  891.8 23.7 %collective-permute-start.69 = (f32[1,3,128,128]{3,2,1,0:T(8,128)}, f32[1,3,128,128]{3,2,1,0:T(8,128)S(1)}, u32[]{:S(2)}, u32[]{:S(2)}) collective-permute-start(f32[1,3,128,128]{3,2,1,0:T(8,128)} %get-tuple-element.716), channel_id=1, source_target_pairs={{0,16},{8,24},{16,0},{24,8},{1,17},{9,25},{17,1},{25,9},{2,18},{10... | collective-permute-start | bytes 589832 | tf_op jit(solution)/shard_map/ppermute | solution.py:706
  896.0 27.8 %collective-permute-start.72 = (bf16[2,3,128,128]{3,2,1,0:T(8,128)(2,1)S(1)}, bf16[2,3,128,128]{3,2,1,0:T(8,128)(2,1)S(1)}, u32[]{:S(2)}, u32[]{:S(2)}) collective-permute-start(bf16[2,3,128,128]{3,2,1,0:T(8,128)(2,1)S(1)} %shard_map.377), channel_id=1, source_target_pairs={{0,8},{8,16},{16,24},{24,0},{1,9},{9,17},{17,25},{25,1},{2,10},{10... | collective-permute-start | bytes 589832 | tf_op jit(solution)/shard_map/ppermute | solution.py:706
  896.1 27.7 %collective-permute-start.73 = (bf16[2,3,128,128]{3,2,1,0:T(8,128)(2,1)S(1)}, bf16[2,3,128,128]{3,2,1,0:T(8,128)(2,1)S(1)}, u32[]{:S(2)}, u32[]{:S(2)}) collective-permute-start(bf16[2,3,128,128]{3,2,1,0:T(8,128)(2,1)S(1)} %shard_map.377), channel_id=1, source_target_pairs={{0,16},{8,24},{16,0},{24,8},{1,17},{9,25},{17,1},{25,9},{2,18},{10... | collective-permute-start | bytes 589832 | tf_op jit(solution)/shard_map/ppermute | solution.py:706
  900.1 23.7 %collective-permute-start.74 = (bf16[2,3,128,128]{3,2,1,0:T(8,128)(2,1)S(1)}, bf16[2,3,128,128]{3,2,1,0:T(8,128)(2,1)S(1)}, u32[]{:S(2)}, u32[]{:S(2)}) collective-permute-start(bf16[2,3,128,128]{3,2,1,0:T(8,128)(2,1)S(1)} %shard_map.377), channel_id=1, source_target_pairs={{0,24},{8,0},{16,8},{24,16},{1,25},{9,1},{17,9},{25,17},{2,26},{10... | collective-permute-start | bytes 589832 | tf_op jit(solution)/shard_map/ppermute | solution.py:706
  924.1 28.7 %collective-permute-start.79 = (bf16[4,2,3,128,128]{4,3,2,0,1:T(8,128)(2,1)S(1)}, bf16[4,2,3,128,128]{4,3,2,0,1:T(8,128)(2,1)}, u32[]{:S(2)}, u32[]{:S(2)}) collective-permute-start(bf16[4,2,3,128,128]{4,3,2,0,1:T(8,128)(2,1)S(1)} %bitcast_dynamic-update-slice_fusion.38), channel_id=1, source_target_pairs={{0,4},{4,0},{1,5},{5,1},{2,6},{6,2},{3,7},{7,3},{8,12},{12,8},{9,1... | collective-permute-start | bytes 2359304 | tf_op jit(solution)/shard_map/ppermute | solution.py:706
  952.8 24.8 %collective-permute-start.81 = (bf16[2,3,128,128]{3,2,1,0:T(8,128)(2,1)S(1)}, bf16[2,3,128,128]{3,2,1,0:T(8,128)(2,1)S(1)}, u32[]{:S(2)}, u32[]{:S(2)}) collective-permute-start(bf16[2,3,128,128]{3,2,1,0:T(8,128)(2,1)S(1)} %pad_maximum_fusion.9), channel_id=1, source_target_pairs={{0,8},{8,16},{16,24},{24,0},{1,9},{9,17},{17,25},{25,1},{2,10},{10... | collective-permute-start | bytes 589832 | tf_op jit(solution)/shard_map/ppermute | solution.py:706
  957.5 20.1 %collective-permute-start.82 = (bf16[2,3,128,128]{3,2,1,0:T(8,128)(2,1)S(1)}, bf16[2,3,128,128]{3,2,1,0:T(8,128)(2,1)S(1)}, u32[]{:S(2)}, u32[]{:S(2)}) collective-permute-start(bf16[2,3,128,128]{3,2,1,0:T(8,128)(2,1)S(1)} %pad_maximum_fusion.9), channel_id=1, source_target_pairs={{0,16},{8,24},{16,0},{24,8},{1,17},{9,25},{17,1},{25,9},{2,18},{10... | collective-permute-start | bytes 589832 | tf_op jit(solution)/shard_map/ppermute | solution.py:706
  (171 other events, 1793.5 us)
Sparse Core Ops, SparseCore 0:
  120.7 84.6 all-gather.3
  207.8 66.8 all-gather.5
  277.2 66.8 all-gather.7
  480.3 77.8 reduce-scatter.3
  561.2 70.9 reduce-scatter.5
  644.0 110.8 reduce-scatter.7

commit v3 on v2

--- a/solution.py
+++ b/solution.py
@@ -608,6 +608,18 @@
     )(*operands)
 
 
+def join_body(*refs):
+    start = 0
+    for ref in refs[:-1]:
+        refs[-1][:, start : start + ref.shape[1]] = ref[...]
+        start += ref.shape[1]
+
+
+def joined(pieces):
+    shape = (pieces[0].shape[0], sum(v.shape[1] for v in pieces))
+    return whole_call(join_body, jax.ShapeDtypeStruct(shape, pieces[0].dtype), *pieces)
+
+
 def fence(*values):
     return lax.optimization_barrier(values)
 
@@ -637,7 +649,7 @@
         self.later = {"up": up, "down": down}
         return (
             self.attn_rows(normed),
-            self.gather_dp(mixed),
+            self.gather_dp(jnp.concatenate(mixed, axis=1)),
             self.gather_dp(out),
             self.gather_dp(gate)[None],
         )
@@ -753,7 +765,7 @@
         return lax.rem(self.z + distance, self.depth)
 
     def open(self, normed, mixed, out, gate, up, down, moments):
-        attn = jnp.concatenate([mixed, out], axis=1)
+        attn = joined((*mixed, out))
         line = [attn, shift(attn, "z", 1)]
         across = [shift(attn, "x", 1)]
         over = shift(normed, "y", 1)
@@ -782,12 +794,13 @@
         )
         self.up_sent, self.down_sent, self.moments = up_sent, down_sent, moments
 
-        mixed_cols = mixed.shape[1]
+        mixed_cols = attn.shape[1] - out.shape[1]
         full = jnp.zeros((2, self.depth) + attn.shape, attn.dtype)
         for k in range(self.depth):
             full = place(full, line[k], self.x, self.back(k))
             full = place(full, across[k], 1 - self.x, self.back(k))
-        full, gate_column = fence(full.reshape((-1,) + attn.shape[1:]), self.column(gate_arrived))
+        gate_column = self.column(gate_arrived)
+        full, gate_column = fence(full.reshape((-1,) + attn.shape[1:]), gate_column)
         return (
             self.order_rows(normed, over, pair),
             full[:, :mixed_cols],
@@ -1128,7 +1141,7 @@
     normalized_input, inverse_in = norm_forward(inputs, norm_gains[0])
     normed_full, mixed_full, out_full, gate_full = ways.open(
         normalized_input.astype(jnp.bfloat16),
-        jnp.concatenate([query_weight, key_matrix, value_matrix], axis=1),
+        (query_weight, key_matrix, value_matrix),
         out_weight,
         gate_weight,
         up_weight,

time: 1040 us -> 1040 us (level)
    unnamed x302 -> x305, local copies, waits for them, and re-layouts: 58.2 us -> 57 us
  transfers between devices with their start and end apart: 99 -> 99, of which waited for: 42 -> 42; matrix products, arithmetic and copies ran while one was open for 22% -> 21% of each run, Pallas kernels for 13% -> 13%
where the time goes in v3:
time: 1040 us; the launch traced here: 1030 us
  waiting for transfers between devices  343 us (33%)
  starting transfers between devices  226 us (22%)
  local copies, waits for them, and re-layouts  173 us (17%)
  Pallas kernels  171 us (16%)
  other arithmetic  69.5 us (7%)
  matrix products  28.9 us (3%)
  between operations  17 us (2%)
    ppermute x93, waiting for transfers between devices, shift(): lax.ppermute(values, axis, [(i, (i + distance) % size) for i in range(siz...  318 us
    ppermute x93, starting transfers between devices, shift(): lax.ppermute(values, axis, [(i, (i + distance) % size) for i in range(siz...  226 us
    pallas_call x9, Pallas kernels, dense_call(): pl.pallas_call(body, grid=grid, in_specs=in_specs, out_specs=out_specs, o...  102 us
    unnamed x305, local copies, waits for them, and re-layouts  57 us
    dynamic_update_slice x48, local copies, waits for them, and re-layouts, place(): lax.dynamic_update_slice(buffer, fresh, tuple(index) + (zero,) * values.n...  34.2 us
    all_gather x3, waiting for transfers between devices, gather_plane(): full = lax.all_gather(column, ('y', 'x'), axis=0, tiled=True)  25 us
    pallas_call x10, Pallas kernels, apply_factor(): pl.pallas_call(apply_body, grid=(high - low,), in_specs=[block, pl.BlockS...  21.8 us
  transfers between devices with their start and end apart: 99, of which 42 were waited for; matrix products, arithmetic and copies ran while one was open for 21% of the time, Pallas kernels for 13%

profile of v3, /device:TPU:0, one launch (start us, length us, event | category | flops | bytes accessed | tf_op | source)
XLA Modules:
  0.0 1027.9 jit_solution(17980387324592474163)
XLA Ops:
  22.0 12.6 %collective-permute-done.2 = bf16[128,2304]{1,0:T(8,128)(2,1)} collective-permute-done((bf16[128,2304]{1,0:T(8,128)(2,1)}, bf16[128,2304]{1,0:T(8,128)(2,1)}, u32[]{:S(2)}, u32[]{:S(2)}) %collective-permute-start.2) | collective-permute-done | bytes 589856 | tf_op jit(solution)/shard_map/ppermute | solution.py:718
  43.9 4.8 fusion.27
  67.4 4.8 fusion.23
  93.3 4.8 fusion.19
  105.5 5.4 collective-permute-done.10
  121.6 7.9 collective-permute-start.12
  132.0 6.7 fusion.3.refs_0_
  138.8 4.6 shard_map.362
  143.3 5.9 fusion.8
  164.2 8.1 collective-permute-start.17
  175.8 15.7 %collective-permute-done.16 = bf16[128,2304]{1,0:T(8,128)(2,1)} collective-permute-done((bf16[128,2304]{1,0:T(8,128)(2,1)}, bf16[128,2304]{1,0:T(8,128)(2,1)}, u32[]{:S(2)}, u32[]{:S(2)}) %collective-permute-start.16) | collective-permute-done | bytes 589856 | tf_op jit(solution)/shard_map/ppermute | solution.py:718
  193.1 6.9 collective-permute-done.18
  206.5 8.4 collective-permute-start.20
  228.8 9.8 fusion.15
  249.2 5.3 constant_dynamic-slice_fusion.14
  265.5 8.6 collective-permute-start.25
  283.1 22.1 %shard_map.363 = (bf16[2,1024,576]{2,1,0:T(8,128)(2,1)S(1)}, bf16[2,1024,576]{2,1,0:T(8,128)(2,1)}, bf16[2,1024,576]{2,1,0:T(8,128)(2,1)}) custom-call(bf16[1024,2304]{1,0:T(8,128)(2,1)} %constant_dynamic-update-slice_fusion.3.rows_ref.left_ref, bf16[2,2304,576]{2,1,0:T(8,128)(2,1)} %bitcast.378, bf16[2,2304,576]{2,1,0:T(8,128)(2,1)} %bitcast.381), custom_call_target="tpu_custom_call" | custom-call | flops 1024 | bytes 1024 | tf_op jit(solution)/shard_map/pallas_call | solution.py:397
  306.7 9.6 collective-permute-done.26
  316.3 24.9 %all-gather.8.cloned.1.call-done = bf16[16,288,576]{2,1,0:T(8,128)(2,1)} async-done(((bf16[4,288,576]{2,1,0:T(8,128)(2,1)}), bf16[16,288,576]{2,1,0:T(8,128)(2,1)}) %all-gather.8.cloned.1.call-update) | async-done | bytes 5308432 | tf_op jit(solution)/shard_map/all_gather | solution.py:881
  341.2 6.4 shard_map.364
  347.7 6.4 shard_map.365
  371.2 5.8 collective-permute-done.31
  377.1 24.8 %collective-permute-done.30 = bf16[128,2304]{1,0:T(8,128)(2,1)} collective-permute-done((bf16[128,2304]{1,0:T(8,128)(2,1)}, bf16[128,2304]{1,0:T(8,128)(2,1)}, u32[]{:S(2)}, u32[]{:S(2)}) %collective-permute-start.30) | collective-permute-done | bytes 589856 | tf_op jit(solution)/shard_map/ppermute | solution.py:718
  405.8 13.2 %collective-permute-start.32 = (bf16[128,2304]{1,0:T(8,128)(2,1)S(1)}, bf16[128,2304]{1,0:T(8,128)(2,1)S(1)}, u32[]{:S(2)}, u32[]{:S(2)}) collective-permute-start(bf16[128,2304]{1,0:T(8,128)(2,1)S(1)} %get-tuple-element.643), channel_id=1, source_target_pairs={{0,8},{8,16},{16,24},{24,0},{1,9},{9,17},{17,25},{25,1},{2,10},{10... | collective-permute-start | bytes 1769480 | tf_op jit(solution)/shard_map/ppermute | solution.py:718
  421.4 12.8 %collective-permute-done.32 = bf16[128,2304]{1,0:T(8,128)(2,1)S(1)} collective-permute-done((bf16[128,2304]{1,0:T(8,128)(2,1)S(1)}, bf16[128,2304]{1,0:T(8,128)(2,1)S(1)}, u32[]{:S(2)}, u32[]{:S(2)}) %collective-permute-start.32) | collective-permute-done | bytes 589856 | tf_op jit(solution)/shard_map/ppermute | solution.py:718
  434.2 24.3 %collective-permute-done.33 = bf16[128,2304]{1,0:T(8,128)(2,1)S(1)} collective-permute-done((bf16[128,2304]{1,0:T(8,128)(2,1)S(1)}, bf16[128,2304]{1,0:T(8,128)(2,1)S(1)}, u32[]{:S(2)}, u32[]{:S(2)}) %collective-permute-start.33) | collective-permute-done | bytes 589856 | tf_op jit(solution)/shard_map/ppermute | solution.py:718
  466.5 10.8 %shard_map.366 = bf16[2,2304,576]{2,1,0:T(8,128)(2,1)} custom-call(bf16[1024,2304]{1,0:T(8,128)(2,1)} %copy-done.66, bf16[2,1024,576]{2,1,0:T(8,128)(2,1)S(1)} %copy-done.4), custom_call_target="tpu_custom_call" | custom-call | flops 1024 | bytes 1024 | tf_op jit(solution)/shard_map/pallas_call | solution.py:397
  477.6 12.7 %shard_map.367 = (bf16[2,1024,576]{2,1,0:T(8,128)(2,1)S(1)}, bf16[2,1024,576]{2,1,0:T(8,128)(2,1)}) custom-call(bf16[1024,2304]{1,0:T(8,128)(2,1)} %copy-done.66, bf16[2,2304,576]{2,1,0:T(8,128)(2,1)} %bitcast.386, bf16[2,1024,576]{2,1,0:T(8,128)(2,1)} %get-tuple-element.373.gelu_ref, bf16[2,1024,576]{2,1,0:T(8,128)(2,1)} %get-tuple-element.374.pull_ref), custom_call_target="tpu_custom_call" | custom-call | flops 1024 | bytes 1024 | tf_op jit(solution)/shard_map/pallas_call | solution.py:397
  491.8 11.0 %shard_map.368 = bf16[512,2304]{1,0:T(8,128)(2,1)S(1)} custom-call(bf16[2,1024,576]{2,1,0:T(8,128)(2,1)} %copy-done.1, bf16[2,1024,576]{2,1,0:T(8,128)(2,1)} %get-tuple-element.378.refs_1_.right_ref, bf16[2,2304,576]{2,1,0:T(8,128)(2,1)} %bitcast.379, bf16[2,2304,576]{2,1,0:T(8,128)(2,1)} %bitcast.382), custom_call_target="tpu_custom_call" | custom-call | flops 1024 | bytes 1024 | tf_op jit(solution)/shard_map/pallas_call | solution.py:397
  503.0 11.0 %shard_map.369 = bf16[512,2304]{1,0:T(8,128)(2,1)S(1)} custom-call(bf16[2,1024,576]{2,1,0:T(8,128)(2,1)} %copy-done.1, bf16[2,1024,576]{2,1,0:T(8,128)(2,1)} %get-tuple-element.378.refs_1_.right_ref, bf16[2,2304,576]{2,1,0:T(8,128)(2,1)} %bitcast.380, bf16[2,2304,576]{2,1,0:T(8,128)(2,1)} %bitcast.383), custom_call_target="tpu_custom_call" | custom-call | flops 1024 | bytes 1024 | tf_op jit(solution)/shard_map/pallas_call | solution.py:397
  520.1 10.8 %shard_map.371 = bf16[2,2304,576]{2,1,0:T(8,128)(2,1)} custom-call(bf16[1024,2304]{1,0:T(8,128)(2,1)} %constant_dynamic-update-slice_fusion.3.rows_ref.left_ref, bf16[2,1024,576]{2,1,0:T(8,128)(2,1)S(1)} %copy-done.2), custom_call_target="tpu_custom_call" | custom-call | flops 1024 | bytes 1024 | tf_op jit(solution)/shard_map/pallas_call | solution.py:397
  531.0 13.5 %collective-permute-start.40 = (bf16[128,2304]{1,0:T(8,128)(2,1)}, bf16[128,2304]{1,0:T(8,128)(2,1)S(1)}, u32[]{:S(2)}, u32[]{:S(2)}) collective-permute-start(bf16[128,2304]{1,0:T(8,128)(2,1)} %get-tuple-element.382), channel_id=1, source_target_pairs={{0,8},{8,16},{16,24},{24,0},{1,9},{9,17},{17,25},{25,1},{2,10},{10... | collective-permute-start | bytes 1769480 | tf_op jit(solution)/shard_map/ppermute | solution.py:718
  547.0 13.4 %collective-permute-done.40 = bf16[128,2304]{1,0:T(8,128)(2,1)S(1)} collective-permute-done((bf16[128,2304]{1,0:T(8,128)(2,1)}, bf16[128,2304]{1,0:T(8,128)(2,1)S(1)}, u32[]{:S(2)}, u32[]{:S(2)}) %collective-permute-start.40) | collective-permute-done | bytes 589856 | tf_op jit(solution)/shard_map/ppermute | solution.py:718
  560.3 24.7 %collective-permute-done.39 = bf16[128,2304]{1,0:T(8,128)(2,1)S(1)} collective-permute-done((bf16[128,2304]{1,0:T(8,128)(2,1)}, bf16[128,2304]{1,0:T(8,128)(2,1)S(1)}, u32[]{:S(2)}, u32[]{:S(2)}) %collective-permute-start.39) | collective-permute-done | bytes 589856 | tf_op jit(solution)/shard_map/ppermute | solution.py:718
  590.6 13.1 %collective-permute-start.42 = (bf16[288,512]{1,0:T(8,128)(2,1)S(1)}, bf16[288,512]{1,0:T(8,128)(2,1)S(1)}, u32[]{:S(2)}, u32[]{:S(2)}) collective-permute-start(bf16[288,512]{1,0:T(8,128)(2,1)S(1)} %bitcast.444), channel_id=1, source_target_pairs={{0,8},{8,16},{16,24},{24,0},{1,9},{9,17},{17,25},{25,1},{2,10},{10... | collective-permute-start | bytes 884744 | tf_op jit(solution)/shard_map/ppermute | solution.py:718
  606.5 5.8 collective-permute-done.42
  612.3 11.2 %collective-permute-done.43 = bf16[288,512]{1,0:T(8,128)(2,1)S(1)} collective-permute-done((bf16[288,512]{1,0:T(8,128)(2,1)S(1)}, bf16[288,512]{1,0:T(8,128)(2,1)S(1)}, u32[]{:S(2)}, u32[]{:S(2)}) %collective-permute-start.43) | collective-permute-done | bytes 294944 | tf_op jit(solution)/shard_map/ppermute | solution.py:718
  630.2 10.8 %shard_map.374 = bf16[2,2304,576]{2,1,0:T(8,128)(2,1)} custom-call(bf16[1024,2304]{1,0:T(8,128)(2,1)} %constant_dynamic-update-slice_fusion.3.rows_ref.left_ref, bf16[2,1024,576]{2,1,0:T(8,128)(2,1)S(1)} %copy-done), custom_call_target="tpu_custom_call" | custom-call | flops 1024 | bytes 1024 | tf_op jit(solution)/shard_map/pallas_call | solution.py:397
  645.0 4.4 shard_map.370
  657.2 6.7 fusion.1
  663.9 6.3 collective-permute-start.47
  672.6 4.3 convolution_convert_fusion
  676.9 4.3 collective-permute-done.47.refs_1_
  681.9 14.2 %collective-permute-done.48.refs_2_ = bf16[288,576]{1,0:T(8,128)(2,1)S(1)} collective-permute-done((bf16[288,576]{1,0:T(8,128)(2,1)S(1)}, bf16[288,576]{1,0:T(8,128)(2,1)S(1)}, u32[]{:S(2)}, u32[]{:S(2)}) %collective-permute-start.48) | collective-permute-done | bytes 331808 | tf_op jit(solution)/shard_map/ppermute | solution.py:718
  697.7 12.2 %collective-permute-done.46 = bf16[1152,512]{1,0:T(8,128)(2,1)} collective-permute-done((bf16[1152,512]{1,0:T(8,128)(2,1)S(1)}, bf16[1152,512]{1,0:T(8,128)(2,1)}, u32[]{:S(2)}, u32[]{:S(2)}) %collective-permute-start.46) | collective-permute-done | bytes 1179680 | tf_op jit(solution)/shard_map/ppermute | solution.py:718
  735.7 11.3 %collective-permute-start.54 = (bf16[288,576]{1,0:T(8,128)(2,1)}, bf16[288,576]{1,0:T(8,128)(2,1)S(1)}, u32[]{:S(2)}, u32[]{:S(2)}) collective-permute-start(bf16[288,576]{1,0:T(8,128)(2,1)} %get-tuple-element.415), channel_id=1, source_target_pairs={{0,8},{8,16},{16,24},{24,0},{1,9},{9,17},{17,25},{25,1},{2,10},{10... | collective-permute-start | bytes 995336 | tf_op jit(solution)/shard_map/ppermute | solution.py:718
  749.5 9.1 collective-permute-start.56
  762.7 15.5 %collective-permute-done.55.refs_2_ = bf16[288,576]{1,0:T(8,128)(2,1)S(1)} collective-permute-done((bf16[288,576]{1,0:T(8,128)(2,1)}, bf16[288,576]{1,0:T(8,128)(2,1)S(1)}, u32[]{:S(2)}, u32[]{:S(2)}) %collective-permute-start.55) | collective-permute-done | bytes 331808 | tf_op jit(solution)/shard_map/ppermute | solution.py:718
  778.2 7.8 collective-permute-done.56.refs_3_
  807.9 23.2 %collective-permute-done.59.refs_2_ = bf16[288,1024]{1,0:T(8,128)(2,1)} collective-permute-done((bf16[288,1024]{1,0:T(8,128)(2,1)}, bf16[288,1024]{1,0:T(8,128)(2,1)}, u32[]{:S(2)}, u32[]{:S(2)}) %collective-permute-start.59) | collective-permute-done | bytes 589856 | tf_op jit(solution)/shard_map/ppermute | solution.py:718
  831.3 4.4 shard_map.376
  837.3 13.0 %collective-permute-start.63 = (bf16[288,576]{1,0:T(8,128)(2,1)S(1)}, bf16[288,576]{1,0:T(8,128)(2,1)S(1)}, u32[]{:S(2)}, u32[]{:S(2)}) collective-permute-start(bf16[288,576]{1,0:T(8,128)(2,1)S(1)} %get-tuple-element.680), channel_id=1, source_target_pairs={{0,8},{8,16},{16,24},{24,0},{1,9},{9,17},{17,25},{25,1},{2,10},{10... | collective-permute-start | bytes 995336 | tf_op jit(solution)/shard_map/ppermute | solution.py:718
  855.4 6.6 shard_map.378
  865.0 9.6 collective-permute-done.64.refs_2_
  880.5 8.3 collective-permute-start.68
  900.2 12.3 %collective-permute-done.69.refs_2_ = f32[1,3,128,128]{3,2,1,0:T(8,128)S(1)} collective-permute-done((f32[1,3,128,128]{3,2,1,0:T(8,128)}, f32[1,3,128,128]{3,2,1,0:T(8,128)S(1)}, u32[]{:S(2)}, u32[]{:S(2)}) %collective-permute-start.69) | collective-permute-done | bytes 196640 | tf_op jit(solution)/shard_map/ppermute | solution.py:718
  913.2 4.2 shard_map.381
  932.6 4.8 collective-permute-start.76
  942.0 4.2 shard_map.382
  949.9 4.7 collective-permute-start.81
  961.3 4.6 shard_map.388.refs_0_
  965.9 4.6 shard_map.392.refs_0_
  970.5 4.2 shard_map.383
  1012.3 4.6 shard_map.390.refs_0_
  (687 shorter events, 382.0 us)
Async XLA Ops:
  7.2 275.9 %all-gather.4.cloned.1.call-start = ((), (), s32[]{:S(2)}) async-start(), calls=%async_computation.3 | async-start | bytes 7372800 | tf_op jit(solution)/shard_map/all_gather | solution.py:881
  11.1 23.6 %collective-permute-start = (bf16[288,1536]{1,0:T(8,128)(2,1)S(1)}, bf16[288,1536]{1,0:T(8,128)(2,1)}, u32[]{:S(2)}, u32[]{:S(2)}) collective-permute-start(bf16[288,1536]{1,0:T(8,128)(2,1)S(1)} %shard_map.361), channel_id=1, source_target_pairs={{0,4},{4,0},{1,5},{5,1},{2,6},{6,2},{3,7},{7,3},{8,12},{12,8},{9,1... | collective-permute-start | bytes 2654216 | tf_op jit(solution)/shard_map/ppermute | solution.py:718
  14.1 23.1 %collective-permute-start.1 = (bf16[288,1536]{1,0:T(8,128)(2,1)S(1)}, bf16[288,1536]{1,0:T(8,128)(2,1)}, u32[]{:S(2)}, u32[]{:S(2)}) collective-permute-start(bf16[288,1536]{1,0:T(8,128)(2,1)S(1)} %shard_map.361), channel_id=1, source_target_pairs={{0,8},{8,16},{16,24},{24,0},{1,9},{9,17},{17,25},{25,1},{2,10},{10... | collective-permute-start | bytes 2654216 | tf_op jit(solution)/shard_map/ppermute | solution.py:718
  37.1 20.6 %collective-permute-start.3 = (bf16[288,1536]{1,0:T(8,128)(2,1)}, bf16[288,1536]{1,0:T(8,128)(2,1)}, u32[]{:S(2)}, u32[]{:S(2)}) collective-permute-start(bf16[288,1536]{1,0:T(8,128)(2,1)} %collective-permute-done.1), channel_id=1, source_target_pairs={{0,4},{4,0},{1,5},{5,1},{2,6},{6,2},{3,7},{7,3},{8,12},{12,8},{9,1... | collective-permute-start | bytes 2654216 | tf_op jit(solution)/shard_map/ppermute | solution.py:718
  37.7 22.4 %collective-permute-start.4 = (bf16[288,1536]{1,0:T(8,128)(2,1)}, bf16[288,1536]{1,0:T(8,128)(2,1)}, u32[]{:S(2)}, u32[]{:S(2)}) collective-permute-start(bf16[288,1536]{1,0:T(8,128)(2,1)} %collective-permute-done.1), channel_id=1, source_target_pairs={{0,8},{8,16},{16,24},{24,0},{1,9},{9,17},{17,25},{25,1},{2,10},{10... | collective-permute-start | bytes 2654216 | tf_op jit(solution)/shard_map/ppermute | solution.py:718
  60.0 19.7 %collective-permute-start.6 = (bf16[288,1536]{1,0:T(8,128)(2,1)}, bf16[288,1536]{1,0:T(8,128)(2,1)}, u32[]{:S(2)}, u32[]{:S(2)}) collective-permute-start(bf16[288,1536]{1,0:T(8,128)(2,1)} %collective-permute-done.4), channel_id=1, source_target_pairs={{0,4},{4,0},{1,5},{5,1},{2,6},{6,2},{3,7},{7,3},{8,12},{12,8},{9,1... | collective-permute-start | bytes 2654216 | tf_op jit(solution)/shard_map/ppermute | solution.py:718
  61.3 20.9 %collective-permute-start.7 = (bf16[288,1536]{1,0:T(8,128)(2,1)}, bf16[288,1536]{1,0:T(8,128)(2,1)}, u32[]{:S(2)}, u32[]{:S(2)}) collective-permute-start(bf16[288,1536]{1,0:T(8,128)(2,1)} %collective-permute-done.4), channel_id=1, source_target_pairs={{0,8},{8,16},{16,24},{24,0},{1,9},{9,17},{17,25},{25,1},{2,10},{10... | collective-permute-start | bytes 2654216 | tf_op jit(solution)/shard_map/ppermute | solution.py:718
  85.0 26.0 %collective-permute-start.8 = (bf16[288,1536]{1,0:T(8,128)(2,1)}, bf16[288,1536]{1,0:T(8,128)(2,1)}, u32[]{:S(2)}, u32[]{:S(2)}) collective-permute-start(bf16[288,1536]{1,0:T(8,128)(2,1)} %collective-permute-done.7), channel_id=1, source_target_pairs={{0,4},{4,0},{1,5},{5,1},{2,6},{6,2},{3,7},{7,3},{8,12},{12,8},{9,1... | collective-permute-start | bytes 2654216 | tf_op jit(solution)/shard_map/ppermute | solution.py:718
  86.0 24.9 %collective-permute-start.10 = (bf16[288,576]{1,0:T(8,128)(2,1)}, bf16[288,576]{1,0:T(8,128)(2,1)}, u32[]{:S(2)}, u32[]{:S(2)}) collective-permute-start(bf16[288,576]{1,0:T(8,128)(2,1)} %bitcast.349), channel_id=1, source_target_pairs={{0,16},{8,24},{16,0},{24,8},{1,17},{9,25},{17,1},{25,9},{2,18},{10... | collective-permute-start | bytes 995336 | tf_op jit(solution)/shard_map/ppermute | solution.py:718
  87.7 23.2 %collective-permute-start.11 = (bf16[288,576]{1,0:T(8,128)(2,1)}, bf16[288,576]{1,0:T(8,128)(2,1)}, u32[]{:S(2)}, u32[]{:S(2)}) collective-permute-start(bf16[288,576]{1,0:T(8,128)(2,1)} %bitcast.348), channel_id=1, source_target_pairs={{0,24},{8,0},{16,8},{24,16},{1,25},{9,1},{17,9},{25,17},{2,26},{10... | collective-permute-start | bytes 995336 | tf_op jit(solution)/shard_map/ppermute | solution.py:718
  117.6 165.4 %all-gather.6.cloned.1.call-start = ((), (), s32[]{:S(2)}) async-start(), calls=%async_computation.4 | async-start | bytes 7372800 | tf_op jit(solution)/shard_map/all_gather | solution.py:881
  121.6 27.6 %collective-permute-start.12 = (bf16[288,576]{1,0:T(8,128)(2,1)S(1)}, bf16[288,576]{1,0:T(8,128)(2,1)S(1)}, u32[]{:S(2)}, u32[]{:S(2)}) collective-permute-start(bf16[288,576]{1,0:T(8,128)(2,1)S(1)} %bitcast.441), channel_id=1, source_target_pairs={{0,8},{8,16},{16,24},{24,0},{1,9},{9,17},{17,25},{25,1},{2,10},{10... | collective-permute-start | bytes 995336 | tf_op jit(solution)/shard_map/ppermute | solution.py:718
  129.5 21.8 %collective-permute-start.13 = (bf16[288,576]{1,0:T(8,128)(2,1)S(1)}, bf16[288,576]{1,0:T(8,128)(2,1)S(1)}, u32[]{:S(2)}, u32[]{:S(2)}) collective-permute-start(bf16[288,576]{1,0:T(8,128)(2,1)S(1)} %bitcast.440), channel_id=1, source_target_pairs={{0,16},{8,24},{16,0},{24,8},{1,17},{9,25},{17,1},{25,9},{2,18},{10... | collective-permute-start | bytes 995336 | tf_op jit(solution)/shard_map/ppermute | solution.py:718
  129.8 23.1 %collective-permute-start.14 = (bf16[288,576]{1,0:T(8,128)(2,1)S(1)}, bf16[288,576]{1,0:T(8,128)(2,1)S(1)}, u32[]{:S(2)}, u32[]{:S(2)}) collective-permute-start(bf16[288,576]{1,0:T(8,128)(2,1)S(1)} %bitcast.439), channel_id=1, source_target_pairs={{0,24},{8,0},{16,8},{24,16},{1,25},{9,1},{17,9},{25,17},{2,26},{10... | collective-permute-start | bytes 995336 | tf_op jit(solution)/shard_map/ppermute | solution.py:718
  154.5 186.8 %all-gather.8.cloned.1.call-start = ((), (), s32[]{:S(2)}) async-start(), calls=%async_computation.5 | async-start | bytes 7372800 | tf_op jit(solution)/shard_map/all_gather | solution.py:881
  162.6 28.8 %collective-permute-start.16 = (bf16[128,2304]{1,0:T(8,128)(2,1)}, bf16[128,2304]{1,0:T(8,128)(2,1)}, u32[]{:S(2)}, u32[]{:S(2)}) collective-permute-start(bf16[128,2304]{1,0:T(8,128)(2,1)} %fusion.31), channel_id=1, source_target_pairs={{0,2},{2,0},{1,3},{3,1},{4,6},{6,4},{5,7},{7,5},{8,10},{10,8},{9,1... | collective-permute-start | bytes 1769480 | tf_op jit(solution)/shard_map/ppermute | solution.py:718
  164.2 28.8 %collective-permute-start.17 = (bf16[288,576]{1,0:T(8,128)(2,1)}, bf16[288,576]{1,0:T(8,128)(2,1)S(1)}, u32[]{:S(2)}, u32[]{:S(2)}) collective-permute-start(bf16[288,576]{1,0:T(8,128)(2,1)} %bitcast.438), channel_id=1, source_target_pairs={{0,8},{8,16},{16,24},{24,0},{1,9},{9,17},{17,25},{25,1},{2,10},{10... | collective-permute-start | bytes 995336 | tf_op jit(solution)/shard_map/ppermute | solution.py:718
  172.4 27.6 %collective-permute-start.18 = (bf16[288,576]{1,0:T(8,128)(2,1)}, bf16[288,576]{1,0:T(8,128)(2,1)S(1)}, u32[]{:S(2)}, u32[]{:S(2)}) collective-permute-start(bf16[288,576]{1,0:T(8,128)(2,1)} %bitcast.437), channel_id=1, source_target_pairs={{0,16},{8,24},{16,0},{24,8},{1,17},{9,25},{17,1},{25,9},{2,18},{10... | collective-permute-start | bytes 995336 | tf_op jit(solution)/shard_map/ppermute | solution.py:718
  175.8 24.2 %collective-permute-start.19 = (bf16[288,576]{1,0:T(8,128)(2,1)}, bf16[288,576]{1,0:T(8,128)(2,1)S(1)}, u32[]{:S(2)}, u32[]{:S(2)}) collective-permute-start(bf16[288,576]{1,0:T(8,128)(2,1)} %bitcast.436), channel_id=1, source_target_pairs={{0,24},{8,0},{16,8},{24,16},{1,25},{9,1},{17,9},{25,17},{2,26},{10... | collective-permute-start | bytes 995336 | tf_op jit(solution)/shard_map/ppermute | solution.py:718
  201.5 451.9 %reduce-scatter.4.cloned.1.call-start = ((), (), s32[]{:S(2)}) async-start(), calls=%async_computation.6 | async-start | bytes 7372800 | tf_op jit(solution)/shard_map/reduce_scatter | solution.py:917
  206.5 51.1 %collective-permute-start.20 = (bf16[128,2304]{1,0:T(8,128)(2,1)}, bf16[128,2304]{1,0:T(8,128)(2,1)}, u32[]{:S(2)}, u32[]{:S(2)}) collective-permute-start(bf16[128,2304]{1,0:T(8,128)(2,1)} %multiply_convert_fusion), channel_id=1, source_target_pairs={{0,8},{8,16},{16,24},{24,0},{1,9},{9,17},{17,25},{25,1},{2,10},{10... | collective-permute-start | bytes 1769480 | tf_op jit(solution)/shard_map/ppermute | solution.py:718
  214.8 42.7 %collective-permute-start.21 = (bf16[128,2304]{1,0:T(8,128)(2,1)}, bf16[128,2304]{1,0:T(8,128)(2,1)}, u32[]{:S(2)}, u32[]{:S(2)}) collective-permute-start(bf16[128,2304]{1,0:T(8,128)(2,1)} %multiply_convert_fusion), channel_id=1, source_target_pairs={{0,16},{8,24},{16,0},{24,8},{1,17},{9,25},{17,1},{25,9},{2,18},{10... | collective-permute-start | bytes 1769480 | tf_op jit(solution)/shard_map/ppermute | solution.py:718
  214.8 42.7 %collective-permute-start.22 = (bf16[128,2304]{1,0:T(8,128)(2,1)}, bf16[128,2304]{1,0:T(8,128)(2,1)}, u32[]{:S(2)}, u32[]{:S(2)}) collective-permute-start(bf16[128,2304]{1,0:T(8,128)(2,1)} %multiply_convert_fusion), channel_id=1, source_target_pairs={{0,24},{8,0},{16,8},{24,16},{1,25},{9,1},{17,9},{25,17},{2,26},{10... | collective-permute-start | bytes 1769480 | tf_op jit(solution)/shard_map/ppermute | solution.py:718
  265.5 41.2 %collective-permute-start.25 = (bf16[288,1024]{1,0:T(8,128)(2,1)}, bf16[288,1024]{1,0:T(8,128)(2,1)}, u32[]{:S(2)}, u32[]{:S(2)}) collective-permute-start(bf16[288,1024]{1,0:T(8,128)(2,1)} %bitcast.338), channel_id=1, source_target_pairs={{0,8},{8,16},{16,24},{24,0},{1,9},{9,17},{17,25},{25,1},{2,10},{10... | collective-permute-start | bytes 1769480 | tf_op jit(solution)/shard_map/ppermute | solution.py:718
  274.1 42.2 %collective-permute-start.26 = (bf16[288,1024]{1,0:T(8,128)(2,1)}, bf16[288,1024]{1,0:T(8,128)(2,1)}, u32[]{:S(2)}, u32[]{:S(2)}) collective-permute-start(bf16[288,1024]{1,0:T(8,128)(2,1)} %bitcast.337), channel_id=1, source_target_pairs={{0,16},{8,24},{16,0},{24,8},{1,17},{9,25},{17,1},{25,9},{2,18},{10... | collective-permute-start | bytes 1769480 | tf_op jit(solution)/shard_map/ppermute | solution.py:718
  277.4 38.9 %collective-permute-start.27 = (bf16[288,1024]{1,0:T(8,128)(2,1)}, bf16[288,1024]{1,0:T(8,128)(2,1)}, u32[]{:S(2)}, u32[]{:S(2)}) collective-permute-start(bf16[288,1024]{1,0:T(8,128)(2,1)} %bitcast.336), channel_id=1, source_target_pairs={{0,24},{8,0},{16,8},{24,16},{1,25},{9,1},{17,9},{25,17},{2,26},{10... | collective-permute-start | bytes 1769480 | tf_op jit(solution)/shard_map/ppermute | solution.py:718
  360.2 41.7 %collective-permute-start.30 = (bf16[128,2304]{1,0:T(8,128)(2,1)}, bf16[128,2304]{1,0:T(8,128)(2,1)}, u32[]{:S(2)}, u32[]{:S(2)}) collective-permute-start(bf16[128,2304]{1,0:T(8,128)(2,1)} %get-tuple-element.370), channel_id=1, source_target_pairs={{0,16},{8,24},{16,0},{24,8},{1,17},{9,25},{17,1},{25,9},{2,18},{10... | collective-permute-start | bytes 1769480 | tf_op jit(solution)/shard_map/ppermute | solution.py:718
  362.6 39.3 %collective-permute-start.29 = (bf16[128,2304]{1,0:T(8,128)(2,1)}, bf16[128,2304]{1,0:T(8,128)(2,1)}, u32[]{:S(2)}, u32[]{:S(2)}) collective-permute-start(bf16[128,2304]{1,0:T(8,128)(2,1)} %get-tuple-element.369), channel_id=1, source_target_pairs={{0,24},{8,0},{16,8},{24,16},{1,25},{9,1},{17,9},{25,17},{2,26},{10... | collective-permute-start | bytes 1769480 | tf_op jit(solution)/shard_map/ppermute | solution.py:718
  405.8 28.4 %collective-permute-start.32 = (bf16[128,2304]{1,0:T(8,128)(2,1)S(1)}, bf16[128,2304]{1,0:T(8,128)(2,1)S(1)}, u32[]{:S(2)}, u32[]{:S(2)}) collective-permute-start(bf16[128,2304]{1,0:T(8,128)(2,1)S(1)} %get-tuple-element.643), channel_id=1, source_target_pairs={{0,8},{8,16},{16,24},{24,0},{1,9},{9,17},{17,25},{25,1},{2,10},{10... | collective-permute-start | bytes 1769480 | tf_op jit(solution)/shard_map/ppermute | solution.py:718
  419.0 39.5 %collective-permute-start.33 = (bf16[128,2304]{1,0:T(8,128)(2,1)S(1)}, bf16[128,2304]{1,0:T(8,128)(2,1)S(1)}, u32[]{:S(2)}, u32[]{:S(2)}) collective-permute-start(bf16[128,2304]{1,0:T(8,128)(2,1)S(1)} %get-tuple-element.643), channel_id=1, source_target_pairs={{0,16},{8,24},{16,0},{24,8},{1,17},{9,25},{17,1},{25,9},{2,18},{10... | collective-permute-start | bytes 1769480 | tf_op jit(solution)/shard_map/ppermute | solution.py:718
  420.4 38.0 %collective-permute-start.34 = (bf16[128,2304]{1,0:T(8,128)(2,1)S(1)}, bf16[128,2304]{1,0:T(8,128)(2,1)S(1)}, u32[]{:S(2)}, u32[]{:S(2)}) collective-permute-start(bf16[128,2304]{1,0:T(8,128)(2,1)S(1)} %get-tuple-element.643), channel_id=1, source_target_pairs={{0,24},{8,0},{16,8},{24,16},{1,25},{9,1},{17,9},{25,17},{2,26},{10... | collective-permute-start | bytes 1769480 | tf_op jit(solution)/shard_map/ppermute | solution.py:718
  477.4 232.5 %reduce-scatter.6.cloned.1.call-start = ((), (), s32[]{:S(2)}) async-start(), calls=%async_computation.7 | async-start | bytes 7372800 | tf_op jit(solution)/shard_map/reduce_scatter | solution.py:917
  530.9 277.0 %reduce-scatter.8.cloned.1.call-start = ((), (), s32[]{:S(2)}) async-start(), calls=%async_computation.8 | async-start | bytes 7372800 | tf_op jit(solution)/shard_map/reduce_scatter | solution.py:917
  531.0 29.3 %collective-permute-start.40 = (bf16[128,2304]{1,0:T(8,128)(2,1)}, bf16[128,2304]{1,0:T(8,128)(2,1)S(1)}, u32[]{:S(2)}, u32[]{:S(2)}) collective-permute-start(bf16[128,2304]{1,0:T(8,128)(2,1)} %get-tuple-element.382), channel_id=1, source_target_pairs={{0,8},{8,16},{16,24},{24,0},{1,9},{9,17},{17,25},{25,1},{2,10},{10... | collective-permute-start | bytes 1769480 | tf_op jit(solution)/shard_map/ppermute | solution.py:718
  544.5 40.6 %collective-permute-start.39 = (bf16[128,2304]{1,0:T(8,128)(2,1)}, bf16[128,2304]{1,0:T(8,128)(2,1)S(1)}, u32[]{:S(2)}, u32[]{:S(2)}) collective-permute-start(bf16[128,2304]{1,0:T(8,128)(2,1)} %get-tuple-element.381), channel_id=1, source_target_pairs={{0,16},{8,24},{16,0},{24,8},{1,17},{9,25},{17,1},{25,9},{2,18},{10... | collective-permute-start | bytes 1769480 | tf_op jit(solution)/shard_map/ppermute | solution.py:718
  546.4 38.7 %collective-permute-start.38 = (bf16[128,2304]{1,0:T(8,128)(2,1)}, bf16[128,2304]{1,0:T(8,128)(2,1)S(1)}, u32[]{:S(2)}, u32[]{:S(2)}) collective-permute-start(bf16[128,2304]{1,0:T(8,128)(2,1)} %get-tuple-element.380), channel_id=1, source_target_pairs={{0,24},{8,0},{16,8},{24,16},{1,25},{9,1},{17,9},{25,17},{2,26},{10... | collective-permute-start | bytes 1769480 | tf_op jit(solution)/shard_map/ppermute | solution.py:718
  589.1 34.4 %collective-permute-start.41 = (bf16[128,2304]{1,0:T(8,128)(2,1)S(1)}, bf16[128,2304]{1,0:T(8,128)(2,1)S(1)}, u32[]{:S(2)}, u32[]{:S(2)}) collective-permute-start(bf16[128,2304]{1,0:T(8,128)(2,1)S(1)} %subtract_convert_fusion), channel_id=1, source_target_pairs={{0,2},{2,0},{1,3},{3,1},{4,6},{6,4},{5,7},{7,5},{8,10},{10,8},{9,1... | collective-permute-start | bytes 1769480 | tf_op jit(solution)/shard_map/ppermute | solution.py:718
  590.6 21.7 %collective-permute-start.42 = (bf16[288,512]{1,0:T(8,128)(2,1)S(1)}, bf16[288,512]{1,0:T(8,128)(2,1)S(1)}, u32[]{:S(2)}, u32[]{:S(2)}) collective-permute-start(bf16[288,512]{1,0:T(8,128)(2,1)S(1)} %bitcast.444), channel_id=1, source_target_pairs={{0,8},{8,16},{16,24},{24,0},{1,9},{9,17},{17,25},{25,1},{2,10},{10... | collective-permute-start | bytes 884744 | tf_op jit(solution)/shard_map/ppermute | solution.py:718
  603.7 19.8 %collective-permute-start.43 = (bf16[288,512]{1,0:T(8,128)(2,1)S(1)}, bf16[288,512]{1,0:T(8,128)(2,1)S(1)}, u32[]{:S(2)}, u32[]{:S(2)}) collective-permute-start(bf16[288,512]{1,0:T(8,128)(2,1)S(1)} %bitcast.443), channel_id=1, source_target_pairs={{0,16},{8,24},{16,0},{24,8},{1,17},{9,25},{17,1},{25,9},{2,18},{10... | collective-permute-start | bytes 884744 | tf_op jit(solution)/shard_map/ppermute | solution.py:718
  655.8 54.0 %collective-permute-start.46 = (bf16[1152,512]{1,0:T(8,128)(2,1)S(1)}, bf16[1152,512]{1,0:T(8,128)(2,1)}, u32[]{:S(2)}, u32[]{:S(2)}) collective-permute-start(bf16[1152,512]{1,0:T(8,128)(2,1)S(1)} %copy-done.97), channel_id=1, source_target_pairs={{0,4},{4,0},{1,5},{5,1},{2,6},{6,2},{3,7},{7,3},{8,12},{12,8},{9,1... | collective-permute-start | bytes 3538952 | tf_op jit(solution)/shard_map/ppermute | solution.py:718
  670.2 26.0 %collective-permute-start.48 = (bf16[288,576]{1,0:T(8,128)(2,1)S(1)}, bf16[288,576]{1,0:T(8,128)(2,1)S(1)}, u32[]{:S(2)}, u32[]{:S(2)}) collective-permute-start(bf16[288,576]{1,0:T(8,128)(2,1)S(1)} %get-tuple-element.402), channel_id=1, source_target_pairs={{0,16},{8,24},{16,0},{24,8},{1,17},{9,25},{17,1},{25,9},{2,18},{10... | collective-permute-start | bytes 995336 | tf_op jit(solution)/shard_map/ppermute | solution.py:718
  672.2 24.7 %collective-permute-start.49 = (bf16[288,576]{1,0:T(8,128)(2,1)S(1)}, bf16[288,576]{1,0:T(8,128)(2,1)S(1)}, u32[]{:S(2)}, u32[]{:S(2)}) collective-permute-start(bf16[288,576]{1,0:T(8,128)(2,1)S(1)} %get-tuple-element.403), channel_id=1, source_target_pairs={{0,24},{8,0},{16,8},{24,16},{1,25},{9,1},{17,9},{25,17},{2,26},{10... | collective-permute-start | bytes 995336 | tf_op jit(solution)/shard_map/ppermute | solution.py:718
  718.6 67.5 %collective-permute-start.50 = (bf16[1152,1024]{1,0:T(8,128)(2,1)}, bf16[1152,1024]{1,0:T(8,128)(2,1)S(1)}, u32[]{:S(2)}, u32[]{:S(2)}) collective-permute-start(bf16[1152,1024]{1,0:T(8,128)(2,1)} %dynamic-slice_bitcast_fusion), channel_id=1, source_target_pairs={{0,4},{4,0},{1,5},{5,1},{2,6},{6,2},{3,7},{7,3},{8,12},{12,8},{9,1... | collective-permute-start | bytes 7077896 | tf_op jit(solution)/shard_map/ppermute | solution.py:718
  721.6 64.4 %collective-permute-start.57 = (bf16[2,128,2304]{2,1,0:T(8,128)(2,1)}, bf16[2,128,2304]{2,1,0:T(8,128)(2,1)}, u32[]{:S(2)}, u32[]{:S(2)}) collective-permute-start(bf16[2,128,2304]{2,1,0:T(8,128)(2,1)} %fusion.14), channel_id=1, source_target_pairs={{0,1},{1,0},{2,3},{3,2},{4,5},{5,4},{6,7},{7,6},{8,9},{9,8},{10,11... | collective-permute-start | bytes 3538952 | tf_op jit(solution)/shard_map/ppermute | solution.py:718
  725.9 22.5 %collective-permute-start.52 = (bf16[288,512]{1,0:T(8,128)(2,1)S(1)}, bf16[288,512]{1,0:T(8,128)(2,1)S(1)}, u32[]{:S(2)}, u32[]{:S(2)}) collective-permute-start(bf16[288,512]{1,0:T(8,128)(2,1)S(1)} %get-tuple-element.412), channel_id=1, source_target_pairs={{0,16},{8,24},{16,0},{24,8},{1,17},{9,25},{17,1},{25,9},{2,18},{10... | collective-permute-start | bytes 884744 | tf_op jit(solution)/shard_map/ppermute | solution.py:718
  728.3 21.2 %collective-permute-start.53 = (bf16[288,512]{1,0:T(8,128)(2,1)S(1)}, bf16[288,512]{1,0:T(8,128)(2,1)S(1)}, u32[]{:S(2)}, u32[]{:S(2)}) collective-permute-start(bf16[288,512]{1,0:T(8,128)(2,1)S(1)} %get-tuple-element.413), channel_id=1, source_target_pairs={{0,24},{8,0},{16,8},{24,16},{1,25},{9,1},{17,9},{25,17},{2,26},{10... | collective-permute-start | bytes 884744 | tf_op jit(solution)/shard_map/ppermute | solution.py:718
  735.7 27.0 %collective-permute-start.54 = (bf16[288,576]{1,0:T(8,128)(2,1)}, bf16[288,576]{1,0:T(8,128)(2,1)S(1)}, u32[]{:S(2)}, u32[]{:S(2)}) collective-permute-start(bf16[288,576]{1,0:T(8,128)(2,1)} %get-tuple-element.415), channel_id=1, source_target_pairs={{0,8},{8,16},{16,24},{24,0},{1,9},{9,17},{17,25},{25,1},{2,10},{10... | collective-permute-start | bytes 995336 | tf_op jit(solution)/shard_map/ppermute | solution.py:718
  748.4 29.8 %collective-permute-start.55 = (bf16[288,576]{1,0:T(8,128)(2,1)}, bf16[288,576]{1,0:T(8,128)(2,1)S(1)}, u32[]{:S(2)}, u32[]{:S(2)}) collective-permute-start(bf16[288,576]{1,0:T(8,128)(2,1)} %get-tuple-element.416), channel_id=1, source_target_pairs={{0,16},{8,24},{16,0},{24,8},{1,17},{9,25},{17,1},{25,9},{2,18},{10... | collective-permute-start | bytes 995336 | tf_op jit(solution)/shard_map/ppermute | solution.py:718
  749.5 36.5 %collective-permute-start.56 = (bf16[288,576]{1,0:T(8,128)(2,1)S(1)}, bf16[288,576]{1,0:T(8,128)(2,1)S(1)}, u32[]{:S(2)}, u32[]{:S(2)}) collective-permute-start(bf16[288,576]{1,0:T(8,128)(2,1)S(1)} %get-tuple-element.417), channel_id=1, source_target_pairs={{0,24},{8,0},{16,8},{24,16},{1,25},{9,1},{17,9},{25,17},{2,26},{10... | collective-permute-start | bytes 995336 | tf_op jit(solution)/shard_map/ppermute | solution.py:718
  790.0 41.2 %collective-permute-start.59 = (bf16[288,1024]{1,0:T(8,128)(2,1)}, bf16[288,1024]{1,0:T(8,128)(2,1)}, u32[]{:S(2)}, u32[]{:S(2)}) collective-permute-start(bf16[288,1024]{1,0:T(8,128)(2,1)} %get-tuple-element.655), channel_id=1, source_target_pairs={{0,16},{8,24},{16,0},{24,8},{1,17},{9,25},{17,1},{25,9},{2,18},{10... | collective-permute-start | bytes 1769480 | tf_op jit(solution)/shard_map/ppermute | solution.py:718
  792.4 38.8 %collective-permute-start.60 = (bf16[288,1024]{1,0:T(8,128)(2,1)}, bf16[288,1024]{1,0:T(8,128)(2,1)}, u32[]{:S(2)}, u32[]{:S(2)}) collective-permute-start(bf16[288,1024]{1,0:T(8,128)(2,1)} %get-tuple-element.654), channel_id=1, source_target_pairs={{0,24},{8,0},{16,8},{24,16},{1,25},{9,1},{17,9},{25,17},{2,26},{10... | collective-permute-start | bytes 1769480 | tf_op jit(solution)/shard_map/ppermute | solution.py:718
  796.9 34.3 %collective-permute-start.62 = (bf16[128,2304]{1,0:T(8,128)(2,1)}, bf16[128,2304]{1,0:T(8,128)(2,1)}, u32[]{:S(2)}, u32[]{:S(2)}) collective-permute-start(bf16[128,2304]{1,0:T(8,128)(2,1)} %fusion.32), channel_id=1, source_target_pairs={{0,2},{2,0},{1,3},{3,1},{4,6},{6,4},{5,7},{7,5},{8,10},{10,8},{9,1... | collective-permute-start | bytes 1769480 | tf_op jit(solution)/shard_map/ppermute | solution.py:718
  835.8 38.8 %collective-permute-start.66 = (f32[4,3,128,128]{3,2,1,0:T(8,128)S(1)}, f32[4,3,128,128]{3,2,1,0:T(8,128)S(1)}, u32[]{:S(2)}, u32[]{:S(2)}) collective-permute-start(f32[4,3,128,128]{3,2,1,0:T(8,128)S(1)} %dynamic-slice_bitcast_fusion.3), channel_id=1, source_target_pairs={{0,4},{4,0},{1,5},{5,1},{2,6},{6,2},{3,7},{7,3},{8,12},{12,8},{9,1... | collective-permute-start | bytes 2359304 | tf_op jit(solution)/shard_map/ppermute | solution.py:718
  837.3 27.7 %collective-permute-start.63 = (bf16[288,576]{1,0:T(8,128)(2,1)S(1)}, bf16[288,576]{1,0:T(8,128)(2,1)S(1)}, u32[]{:S(2)}, u32[]{:S(2)}) collective-permute-start(bf16[288,576]{1,0:T(8,128)(2,1)S(1)} %get-tuple-element.680), channel_id=1, source_target_pairs={{0,8},{8,16},{16,24},{24,0},{1,9},{9,17},{17,25},{25,1},{2,10},{10... | collective-permute-start | bytes 995336 | tf_op jit(solution)/shard_map/ppermute | solution.py:718
  850.3 24.3 %collective-permute-start.64 = (bf16[288,576]{1,0:T(8,128)(2,1)S(1)}, bf16[288,576]{1,0:T(8,128)(2,1)S(1)}, u32[]{:S(2)}, u32[]{:S(2)}) collective-permute-start(bf16[288,576]{1,0:T(8,128)(2,1)S(1)} %get-tuple-element.679), channel_id=1, source_target_pairs={{0,16},{8,24},{16,0},{24,8},{1,17},{9,25},{17,1},{25,9},{2,18},{10... | collective-permute-start | bytes 995336 | tf_op jit(solution)/shard_map/ppermute | solution.py:718
  851.6 23.0 %collective-permute-start.65 = (bf16[288,576]{1,0:T(8,128)(2,1)S(1)}, bf16[288,576]{1,0:T(8,128)(2,1)S(1)}, u32[]{:S(2)}, u32[]{:S(2)}) collective-permute-start(bf16[288,576]{1,0:T(8,128)(2,1)S(1)} %get-tuple-element.678), channel_id=1, source_target_pairs={{0,24},{8,0},{16,8},{24,16},{1,25},{9,1},{17,9},{25,17},{2,26},{10... | collective-permute-start | bytes 995336 | tf_op jit(solution)/shard_map/ppermute | solution.py:718
  879.0 41.8 %collective-permute-start.71 = (f32[4,3,128,128]{3,2,1,0:T(8,128)}, f32[4,3,128,128]{3,2,1,0:T(8,128)}, u32[]{:S(2)}, u32[]{:S(2)}) collective-permute-start(f32[4,3,128,128]{3,2,1,0:T(8,128)} %dynamic-slice_bitcast_fusion.2), channel_id=1, source_target_pairs={{0,4},{4,0},{1,5},{5,1},{2,6},{6,2},{3,7},{7,3},{8,12},{12,8},{9,1... | collective-permute-start | bytes 2359304 | tf_op jit(solution)/shard_map/ppermute | solution.py:718
  888.8 23.7 %collective-permute-start.69 = (f32[1,3,128,128]{3,2,1,0:T(8,128)}, f32[1,3,128,128]{3,2,1,0:T(8,128)S(1)}, u32[]{:S(2)}, u32[]{:S(2)}) collective-permute-start(f32[1,3,128,128]{3,2,1,0:T(8,128)} %get-tuple-element.716), channel_id=1, source_target_pairs={{0,16},{8,24},{16,0},{24,8},{1,17},{9,25},{17,1},{25,9},{2,18},{10... | collective-permute-start | bytes 589832 | tf_op jit(solution)/shard_map/ppermute | solution.py:718
  893.1 27.8 %collective-permute-start.72 = (bf16[2,3,128,128]{3,2,1,0:T(8,128)(2,1)S(1)}, bf16[2,3,128,128]{3,2,1,0:T(8,128)(2,1)S(1)}, u32[]{:S(2)}, u32[]{:S(2)}) collective-permute-start(bf16[2,3,128,128]{3,2,1,0:T(8,128)(2,1)S(1)} %shard_map.378), channel_id=1, source_target_pairs={{0,8},{8,16},{16,24},{24,0},{1,9},{9,17},{17,25},{25,1},{2,10},{10... | collective-permute-start | bytes 589832 | tf_op jit(solution)/shard_map/ppermute | solution.py:718
  893.2 27.7 %collective-permute-start.73 = (bf16[2,3,128,128]{3,2,1,0:T(8,128)(2,1)S(1)}, bf16[2,3,128,128]{3,2,1,0:T(8,128)(2,1)S(1)}, u32[]{:S(2)}, u32[]{:S(2)}) collective-permute-start(bf16[2,3,128,128]{3,2,1,0:T(8,128)(2,1)S(1)} %shard_map.378), channel_id=1, source_target_pairs={{0,16},{8,24},{16,0},{24,8},{1,17},{9,25},{17,1},{25,9},{2,18},{10... | collective-permute-start | bytes 589832 | tf_op jit(solution)/shard_map/ppermute | solution.py:718
  897.2 23.7 %collective-permute-start.74 = (bf16[2,3,128,128]{3,2,1,0:T(8,128)(2,1)S(1)}, bf16[2,3,128,128]{3,2,1,0:T(8,128)(2,1)S(1)}, u32[]{:S(2)}, u32[]{:S(2)}) collective-permute-start(bf16[2,3,128,128]{3,2,1,0:T(8,128)(2,1)S(1)} %shard_map.378), channel_id=1, source_target_pairs={{0,24},{8,0},{16,8},{24,16},{1,25},{9,1},{17,9},{25,17},{2,26},{10... | collective-permute-start | bytes 589832 | tf_op jit(solution)/shard_map/ppermute | solution.py:718
  921.2 28.7 %collective-permute-start.79 = (bf16[4,2,3,128,128]{4,3,2,0,1:T(8,128)(2,1)S(1)}, bf16[4,2,3,128,128]{4,3,2,0,1:T(8,128)(2,1)}, u32[]{:S(2)}, u32[]{:S(2)}) collective-permute-start(bf16[4,2,3,128,128]{4,3,2,0,1:T(8,128)(2,1)S(1)} %bitcast_dynamic-update-slice_fusion.38), channel_id=1, source_target_pairs={{0,4},{4,0},{1,5},{5,1},{2,6},{6,2},{3,7},{7,3},{8,12},{12,8},{9,1... | collective-permute-start | bytes 2359304 | tf_op jit(solution)/shard_map/ppermute | solution.py:718
  949.9 24.8 %collective-permute-start.81 = (bf16[2,3,128,128]{3,2,1,0:T(8,128)(2,1)S(1)}, bf16[2,3,128,128]{3,2,1,0:T(8,128)(2,1)S(1)}, u32[]{:S(2)}, u32[]{:S(2)}) collective-permute-start(bf16[2,3,128,128]{3,2,1,0:T(8,128)(2,1)S(1)} %pad_maximum_fusion.9), channel_id=1, source_target_pairs={{0,8},{8,16},{16,24},{24,0},{1,9},{9,17},{17,25},{25,1},{2,10},{10... | collective-permute-start | bytes 589832 | tf_op jit(solution)/shard_map/ppermute | solution.py:718
  954.6 20.2 %collective-permute-start.82 = (bf16[2,3,128,128]{3,2,1,0:T(8,128)(2,1)S(1)}, bf16[2,3,128,128]{3,2,1,0:T(8,128)(2,1)S(1)}, u32[]{:S(2)}, u32[]{:S(2)}) collective-permute-start(bf16[2,3,128,128]{3,2,1,0:T(8,128)(2,1)S(1)} %pad_maximum_fusion.9), channel_id=1, source_target_pairs={{0,16},{8,24},{16,0},{24,8},{1,17},{9,25},{17,1},{25,9},{2,18},{10... | collective-permute-start | bytes 589832 | tf_op jit(solution)/shard_map/ppermute | solution.py:718
  (174 other events, 1802.0 us)
Sparse Core Ops, SparseCore 0:
  117.7 84.7 all-gather.3
  205.0 66.8 all-gather.5
  274.3 66.8 all-gather.7
  477.5 77.8 reduce-scatter.3
  558.3 70.9 reduce-scatter.5
  641.2 110.8 reduce-scatter.7
